TPU v7x, 512 devices: a whole 4x4x16 slice. The times are simulated.
512 devices in a mesh: expert: 32 (over x, y, core), tensor: 16 (over z).
Axes of the slice: x: 4, y: 4, z: 16, core: 2. Of those that a mesh axis runs over, the one named last changes fastest.
Arguments:
- picked_rows: bfloat16 [32, 256, 6144], P('expert', None, 'tensor'), may hold values from -6 to 6
- w_gate: bfloat16 [32, 6144, 1536], P('expert', 'tensor'), may hold values from -0.078125 to 0.078125
- w_up: bfloat16 [32, 6144, 1536], P('expert', 'tensor'), may hold values from -0.078125 to 0.078125
- w_down: bfloat16 [32, 1536, 6144], P('expert', None, 'tensor'), may hold values from -0.15625 to 0.15625
- combine_gate: float32 [32, 256], P('expert'), may hold values from 0.3 to 3
- pick_owner: int32 [32, 256], replicated, may hold values from 0 to 31, as said below
- pick_row: int32 [32, 256], replicated, may hold values from 0 to 767, as said below
- residual_in: bfloat16 [24576, 6144], P('expert', 'tensor'), may hold values from -60 to 60
- norm_gain: float32 [6144], P('tensor'), may hold values from 0.5 to 2
- projection: bfloat16 [6144, 6144], P('expert', 'tensor'), may hold values from -0.078125 to 0.078125
Outputs:
- projected: bfloat16 [24576, 6144], P('expert', 'tensor')
Inputs may be any that keep to these rules, and one draw needn't show every extreme that they name: `pick_owner`: for every expert, at most 24 of its picks have one owner group, and one owner group gets exactly 24 picks from every expert. The picks of one expert are distinct tokens. `pick_row`: together with pick_owner it names a token; no expert names a token twice.
All inputs are finite; a program needn't handle non-finite values.
Results may differ from a plain program's by a relative error of at most 0.0051.
Values may be sent and summed in bfloat16 or wider, within the bound.
No kernel may reach another device: no remote copies, remote signals or barrier semaphores. Data moves between devices by JAX's collectives and lax.ppermute only.
A program may use at most 64 MiB of HBM per device.

v0:
```python
import jax
import jax.numpy as jnp
from jax import lax
from jax.sharding import PartitionSpec as P

D = 6144


def shards(
    picked_rows,
    w_gate,
    w_up,
    w_down,
    combine_gate,
    pick_owner,
    pick_row,
    residual_in,
    norm_gain,
    projection,
):
    my_rows = picked_rows[0]
    gate_mat = w_gate[0]
    up_mat = w_up[0]
    down_mat = w_down[0]
    capacity = my_rows.shape[0]
    gate_part = jnp.dot(my_rows, gate_mat, preferred_element_type=jnp.float32)
    up_part = jnp.dot(my_rows, up_mat, preferred_element_type=jnp.float32)
    gate_pre, up_pre = lax.psum((gate_part, up_part), "tensor")
    hidden = (jax.nn.silu(gate_pre) * up_pre).astype(jnp.bfloat16)
    expert_out = jnp.dot(hidden, down_mat, preferred_element_type=jnp.float32)
    weighted = (combine_gate[0][:, None] * expert_out).astype(jnp.bfloat16)
    n_groups = pick_owner.shape[0]
    slot_most = max(3 * capacity // n_groups, 2)
    my_index = lax.axis_index("expert")
    group_ids = jnp.arange(n_groups, dtype=jnp.int32)
    owner_hits = (pick_owner[:, :, None] == group_ids[None, None, :]).astype(jnp.int32)
    earlier = jnp.cumsum(owner_hits, axis=1) - owner_hits
    position = jnp.sum(earlier * owner_hits, axis=2)
    my_owner = lax.dynamic_index_in_dim(pick_owner, my_index, 0, keepdims=False)
    my_position = lax.dynamic_index_in_dim(position, my_index, 0, keepdims=False)
    my_slot = my_owner * slot_most + my_position
    slot_ids = jnp.arange(n_groups * slot_most, dtype=jnp.int32)
    send_table = (my_slot[None, :] == slot_ids[:, None]).astype(jnp.bfloat16)
    outgoing = jnp.dot(send_table, weighted, preferred_element_type=jnp.float32).astype(
        jnp.bfloat16
    )
    outgoing = outgoing.reshape(n_groups, slot_most, weighted.shape[1])
    received = lax.all_to_all(outgoing, "expert", split_axis=0, concat_axis=0, tiled=True)
    mine = pick_owner == my_index
    slot_range = jnp.arange(slot_most, dtype=jnp.int32)
    matches = mine[:, None, :] & (position[:, None, :] == slot_range[None, :, None])
    row_of = jnp.sum(jnp.where(matches, pick_row[:, None, :] + 1, 0), axis=2) - 1
    tok_group = residual_in.shape[0]
    token_ids = jnp.arange(tok_group, dtype=jnp.int32)
    recv_table = (row_of.reshape(-1)[None, :] == token_ids[:, None]).astype(jnp.bfloat16)
    moe = jnp.dot(
        recv_table,
        received.reshape(n_groups * slot_most, weighted.shape[1]),
        preferred_element_type=jnp.float32,
    )
    mixed = residual_in.astype(jnp.float32) + moe
    square_total = lax.psum(jnp.sum(mixed * mixed, axis=1), "tensor")
    inverse_rms = lax.rsqrt(square_total / D + 1e-05)
    normed = (mixed * inverse_rms[:, None] * norm_gain[None, :]).astype(jnp.bfloat16)
    full_normed = lax.all_gather(normed, "tensor", axis=1, tiled=True)
    projected = jnp.dot(
        full_normed,
        lax.all_gather(projection, "expert", axis=0, tiled=True),
        preferred_element_type=jnp.float32,
    )
    return projected.astype(jnp.bfloat16)


def solution(mesh):
    return jax.shard_map(
        shards,
        mesh=mesh,
        in_specs=(
            P("expert", None, "tensor"),
            P("expert", "tensor", None),
            P("expert", "tensor", None),
            P("expert", None, "tensor"),
            P("expert", None),
            P(),
            P(),
            P("expert", "tensor"),
            P("tensor"),
            P("expert", "tensor"),
        ),
        out_specs=P("expert", "tensor"),
        check_vma=False,
    )
```

profile of v0, /device:TPU:1, one launch (start us, length us, event | category | flops | bytes accessed | tf_op | source)
XLA Modules:
  0.0 349.4 jit_solution(12543989698631258117)
XLA Ops:
  7.4 0.0 copy-start
  7.4 0.0 copy-start.2
  7.4 0.0 copy-start.1
  7.4 0.0 all-reduce.3.cloned.1.call-start
  7.4 1.3 copy-done
  8.6 2.6 fusion.3
  11.3 0.0 copy-done.2
  11.3 0.0 copy-done.1
  11.3 1.7 fusion.5
  13.0 0.0 copy-start.4
  13.0 0.0 all-reduce.3.cloned.1.call-update
  13.0 0.0 all-gather.5.cloned.1.call-start
  13.1 0.5 all-gather.5.cloned.1.call-update
  13.6 0.1 copy-done.4
  13.8 0.1 fusion.16
  14.0 18.4 %reduce-window.6 = s32[32,32,2,128]{3,1,2,0:T(8,128)S(1)} reduce-window(s32[32,32,2,128]{3,1,2,0:T(8,128)S(1)} %fusion.16, s32[]{:T(128)} %constant.27.clone.1), window={size=1x1x1x128 pad=0_0x0_0x0_0x127_0}, to_apply=%region_0.0 | reduce-window | flops 33292288 | bytes 2097156 | tf_op jit(solution)/shard_map/reduce-window
  32.4 0.3 slice.8
  32.7 0.0 copy-start.5
  32.8 0.0 copy-start.7
  32.8 0.4 copy.17
  33.2 0.1 fusion.22
  33.3 0.4 fusion.15
  33.8 0.0 copy-done.5
  33.8 127.0 %all-reduce.3.cloned.1.call-done = (f32[256,1536]{1,0:T(8,128)}, f32[256,1536]{1,0:T(8,128)}) async-done(((f32[256,1536]{1,0:T(8,128)}, f32[256,1536]{1,0:T(8,128)}), (f32[256,1536]{1,0:T(8,128)}, f32[256,1536]{1,0:T(8,128)})) %all-reduce.3.cloned.1.call-update) | async-done | bytes 3145744 | tf_op jit(solution)/shard_map/psum | solution.py:28
  160.8 0.0 copy-done.7
  160.8 4.0 %convolution_convert_fusion.1 = bf16[768,384]{1,0:T(8,128)(2,1)} fusion(bf16[1,1536,384]{2,1,0:T(8,128)(2,1)} %param.13, f32[256,1536]{1,0:T(8,128)} %get-tuple-element.5, f32[256,1536]{1,0:T(8,128)} %get-tuple-element.6, s32[256]{0:T(256)S(1)} %bitcast.48, f32[256]{0:T(256)S(1)} %bitcast.49), kind=kOutput, calls=%fused_computation.5 | convolution fusion | flops 456032256 | bytes 4917248 | tf_op jit(solution)/shard_map/dot_general | solution.py:44
  164.8 0.0 copy-start.3
  164.8 16.3 %all-to-all-start = ((bf16[32,24,384]{2,1,0:T(8,128)(2,1)}), bf16[32,24,384]{2,1,0:T(8,128)(2,1)S(1)}, u32[]{:S(2)}, u32[]{:S(2)}) async-start(bf16[32,24,384]{2,1,0:T(8,128)(2,1)} %bitcast.8), calls=%async_computation | async-start | bytes 1179648 | tf_op jit(solution)/shard_map/all_to_all | solution.py:48
  181.1 0.0 all-gather.3.cloned.1.call-start
  181.2 0.6 select_reduce_fusion
  181.9 0.1 sub.11
  181.9 0.0 copy-done.3
  181.9 0.3 copy.16
  182.2 11.2 %all-to-all-done = bf16[32,24,384]{2,1,0:T(8,128)(2,1)S(1)} async-done(((bf16[32,24,384]{2,1,0:T(8,128)(2,1)}), bf16[32,24,384]{2,1,0:T(8,128)(2,1)S(1)}, u32[]{:S(2)}, u32[]{:S(2)}) %all-to-all-start) | async-done | bytes 589856 | tf_op jit(solution)/shard_map/all_to_all | solution.py:48
  193.4 0.0 copy-start.6
  193.4 0.8 multiply_reduce_fusion
  194.2 21.5 %psum.23 = f32[768]{0:T(1024)S(1)} all-reduce(f32[768]{0:T(1024)S(1)} %get-tuple-element.7), channel_id=1, replica_groups=mesh['expert'=32,'tensor'=16] {'tensor'}, use_global_device_ids=true, to_apply=%region_7.8 | all-reduce | flops 768 | bytes 6144 | tf_op jit(solution)/shard_map/psum | solution.py:62
  215.7 0.0 copy-done.6
  215.7 1.0 multiply_convert_fusion.1
  216.7 0.0 all-gather.3.cloned.1.call-update
  216.7 0.0 all-gather.5.cloned.1.call-done
  216.7 115.5 %all-gather.3.cloned.1.call-done = bf16[768,6144]{0,1:T(8,128)(2,1)} async-done(((bf16[768,384]{0,1:T(8,128)(2,1)}), bf16[768,6144]{0,1:T(8,128)(2,1)}) %all-gather.3.cloned.1.call-update) | async-done | bytes 9437200 | tf_op jit(solution)/shard_map/all_gather | solution.py:65
  332.3 9.7 %convolution_convert_fusion = bf16[768,384]{1,0:T(8,128)(2,1)} fusion(bf16[768,6144]{0,1:T(8,128)(2,1)} %all-gather.3.cloned.1.call-done, bf16[6144,384]{1,0:T(8,128)(2,1)} %all-gather.5.cloned.1.call-done), kind=kOutput, calls=%fused_computation.4 | convolution fusion | flops 3624173568 | bytes 14745600 | tf_op jit(solution)/shard_map/dot_general | solution.py:66
  (8 shorter events, 0.1 us)
Async XLA Ops:
  7.4 1.3 copy-start
  7.4 3.9 %copy-start.2 = (bf16[1,256,384]{2,1,0:T(8,128)(2,1)S(1)}, bf16[1,256,384]{2,1,0:T(8,128)(2,1)}, u32[]{:S(2)}) copy-start(bf16[1,256,384]{2,1,0:T(8,128)(2,1)} %param.10) | copy-start | bytes 589828
  7.4 3.9 %copy-start.1 = (bf16[1,384,1536]{2,1,0:T(8,128)(2,1)S(1)}, bf16[1,384,1536]{2,1,0:T(8,128)(2,1)}, u32[]{:S(2)}) copy-start(bf16[1,384,1536]{2,1,0:T(8,128)(2,1)} %param.11) | copy-start | bytes 3538948
  7.4 153.4 %all-reduce.3.cloned.1.call-start = ((), (), s32[]{:S(2)}) async-start(), calls=%async_computation.3 | async-start | bytes 6291456 | tf_op jit(solution)/shard_map/psum | solution.py:28
  13.0 0.8 copy-start.4
  13.0 203.7 %all-gather.5.cloned.1.call-start = ((), (), s32[]{:S(2)}) async-start(), calls=%async_computation.2 | async-start | bytes 4866048 | tf_op jit(solution)/shard_map/all_gather | solution.py:68
  32.7 1.1 copy-start.5
  32.8 128.1 %copy-start.7 = (f32[1,256]{1,0:T(1,128)S(1)}, f32[1,256]{1,0:T(1,128)}, u32[]{:S(2)}) copy-start(f32[1,256]{1,0:T(1,128)} %param.14) | copy-start | bytes 3076
  164.8 17.1 %copy-start.3 = (bf16[768,384]{1,0:T(8,128)(2,1)S(1)}, bf16[768,384]{1,0:T(8,128)(2,1)}, u32[]{:S(2)}) copy-start(bf16[768,384]{1,0:T(8,128)(2,1)} %param.17) | copy-start | bytes 1769476
  164.8 28.6 %all-to-all-start = ((bf16[32,24,384]{2,1,0:T(8,128)(2,1)}), bf16[32,24,384]{2,1,0:T(8,128)(2,1)S(1)}, u32[]{:S(2)}, u32[]{:S(2)}) async-start(bf16[32,24,384]{2,1,0:T(8,128)(2,1)} %bitcast.8), calls=%async_computation | async-start | bytes 1179648 | tf_op jit(solution)/shard_map/all_to_all | solution.py:48
  181.1 151.1 %all-gather.3.cloned.1.call-start = ((), (), s32[]{:S(2)}) async-start(), calls=%async_computation.1 | async-start | bytes 10027008 | tf_op jit(solution)/shard_map/all_gather | solution.py:65
  193.4 22.3 %copy-start.6 = (f32[384]{0:T(512)S(1)}, f32[384]{0:T(512)}, u32[]{:S(2)}) copy-start(f32[384]{0:T(512)} %param.18) | copy-start | bytes 4612
Sparse Core Ops, SparseCore 0:
  13.2 147.6 all-reduce.2
Sparse Core Ops, SparseCore 1:
  16.6 68.0 all-gather.4
  216.8 115.4 all-gather.2
where the time goes:
time: 350 us; the launch traced here: 349 us
  waiting for transfers between devices  254 us (73%)
  blocking collectives  21.5 us (6%)
  other arithmetic  20.7 us (6%)
  matrix products  18.9 us (5%)
  starting transfers between devices  16.4 us (5%)
  between operations  15 us (4%)
    psum x1, waiting for transfers between devices, shards(): gate_pre, up_pre = lax.psum((gate_part, up_part), 'tensor')  127 us
    all_gather x1, waiting for transfers between devices, shards(): full_normed = lax.all_gather(normed, 'tensor', axis=1, tiled=True)  116 us
    psum x1, blocking collectives, shards(): square_total = lax.psum(jnp.sum(mixed * mixed, axis=1), 'tensor')  21.5 us
    another operation x2, other arithmetic  18.5 us
    all_to_all x1, starting transfers between devices, shards(): lax.all_to_all(outgoing, 'expert', split_axis=0, concat_axis=0, tiled=True)  16.3 us
    all_to_all x1, waiting for transfers between devices, shards(): lax.all_to_all(outgoing, 'expert', split_axis=0, concat_axis=0, tiled=True)  11.2 us
    dot_general x1, matrix products, shards(): jnp.dot(full_normed, lax.all_gather(projection, 'expert', axis=0, tiled=T...  9.74 us
  transfers between devices with their start and end apart: 4, of which 3 were waited for; matrix products, arithmetic and copies ran while one was open for 8% of the time, Pallas kernels for 0%

commit v1 on v0

v1 whole, which is shorter than its diff:
```python
import jax
import jax.numpy as jnp
from jax import lax
from jax.experimental import pallas as pl
from jax.experimental.pallas import tpu as pltpu
from jax.sharding import PartitionSpec as P

D = 6144
PIECE_ROWS = 16
PIECE_COLS = 512
VMEM_BYTES = 48 * 1024 * 1024


def piece_places(capacity, ff):
    return [(r, c) for r in range(0, capacity, PIECE_ROWS) for c in range(0, ff, PIECE_COLS)]


def gate_up_kernel(rows_ref, gate_ref, up_ref, *out_refs):
    capacity, ff = rows_ref.shape[0], gate_ref.shape[1]
    n_row = capacity // PIECE_ROWS
    n_col = ff // PIECE_COLS
    rows = rows_ref[...]
    for half, weights in enumerate((gate_ref, up_ref)):
        for c in range(n_col):
            part = jnp.dot(
                rows,
                weights[:, c * PIECE_COLS : (c + 1) * PIECE_COLS],
                preferred_element_type=jnp.float32,
            )
            for r in range(n_row):
                out_refs[(half * n_row + r) * n_col + c][...] = part[
                    r * PIECE_ROWS : (r + 1) * PIECE_ROWS
                ]


def gate_up(rows, gate_mat, up_mat):
    n_pieces = 2 * len(piece_places(rows.shape[0], gate_mat.shape[1]))
    return pl.pallas_call(
        gate_up_kernel,
        out_shape=[jax.ShapeDtypeStruct((PIECE_ROWS, PIECE_COLS), jnp.float32)] * n_pieces,
        in_specs=[pl.BlockSpec(memory_space=pltpu.VMEM)] * 3,
        out_specs=[pl.BlockSpec(memory_space=pltpu.VMEM)] * n_pieces,
        compiler_params=pltpu.CompilerParams(vmem_limit_bytes=VMEM_BYTES),
        name="gate_up",
    )(rows, gate_mat, up_mat)


def tail_kernel(down_ref, combine_ref, slot_ref, *refs):
    out_ref, hidden_ref = refs[-2:]
    pieces = refs[:-2]
    capacity, ff = hidden_ref.shape
    half = len(pieces) // 2
    for k, (r, c) in enumerate(piece_places(capacity, ff)):
        gate = pieces[k][...]
        up = pieces[half + k][...]
        hidden_ref[r : r + PIECE_ROWS, c : c + PIECE_COLS] = (gate / (1.0 + jnp.exp(-gate)) * up).astype(
            jnp.bfloat16
        )
    expert_out = jnp.dot(hidden_ref[...], down_ref[...], preferred_element_type=jnp.float32)
    weighted = (combine_ref[...] * expert_out).astype(jnp.bfloat16)
    slots = out_ref.shape[0]
    slot_ids = lax.broadcasted_iota(jnp.int32, (slots, capacity), 0)
    table = jnp.where(slot_ref[...] == slot_ids, 1.0, 0.0).astype(jnp.bfloat16)
    out_ref[...] = jnp.dot(table, weighted, preferred_element_type=jnp.float32).astype(jnp.bfloat16)


def expert_tail(pieces, down_mat, combine, slot, slots):
    ff, width = down_mat.shape
    capacity = combine.shape[0]
    return pl.pallas_call(
        tail_kernel,
        out_shape=jax.ShapeDtypeStruct((slots, width), jnp.bfloat16),
        in_specs=[pl.BlockSpec(memory_space=pltpu.VMEM)] * (3 + len(pieces)),
        out_specs=pl.BlockSpec(memory_space=pltpu.VMEM),
        scratch_shapes=[pltpu.VMEM((capacity, ff), jnp.bfloat16)],
        compiler_params=pltpu.CompilerParams(vmem_limit_bytes=VMEM_BYTES),
        name="expert_tail",
    )(down_mat, combine[:, None], slot[None, :], *pieces)


def shards(
    picked_rows,
    w_gate,
    w_up,
    w_down,
    combine_gate,
    pick_owner,
    pick_row,
    residual_in,
    norm_gain,
    projection,
):
    my_rows = picked_rows[0]
    capacity = my_rows.shape[0]
    n_groups = pick_owner.shape[0]
    slot_most = max(3 * capacity // n_groups, 2)
    tok_group, width = residual_in.shape
    my_index = lax.axis_index("expert")

    full_projection = lax.all_gather(projection, "expert", axis=0, tiled=True)

    parts = gate_up(my_rows, w_gate[0], w_up[0])

    my_owner = lax.dynamic_index_in_dim(pick_owner, my_index, 0, keepdims=False)
    pick_ids = jnp.arange(capacity, dtype=jnp.int32)
    same_earlier = (my_owner[:, None] == my_owner[None, :]) & (pick_ids[:, None] < pick_ids[None, :])
    my_position = jnp.sum(same_earlier.astype(jnp.int32), axis=0)
    my_slot = my_owner * slot_most + my_position

    mine = pick_owner == my_index
    before = (pick_ids[:, None] < pick_ids[None, :]).astype(jnp.bfloat16)
    position = jnp.dot(
        mine.astype(jnp.bfloat16), before, preferred_element_type=jnp.float32
    ).astype(jnp.int32)
    slot_range = jnp.arange(slot_most, dtype=jnp.int32)
    matches = mine[:, None, :] & (position[:, None, :] == slot_range[None, :, None])
    row_of = jnp.sum(jnp.where(matches, pick_row[:, None, :] + 1, 0), axis=2) - 1
    token_ids = jnp.arange(tok_group, dtype=jnp.int32)
    recv_table = (row_of.reshape(-1)[None, :] == token_ids[:, None]).astype(jnp.bfloat16)

    sums = lax.psum(tuple(parts), "tensor")
    outgoing = expert_tail(sums, w_down[0], combine_gate[0], my_slot, n_groups * slot_most)
    outgoing = outgoing.reshape(n_groups, slot_most, width)
    received = lax.all_to_all(outgoing, "expert", split_axis=0, concat_axis=0, tiled=True)
    moe = jnp.dot(
        recv_table,
        received.reshape(n_groups * slot_most, width),
        preferred_element_type=jnp.float32,
    )
    mixed = residual_in.astype(jnp.float32) + moe
    gained = (mixed * norm_gain[None, :]).astype(jnp.bfloat16)
    full_gained = lax.all_gather(gained, "tensor", axis=1, tiled=True)
    square_total = lax.psum(jnp.sum(mixed * mixed, axis=1), "tensor")
    inverse_rms = lax.rsqrt(square_total / D + 1e-05)
    projected = jnp.dot(full_gained, full_projection, preferred_element_type=jnp.float32)
    return (projected * inverse_rms[:, None]).astype(jnp.bfloat16)


def solution(mesh):
    return jax.shard_map(
        shards,
        mesh=mesh,
        in_specs=(
            P("expert", None, "tensor"),
            P("expert", "tensor", None),
            P("expert", "tensor", None),
            P("expert", None, "tensor"),
            P("expert", None),
            P(),
            P(),
            P("expert", "tensor"),
            P("tensor"),
            P("expert", "tensor"),
        ),
        out_specs=P("expert", "tensor"),
        check_vma=False,
    )
```

time: 350 us -> 333 us (0.951)
  waiting for transfers between devices: 254 us -> 98.7 us
  blocking collectives: 21.5 us -> 103 us
  local copies, waits for them, and re-layouts: 2.6 us -> 82.7 us
  other arithmetic: 20.7 us -> 1.48 us
  matrix products: 18.9 us -> 11.5 us
    psum x1 -> x0, waiting for transfers between devices: 127 us -> none  [shards(): gate_pre, up_pre = lax.psum((gate_part, up_part), 'tensor')]
    psum x0 -> x1, blocking collectives: none -> 80.2 us  [shards(): sums = lax.psum(tuple(parts), 'tensor')]
    unnamed x17 -> x265, local copies, waits for them, and re-layouts: 1.68 us -> 81.1 us
    all_gather x2, waiting for transfers between devices: 116 us -> 87 us  [the longest x1 87 us: shards(): full_gained = lax.all_gather(gained, 'tensor', axis=1, tiled=True)]
    another operation x2 -> x0, other arithmetic: 18.5 us -> none
    dot_general x5 -> x3, matrix products: 18.9 us -> 11.5 us  [the longest x1 9.72 us: shards(): jnp.dot(full_gained, full_projection, preferred_element_type=jnp.float32)]
  transfers between devices with their start and end apart: 4 -> 3, of which waited for: 3 -> 2; matrix products, arithmetic and copies ran while one was open for 8% -> 2% of each run, Pallas kernels for 0% -> 1%
where the time goes in v1:
time: 333 us; the launch traced here: 330 us
  blocking collectives  103 us (31%)
  waiting for transfers between devices  98.7 us (30%)
  local copies, waits for them, and re-layouts  82.7 us (25%)
  starting transfers between devices  16.4 us (5%)
  between operations  13.7 us (4%)
  matrix products  11.5 us (3%)
    all_gather x1, waiting for transfers between devices, shards(): full_gained = lax.all_gather(gained, 'tensor', axis=1, tiled=True)  87 us
    unnamed x265, local copies, waits for them, and re-layouts  81.1 us
    psum x1, blocking collectives, shards(): sums = lax.psum(tuple(parts), 'tensor')  80.2 us
    psum x1, blocking collectives, shards(): square_total = lax.psum(jnp.sum(mixed * mixed, axis=1), 'tensor')  23.1 us
    all_to_all x1, starting transfers between devices, shards(): lax.all_to_all(outgoing, 'expert', split_axis=0, concat_axis=0, tiled=True)  16.3 us
    all_to_all x1, waiting for transfers between devices, shards(): lax.all_to_all(outgoing, 'expert', split_axis=0, concat_axis=0, tiled=True)  11 us
    dot_general x1, matrix products, shards(): jnp.dot(full_gained, full_projection, preferred_element_type=jnp.float32)  9.72 us
  transfers between devices with their start and end apart: 3, of which 2 were waited for; matrix products, arithmetic and copies ran while one was open for 2% of the time, Pallas kernels for 1%

profile of v1, /device:TPU:1, one launch (start us, length us, event | category | flops | bytes accessed | tf_op | source)
XLA Modules:
  0.0 330.4 jit_solution(6243699211115825455)
XLA Ops:
  6.5 0.7 all-gather.5.cloned.1.call-update
  7.3 0.8 copy.15.combine_ref
  8.1 1.3 copy-done
  9.4 1.3 copy-done.1
  10.6 0.9 copy-done.3
  11.6 1.0 gate_up.1
  39.4 0.6 copy-done.81
  49.1 0.6 copy-done.97
  62.6 0.6 copy-done.119
  68.8 80.2 %all-reduce.2 = (f32[16,512]{1,0:T(8,128)S(1)}, f32[16,512]{1,0:T(8,128)S(1)}, f32[16,512]{1,0:T(8,128)S(1)}, f32[16,512]{1,0:T(8,128)S(1)}, f32[16,512]{1,0:T(8...) all-reduce(f32[16,512]{1,0:T(8,128)} %copy-done.32, ...), channel_id=1, replica_groups=mesh['expert'=32,'tensor'=16] {'tensor'}, use_global_device_ids=true, to_apply=%region_2.3 | all-reduce | flops 786432 | bytes 6291456 | tf_op jit(solution)/shard_map/psum | solution.py:121
  149.0 0.7 constant_dynamic-slice_fusion
  149.8 0.7 multiply_add_fusion.slot_ref
  150.5 0.8 copy-done.4
  151.3 0.8 copy-done.5
  152.1 0.8 copy-done.6
  152.8 0.8 copy-done.7
  153.6 0.8 copy-done.8
  154.3 0.8 copy-done.9
  155.1 0.8 copy-done.10
  155.8 0.8 copy-done.11
  156.6 0.8 copy-done.12
  157.4 0.8 copy-done.13
  158.1 0.8 copy-done.14
  158.9 0.8 copy-done.15
  159.6 0.8 copy-done.16
  160.4 0.8 copy-done.17
  161.2 0.8 copy-done.18
  161.9 0.8 copy-done.19
  162.7 0.8 copy-done.20
  163.4 0.8 copy-done.21
  164.2 0.8 copy-done.22
  164.9 0.8 copy-done.23
  165.7 0.8 copy-done.24
  166.5 0.8 copy-done.25
  167.2 0.8 copy-done.26
  168.0 0.8 copy-done.27
  168.7 0.8 copy-done.28
  169.5 0.8 copy-done.29
  170.3 0.8 copy-done.30
  171.0 0.8 copy-done.31
  171.8 1.8 expert_tail.1
  173.6 16.3 %all-to-all-start = ((bf16[32,24,384]{2,1,0:T(8,128)(2,1)}), bf16[32,24,384]{2,1,0:T(8,128)(2,1)S(1)}, u32[]{:S(2)}, u32[]{:S(2)}) async-start(bf16[32,24,384]{2,1,0:T(8,128)(2,1)} %bitcast.7), calls=%async_computation | async-start | bytes 1179648 | tf_op jit(solution)/shard_map/all_to_all | solution.py:124
  190.1 0.6 select_reduce_fusion
  191.1 11.0 %all-to-all-done = bf16[32,24,384]{2,1,0:T(8,128)(2,1)S(1)} async-done(((bf16[32,24,384]{2,1,0:T(8,128)(2,1)}), bf16[32,24,384]{2,1,0:T(8,128)(2,1)S(1)}, u32[]{:S(2)}, u32[]{:S(2)}) %all-to-all-start) | async-done | bytes 589856 | tf_op jit(solution)/shard_map/all_to_all | solution.py:124
  202.2 1.6 multiply_reduce_fusion
  203.8 23.1 %psum.775 = f32[768]{0:T(1024)S(1)} all-reduce(f32[768]{0:T(1024)S(1)} %get-tuple-element.293), channel_id=1, replica_groups=mesh['expert'=32,'tensor'=16] {'tensor'}, use_global_device_ids=true, to_apply=%region_99.100 | all-reduce | flops 768 | bytes 6144 | tf_op jit(solution)/shard_map/psum | solution.py:133
  226.9 87.0 %all-gather.3.cloned.1.call-done = bf16[768,6144]{0,1:T(8,128)(2,1)} async-done(((bf16[768,384]{0,1:T(8,128)(2,1)}), bf16[768,6144]{0,1:T(8,128)(2,1)}) %all-gather.3.cloned.1.call-update) | async-done | bytes 9437200 | tf_op jit(solution)/shard_map/all_gather | solution.py:132
  313.9 9.7 %fusion.2 = bf16[768,384]{1,0:T(8,128)(2,1)} fusion(bf16[768,6144]{0,1:T(8,128)(2,1)} %all-gather.3.cloned.1.call-done, bf16[6144,384]{1,0:T(8,128)(2,1)} %all-gather.5.cloned.1.call-done, f32[768]{0:T(1024)S(1)} %add_rsqrt_fusion), kind=kOutput, calls=%fused_computation.4 | convolution fusion | flops 3624468480 | bytes 14748672 | tf_op jit(solution)/shard_map/dot_general | solution.py:135
  (242 shorter events, 55.1 us)
Async XLA Ops:
  6.5 220.4 %all-gather.5.cloned.1.call-start = ((), (), s32[]{:S(2)}) async-start(), calls=%async_computation.2 | async-start | bytes 4866048 | tf_op jit(solution)/shard_map/all_gather | solution.py:100
  8.1 1.3 copy-start
  9.4 1.3 copy-start.1
  10.6 0.9 copy-start.3
  23.5 0.6 copy-start.55
  39.4 0.6 copy-start.81
  40.0 0.6 copy-start.82
  49.1 0.6 copy-start.97
  62.6 0.6 copy-start.119
  68.1 0.6 copy-start.33
  68.1 0.6 copy-start.34
  68.1 0.6 copy-start.35
  68.1 0.6 copy-start.36
  68.8 81.7 %copy-start.2 = (bf16[1,1536,384]{2,1,0:T(8,128)(2,1)S(1)}, bf16[1,1536,384]{2,1,0:T(8,128)(2,1)}, u32[]{:S(2)}) copy-start(bf16[1,1536,384]{2,1,0:T(8,128)(2,1)} %param.13) | copy-start | bytes 3538948
  150.5 0.8 copy-start.4
  151.3 0.8 copy-start.5
  152.1 0.8 copy-start.6
  152.8 0.8 copy-start.7
  153.6 0.8 copy-start.8
  154.3 0.8 copy-start.9
  155.1 0.8 copy-start.10
  155.8 0.8 copy-start.11
  156.6 0.8 copy-start.12
  157.4 0.8 copy-start.13
  158.1 0.8 copy-start.14
  158.9 0.8 copy-start.15
  159.6 0.8 copy-start.16
  160.4 0.8 copy-start.17
  161.2 0.8 copy-start.18
  161.9 0.8 copy-start.19
  162.7 0.8 copy-start.20
  163.4 0.8 copy-start.21
  164.2 0.8 copy-start.22
  164.9 0.8 copy-start.23
  165.7 0.8 copy-start.24
  166.5 0.8 copy-start.25
  167.2 0.8 copy-start.26
  168.0 0.8 copy-start.27
  168.7 0.8 copy-start.28
  169.5 0.8 copy-start.29
  170.3 0.8 copy-start.30
  171.0 0.8 copy-start.31
  173.5 16.4 %copy-start.129 = (s32[32,256]{1,0:T(8,128)S(1)}, s32[32,256]{1,0:T(8,128)}, u32[]{:S(2)}) copy-start(s32[32,256]{1,0:T(8,128)} %param.15) | copy-start | bytes 98308
  173.5 16.4 %copy-start.130 = (s32[32,256]{1,0:T(8,128)S(1)}, s32[32,256]{1,0:T(8,128)}, u32[]{:S(2)}) copy-start(s32[32,256]{1,0:T(8,128)} %param.16) | copy-start | bytes 98308
  173.5 17.3 %copy-start.128 = (bf16[768,384]{1,0:T(8,128)(2,1)S(1)}, bf16[768,384]{1,0:T(8,128)(2,1)}, u32[]{:S(2)}) copy-start(bf16[768,384]{1,0:T(8,128)(2,1)} %param.17) | copy-start | bytes 1769476
  173.5 28.6 %copy-start.131 = (f32[384]{0:T(512)S(1)}, f32[384]{0:T(512)}, u32[]{:S(2)}) copy-start(f32[384]{0:T(512)} %param.18) | copy-start | bytes 4612
  173.6 28.6 %all-to-all-start = ((bf16[32,24,384]{2,1,0:T(8,128)(2,1)}), bf16[32,24,384]{2,1,0:T(8,128)(2,1)S(1)}, u32[]{:S(2)}, u32[]{:S(2)}) async-start(bf16[32,24,384]{2,1,0:T(8,128)(2,1)} %bitcast.7), calls=%async_computation | async-start | bytes 1179648 | tf_op jit(solution)/shard_map/all_to_all | solution.py:124
  189.9 124.0 %all-gather.3.cloned.1.call-start = ((), (), s32[]{:S(2)}) async-start(), calls=%async_computation.1 | async-start | bytes 10027008 | tf_op jit(solution)/shard_map/all_gather | solution.py:132
  (87 other events, 53.1 us)
Sparse Core Ops, SparseCore 0:
  10.5 67.8 all-gather.4
  203.9 109.8 all-gather.2

commit v2 on v1

--- a/solution.py
+++ b/solution.py
@@ -7,56 +7,75 @@
 
 D = 6144
 PIECE_ROWS = 16
-PIECE_COLS = 512
+PIECE_COLS = 768
 VMEM_BYTES = 48 * 1024 * 1024
+TAIL_VMEM_BYTES = 63 * 1024 * 1024
 
 
 def piece_places(capacity, ff):
     return [(r, c) for r in range(0, capacity, PIECE_ROWS) for c in range(0, ff, PIECE_COLS)]
 
 
-def gate_up_kernel(rows_ref, gate_ref, up_ref, *out_refs):
+def gate_up_kernel(rows_ref, gate_ref, up_ref, *refs):
+    spare_ref, parts_ref, spare_part_ref, sems = refs[-4:]
+    out_refs = refs[:-4]
     capacity, ff = rows_ref.shape[0], gate_ref.shape[1]
-    n_row = capacity // PIECE_ROWS
-    n_col = ff // PIECE_COLS
+    places = piece_places(capacity, ff)
+    spare_part_ref[...] = jnp.zeros_like(spare_part_ref)
+    copies = [pltpu.make_async_copy(spare_part_ref, spare_ref, sems.at[len(out_refs)])]
+    copies[0].start()
     rows = rows_ref[...]
     for half, weights in enumerate((gate_ref, up_ref)):
-        for c in range(n_col):
-            part = jnp.dot(
-                rows,
-                weights[:, c * PIECE_COLS : (c + 1) * PIECE_COLS],
-                preferred_element_type=jnp.float32,
+        parts_ref[half] = jnp.dot(rows, weights[...], preferred_element_type=jnp.float32)
+        for k, (r, c) in enumerate(places):
+            n = half * len(places) + k
+            copy = pltpu.make_async_copy(
+                parts_ref.at[half, r : r + PIECE_ROWS, c : c + PIECE_COLS], out_refs[n], sems.at[n]
             )
-            for r in range(n_row):
-                out_refs[(half * n_row + r) * n_col + c][...] = part[
-                    r * PIECE_ROWS : (r + 1) * PIECE_ROWS
-                ]
+            copy.start()
+            copies.append(copy)
+    for copy in copies:
+        copy.wait()
 
 
 def gate_up(rows, gate_mat, up_mat):
-    n_pieces = 2 * len(piece_places(rows.shape[0], gate_mat.shape[1]))
+    capacity, ff = rows.shape[0], gate_mat.shape[1]
+    n_pieces = 2 * len(piece_places(capacity, ff))
     return pl.pallas_call(
         gate_up_kernel,
-        out_shape=[jax.ShapeDtypeStruct((PIECE_ROWS, PIECE_COLS), jnp.float32)] * n_pieces,
+        out_shape=[pltpu.HBM((PIECE_ROWS, PIECE_COLS), jnp.float32)] * n_pieces
+        + [pltpu.HBM((8, 128), jnp.float32)],
         in_specs=[pl.BlockSpec(memory_space=pltpu.VMEM)] * 3,
-        out_specs=[pl.BlockSpec(memory_space=pltpu.VMEM)] * n_pieces,
+        out_specs=[pl.BlockSpec(memory_space=pltpu.HBM)] * (n_pieces + 1),
+        scratch_shapes=[
+            pltpu.VMEM((2, capacity, ff), jnp.float32),
+            pltpu.VMEM((8, 128), jnp.float32),
+            pltpu.SemaphoreType.DMA((n_pieces + 1,)),
+        ],
         compiler_params=pltpu.CompilerParams(vmem_limit_bytes=VMEM_BYTES),
         name="gate_up",
     )(rows, gate_mat, up_mat)
 
 
 def tail_kernel(down_ref, combine_ref, slot_ref, *refs):
-    out_ref, hidden_ref = refs[-2:]
-    pieces = refs[:-2]
-    capacity, ff = hidden_ref.shape
-    half = len(pieces) // 2
-    for k, (r, c) in enumerate(piece_places(capacity, ff)):
-        gate = pieces[k][...]
-        up = pieces[half + k][...]
-        hidden_ref[r : r + PIECE_ROWS, c : c + PIECE_COLS] = (gate / (1.0 + jnp.exp(-gate)) * up).astype(
-            jnp.bfloat16
-        )
-    expert_out = jnp.dot(hidden_ref[...], down_ref[...], preferred_element_type=jnp.float32)
+    out_ref, sums_ref, sems = refs[-3:]
+    pieces = refs[:-4]
+    capacity, ff = sums_ref.shape[1:]
+    places = piece_places(capacity, ff)
+    copies = []
+    for half in range(2):
+        for k, (r, c) in enumerate(places):
+            n = half * len(places) + k
+            copy = pltpu.make_async_copy(
+                pieces[n], sums_ref.at[half, r : r + PIECE_ROWS, c : c + PIECE_COLS], sems.at[n]
+            )
+            copy.start()
+            copies.append(copy)
+    for copy in copies:
+        copy.wait()
+    gate = sums_ref[0]
+    hidden = (gate / (1.0 + jnp.exp(-gate)) * sums_ref[1]).astype(jnp.bfloat16)
+    expert_out = jnp.dot(hidden, down_ref[...], preferred_element_type=jnp.float32)
     weighted = (combine_ref[...] * expert_out).astype(jnp.bfloat16)
     slots = out_ref.shape[0]
     slot_ids = lax.broadcasted_iota(jnp.int32, (slots, capacity), 0)
@@ -64,18 +83,22 @@
     out_ref[...] = jnp.dot(table, weighted, preferred_element_type=jnp.float32).astype(jnp.bfloat16)
 
 
-def expert_tail(pieces, down_mat, combine, slot, slots):
+def expert_tail(sums, down_mat, combine, slot, slots):
     ff, width = down_mat.shape
     capacity = combine.shape[0]
     return pl.pallas_call(
         tail_kernel,
         out_shape=jax.ShapeDtypeStruct((slots, width), jnp.bfloat16),
-        in_specs=[pl.BlockSpec(memory_space=pltpu.VMEM)] * (3 + len(pieces)),
+        in_specs=[pl.BlockSpec(memory_space=pltpu.VMEM)] * 3
+        + [pl.BlockSpec(memory_space=pltpu.HBM)] * len(sums),
         out_specs=pl.BlockSpec(memory_space=pltpu.VMEM),
-        scratch_shapes=[pltpu.VMEM((capacity, ff), jnp.bfloat16)],
-        compiler_params=pltpu.CompilerParams(vmem_limit_bytes=VMEM_BYTES),
+        scratch_shapes=[
+            pltpu.VMEM((2, capacity, ff), jnp.float32),
+            pltpu.SemaphoreType.DMA((len(sums) - 1,)),
+        ],
+        compiler_params=pltpu.CompilerParams(vmem_limit_bytes=TAIL_VMEM_BYTES),
         name="expert_tail",
-    )(down_mat, combine[:, None], slot[None, :], *pieces)
+    )(down_mat, combine[:, None], slot[None, :], *sums)
 
 
 def shards(

time: 333 us -> 259 us (0.78)
  local copies, waits for them, and re-layouts: 82.7 us -> 5.3 us
  Pallas kernels: 2.74 us -> 8.31 us
    unnamed x265 -> x15, local copies, waits for them, and re-layouts: 81.1 us -> 3.75 us
    pallas_call x1, Pallas kernels: 1.77 us -> 5.54 us  [expert_tail(): pl.pallas_call(tail_kernel, out_shape=jax.ShapeDtypeStruct((slots, width)...]
  transfers between devices with their start and end apart: 3 -> 3, of which waited for: 2 -> 2; matrix products, arithmetic and copies ran while one was open for 2% -> 2% of each run, Pallas kernels for 1% -> 3%
where the time goes in v2:
time: 259 us; the launch traced here: 258 us
  blocking collectives  104 us (40%)
  waiting for transfers between devices  98 us (38%)
  starting transfers between devices  16.2 us (6%)
  between operations  13.5 us (5%)
  matrix products  11.5 us (4%)
  Pallas kernels  8.31 us (3%)
  local copies, waits for them, and re-layouts  5.3 us (2%)
    all_gather x1, waiting for transfers between devices, shards(): full_gained = lax.all_gather(gained, 'tensor', axis=1, tiled=True)  86.3 us
    psum x1, blocking collectives, shards(): sums = lax.psum(tuple(parts), 'tensor')  81 us
    psum x1, blocking collectives, shards(): square_total = lax.psum(jnp.sum(mixed * mixed, axis=1), 'tensor')  23.1 us
    all_to_all x1, starting transfers between devices, shards(): lax.all_to_all(outgoing, 'expert', split_axis=0, concat_axis=0, tiled=True)  16.2 us
    all_to_all x1, waiting for transfers between devices, shards(): lax.all_to_all(outgoing, 'expert', split_axis=0, concat_axis=0, tiled=True)  11 us
    dot_general x1, matrix products, shards(): jnp.dot(full_gained, full_projection, preferred_element_type=jnp.float32)  9.74 us
    pallas_call x1, Pallas kernels, expert_tail(): pl.pallas_call(tail_kernel, out_shape=jax.ShapeDtypeStruct((slots, width)...  5.54 us
  transfers between devices with their start and end apart: 3, of which 2 were waited for; matrix products, arithmetic and copies ran while one was open for 2% of the time, Pallas kernels for 3%

profile of v2, /device:TPU:1, one launch (start us, length us, event | category | flops | bytes accessed | tf_op | source)
XLA Modules:
  0.0 258.4 jit_solution(12197871755889465381)
XLA Ops:
  6.5 0.0 all-gather.5.cloned.1.call-start
  6.5 0.7 all-gather.5.cloned.1.call-update
  7.3 1.5 copy.15.combine_ref
  8.7 0.0 copy-start
  8.7 1.3 copy-done
  10.0 0.0 copy-start.1
  10.0 1.3 copy-done.1
  11.3 0.0 copy-start.2
  11.3 0.9 copy-done.2
  12.2 2.8 %gate_up.1 = (f32[16,768]{1,0:T(8,128)}, f32[16,768]{1,0:T(8,128)}, f32[16,768]{1,0:T(8,128)}, f32[16,768]{1,0:T(8,128)}, f32[16,768]{1,0:T(8,128)}, /*index=5*/...) custom-call(bf16[256,384]{1,0:T(8,128)(2,1)S(1)} %bitcast.15, ...), custom_call_target="tpu_custom_call" | custom-call | tf_op jit(solution)/shard_map/gate_up/pallas_call | solution.py:44
  15.0 0.0 copy-start.4
  15.0 81.0 %all-reduce.2 = (f32[16,768]{1,0:T(8,128)}, f32[16,768]{1,0:T(8,128)}, f32[16,768]{1,0:T(8,128)}, f32[16,768]{1,0:T(8,128)}, f32[16,768]{1,0:T(8,128)}, /*index=...) all-reduce(f32[16,768]{1,0:T(8,128)} %get-tuple-element.70, ...), channel_id=1, replica_groups=mesh['expert'=32,'tensor'=16] {'tensor'}, use_global_device_ids=true, to_apply=%region_2.3 | all-reduce | flops 787456 | bytes 6299648 | tf_op jit(solution)/shard_map/psum | solution.py:144
  96.0 0.0 copy-done.4
  96.0 0.1 convert_reduce_fusion
  96.2 0.5 multiply_add_fusion.slot_ref
  96.7 5.5 %expert_tail.1 = bf16[768,384]{1,0:T(8,128)(2,1)} custom-call(bf16[1536,384]{1,0:T(8,128)(2,1)} %bitcast.17, f32[256,1]{1,0:T(8,128)} %copy.15.combine_ref, s32[1,256]{1,0:T(1,128)} %multiply_add_fusion.slot_ref, f32[16,768]{1,0:T(8,128)} %get-tuple-element.135.refs_0_, f32[16,768]{1,0:T(8,128)} %get-tuple-element.136.refs_1_, ...), custom_call_target="tpu_custom_call" | custom-call | tf_op jit(solution)/shard_map/expert_tail/pallas_call | solution.py:89
  102.3 0.0 copy-start.5
  102.3 0.0 copy-start.3
  102.3 0.0 copy-start.6
  102.3 16.2 %all-to-all-start = ((bf16[32,24,384]{2,1,0:T(8,128)(2,1)}), bf16[32,24,384]{2,1,0:T(8,128)(2,1)S(1)}, u32[]{:S(2)}, u32[]{:S(2)}) async-start(bf16[32,24,384]{2,1,0:T(8,128)(2,1)} %bitcast.16), calls=%async_computation | async-start | bytes 1179648 | tf_op jit(solution)/shard_map/all_to_all | solution.py:147
  118.5 0.0 all-gather.3.cloned.1.call-start
  118.5 0.0 copy-done.5
  118.6 0.2 convolution_convert_fusion
  118.7 0.6 select_reduce_fusion
  119.4 0.1 sub.7
  119.4 0.0 copy-done.3
  119.5 0.3 copy.14
  119.7 11.0 %all-to-all-done = bf16[32,24,384]{2,1,0:T(8,128)(2,1)S(1)} async-done(((bf16[32,24,384]{2,1,0:T(8,128)(2,1)}), bf16[32,24,384]{2,1,0:T(8,128)(2,1)S(1)}, u32[]{:S(2)}, u32[]{:S(2)}) %all-to-all-start) | async-done | bytes 589856 | tf_op jit(solution)/shard_map/all_to_all | solution.py:147
  130.8 0.0 copy-done.6
  130.8 1.6 multiply_reduce_fusion
  132.4 0.0 all-gather.3.cloned.1.call-update
  132.4 23.1 %psum.527 = f32[768]{0:T(1024)S(1)} all-reduce(f32[768]{0:T(1024)S(1)} %get-tuple-element.200), channel_id=1, replica_groups=mesh['expert'=32,'tensor'=16] {'tensor'}, use_global_device_ids=true, to_apply=%region_68.69 | all-reduce | flops 768 | bytes 6144 | tf_op jit(solution)/shard_map/psum | solution.py:156
  155.5 0.0 all-gather.5.cloned.1.call-done
  155.5 86.3 %all-gather.3.cloned.1.call-done = bf16[768,6144]{0,1:T(8,128)(2,1)} async-done(((bf16[768,384]{0,1:T(8,128)(2,1)}), bf16[768,6144]{0,1:T(8,128)(2,1)}) %all-gather.3.cloned.1.call-update) | async-done | bytes 9437200 | tf_op jit(solution)/shard_map/all_gather | solution.py:155
  241.8 9.7 %fusion.2 = bf16[768,384]{1,0:T(8,128)(2,1)} fusion(bf16[768,6144]{0,1:T(8,128)(2,1)} %all-gather.3.cloned.1.call-done, bf16[6144,384]{1,0:T(8,128)(2,1)} %all-gather.5.cloned.1.call-done, f32[768]{0:T(1024)S(1)} %add_rsqrt_fusion), kind=kOutput, calls=%fused_computation.4 | convolution fusion | flops 3624468480 | bytes 14748672 | tf_op jit(solution)/shard_map/dot_general | solution.py:158
  (5 shorter events, 0.0 us)
Async XLA Ops:
  6.5 149.0 %all-gather.5.cloned.1.call-start = ((), (), s32[]{:S(2)}) async-start(), calls=%async_computation.2 | async-start | bytes 4866048 | tf_op jit(solution)/shard_map/all_gather | solution.py:123
  8.7 1.3 copy-start
  10.0 1.3 copy-start.1
  11.3 0.9 copy-start.2
  15.0 81.1 %copy-start.4 = (s32[32,256]{1,0:T(8,128)S(1)}, s32[32,256]{1,0:T(8,128)}, u32[]{:S(2)}) copy-start(s32[32,256]{1,0:T(8,128)} %param.15) | copy-start | bytes 98308
  102.3 16.3 %copy-start.5 = (s32[32,256]{1,0:T(8,128)S(1)}, s32[32,256]{1,0:T(8,128)}, u32[]{:S(2)}) copy-start(s32[32,256]{1,0:T(8,128)} %param.16) | copy-start | bytes 98308
  102.3 17.2 %copy-start.3 = (bf16[768,384]{1,0:T(8,128)(2,1)S(1)}, bf16[768,384]{1,0:T(8,128)(2,1)}, u32[]{:S(2)}) copy-start(bf16[768,384]{1,0:T(8,128)(2,1)} %param.17) | copy-start | bytes 1769476
  102.3 28.5 %copy-start.6 = (f32[384]{0:T(512)S(1)}, f32[384]{0:T(512)}, u32[]{:S(2)}) copy-start(f32[384]{0:T(512)} %param.18) | copy-start | bytes 4612
  102.3 28.5 %all-to-all-start = ((bf16[32,24,384]{2,1,0:T(8,128)(2,1)}), bf16[32,24,384]{2,1,0:T(8,128)(2,1)S(1)}, u32[]{:S(2)}, u32[]{:S(2)}) async-start(bf16[32,24,384]{2,1,0:T(8,128)(2,1)} %bitcast.16), calls=%async_computation | async-start | bytes 1179648 | tf_op jit(solution)/shard_map/all_to_all | solution.py:147
  118.5 123.3 %all-gather.3.cloned.1.call-start = ((), (), s32[]{:S(2)}) async-start(), calls=%async_computation.1 | async-start | bytes 10027008 | tf_op jit(solution)/shard_map/all_gather | solution.py:155
Sparse Core Ops, SparseCore 0:
  10.5 67.9 all-gather.4
  132.5 109.2 all-gather.2

commit v3 on v2

--- a/solution.py
+++ b/solution.py
@@ -1,3 +1,5 @@
+import functools
+
 import jax
 import jax.numpy as jnp
 from jax import lax
@@ -10,6 +12,8 @@
 PIECE_COLS = 768
 VMEM_BYTES = 48 * 1024 * 1024
 TAIL_VMEM_BYTES = 63 * 1024 * 1024
+RING_ROWS = 384
+EXTRA_ROWS = 16
 
 
 def piece_places(capacity, ff):
@@ -76,7 +80,8 @@
     gate = sums_ref[0]
     hidden = (gate / (1.0 + jnp.exp(-gate)) * sums_ref[1]).astype(jnp.bfloat16)
     expert_out = jnp.dot(hidden, down_ref[...], preferred_element_type=jnp.float32)
-    weighted = (combine_ref[...] * expert_out).astype(jnp.bfloat16)
+    combine = jnp.broadcast_to(combine_ref[...], (128, capacity)).T[:, 0:1]
+    weighted = (combine * expert_out).astype(jnp.bfloat16)
     slots = out_ref.shape[0]
     slot_ids = lax.broadcasted_iota(jnp.int32, (slots, capacity), 0)
     table = jnp.where(slot_ref[...] == slot_ids, 1.0, 0.0).astype(jnp.bfloat16)
@@ -98,7 +103,124 @@
         ],
         compiler_params=pltpu.CompilerParams(vmem_limit_bytes=TAIL_VMEM_BYTES),
         name="expert_tail",
-    )(down_mat, combine[:, None], slot[None, :], *sums)
+    )(down_mat, combine[None, :], slot[None, :], *sums)
+
+
+def mix_kernel(residual_ref, received_ref, row_ref, gain_ref, ring_ref, gather_ref):
+    tokens, width = residual_ref.shape
+    slots = received_ref.shape[0]
+    token_ids = lax.broadcasted_iota(jnp.int32, (tokens, slots), 0)
+    table = jnp.where(row_ref[...] == token_ids, 1.0, 0.0).astype(jnp.bfloat16)
+    moe = jnp.dot(table, received_ref[...], preferred_element_type=jnp.float32)
+    mixed = residual_ref[...].astype(jnp.float32) + moe
+    gained = (mixed * gain_ref[...]).astype(jnp.bfloat16)
+    ring_rows = ring_ref.shape[0]
+    rest = tokens - ring_rows
+    ring_ref[...] = gained[:ring_rows]
+    gather_ref[:rest] = gained[ring_rows:]
+    squares = jnp.sum(mixed * mixed, axis=1, keepdims=True)
+    flat = jnp.broadcast_to(squares, (tokens, 128)).T[0:1]
+    high = flat.astype(jnp.bfloat16).astype(jnp.float32)
+    low = flat - high
+    lines = [part[:, i : i + width] for part in (high, low) for i in range(0, tokens, width)]
+    lines.append(jnp.zeros((EXTRA_ROWS - len(lines), width), jnp.float32))
+    gather_ref[rest:] = jnp.concatenate(lines, axis=0).astype(jnp.bfloat16)
+
+
+def mix(residual, received, row_of, gain, ring_rows):
+    tokens, width = residual.shape
+    return pl.pallas_call(
+        mix_kernel,
+        out_shape=[
+            jax.ShapeDtypeStruct((ring_rows, width), jnp.bfloat16),
+            jax.ShapeDtypeStruct((tokens - ring_rows + EXTRA_ROWS, width), jnp.bfloat16),
+        ],
+        in_specs=[pl.BlockSpec(memory_space=pltpu.VMEM)] * 4,
+        out_specs=[pl.BlockSpec(memory_space=pltpu.VMEM)] * 2,
+        compiler_params=pltpu.CompilerParams(vmem_limit_bytes=VMEM_BYTES),
+        name="mix",
+    )(residual, received, row_of[None, :], gain[None, :])
+
+
+def final_kernel(gathered_ref, proj_ref, ring_ref, out_ref, acc_ref, squares_ref):
+    step = pl.program_id(0)
+
+    @pl.when(step == 0)
+    def _():
+        acc_ref[...] = jnp.zeros_like(acc_ref)
+        squares_ref[...] = jnp.zeros_like(squares_ref)
+
+    per_step, rows, width = gathered_ref.shape
+    rest = rows - EXTRA_ROWS
+    total = acc_ref[...]
+    for z in range(per_step):
+        total += jnp.dot(
+            gathered_ref[z, :rest],
+            proj_ref[z * width : (z + 1) * width],
+            preferred_element_type=jnp.float32,
+        )
+        squares_ref[...] += gathered_ref[z, rest:].astype(jnp.float32)
+    acc_ref[...] = total
+
+    @pl.when(step == pl.num_programs(0) - 1)
+    def _():
+        tokens = out_ref.shape[0]
+        ring_rows = tokens - rest
+        lines = tokens // width
+        columns = []
+        for i in range(lines):
+            line = squares_ref[i : i + 1] + squares_ref[lines + i : lines + i + 1]
+            columns.append(jnp.broadcast_to(line, (128, width)).T[:, 0:1])
+        squares = jnp.concatenate(columns, axis=0)
+        inverse = lax.rsqrt(squares / D + 1e-05)
+        out_ref[:ring_rows] = (ring_ref[...] * inverse[:ring_rows]).astype(jnp.bfloat16)
+        out_ref[ring_rows:] = (acc_ref[...] * inverse[ring_rows:]).astype(jnp.bfloat16)
+
+
+def final(gathered, full_projection, ring_acc, tokens):
+    n, rows, width = gathered.shape
+    columns = full_projection.shape[1]
+    rest = rows - EXTRA_ROWS
+    per_step = 4
+    return pl.pallas_call(
+        final_kernel,
+        grid=(n // per_step,),
+        out_shape=jax.ShapeDtypeStruct((tokens, columns), jnp.bfloat16),
+        in_specs=[
+            pl.BlockSpec((per_step, rows, width), lambda i: (i, 0, 0)),
+            pl.BlockSpec((per_step * width, columns), lambda i: (i, 0)),
+            pl.BlockSpec((tokens - rest, columns), lambda i: (0, 0)),
+        ],
+        out_specs=pl.BlockSpec((tokens, columns), lambda i: (0, 0)),
+        scratch_shapes=[
+            pltpu.VMEM((rest, columns), jnp.float32),
+            pltpu.VMEM((EXTRA_ROWS, width), jnp.float32),
+        ],
+        compiler_params=pltpu.CompilerParams(vmem_limit_bytes=TAIL_VMEM_BYTES),
+        name="final",
+    )(gathered, full_projection, ring_acc)
+
+
+def ring_projection(rows, full_projection, axis, n):
+    me = lax.axis_index(axis)
+    width = rows.shape[1]
+    onward = [(i, (i + 1) % n) for i in range(n)]
+    back = [(i, (i - 1) % n) for i in range(n)]
+
+    def product(block, source):
+        part = lax.dynamic_slice_in_dim(full_projection, lax.rem(source, n) * width, width, 0)
+        return jnp.dot(block, part, preferred_element_type=jnp.float32)
+
+    total = product(rows, me)
+    ahead = behind = rows
+    for k in range(1, n // 2 + 1):
+        ahead = lax.ppermute(ahead, axis, onward)
+        if k < n - k:
+            behind = lax.ppermute(behind, axis, back)
+        total = total + product(ahead, me + (n - k))
+        if k < n - k:
+            total = total + product(behind, me + k)
+    return total
 
 
 def shards(
@@ -112,6 +234,7 @@
     residual_in,
     norm_gain,
     projection,
+    n_tensor,
 ):
     my_rows = picked_rows[0]
     capacity = my_rows.shape[0]
@@ -120,9 +243,9 @@
     tok_group, width = residual_in.shape
     my_index = lax.axis_index("expert")
 
+    parts = gate_up(my_rows, w_gate[0], w_up[0])
+    spare, projection = lax.optimization_barrier((parts[-1], projection))
     full_projection = lax.all_gather(projection, "expert", axis=0, tiled=True)
-
-    parts = gate_up(my_rows, w_gate[0], w_up[0])
 
     my_owner = lax.dynamic_index_in_dim(pick_owner, my_index, 0, keepdims=False)
     pick_ids = jnp.arange(capacity, dtype=jnp.int32)
@@ -138,30 +261,26 @@
     slot_range = jnp.arange(slot_most, dtype=jnp.int32)
     matches = mine[:, None, :] & (position[:, None, :] == slot_range[None, :, None])
     row_of = jnp.sum(jnp.where(matches, pick_row[:, None, :] + 1, 0), axis=2) - 1
-    token_ids = jnp.arange(tok_group, dtype=jnp.int32)
-    recv_table = (row_of.reshape(-1)[None, :] == token_ids[:, None]).astype(jnp.bfloat16)
-
-    sums = lax.psum(tuple(parts), "tensor")
+
+    sums = lax.psum((*parts[:-1], spare), "tensor")
     outgoing = expert_tail(sums, w_down[0], combine_gate[0], my_slot, n_groups * slot_most)
     outgoing = outgoing.reshape(n_groups, slot_most, width)
     received = lax.all_to_all(outgoing, "expert", split_axis=0, concat_axis=0, tiled=True)
-    moe = jnp.dot(
-        recv_table,
+    ring_rows, gather_rows = mix(
+        residual_in,
         received.reshape(n_groups * slot_most, width),
-        preferred_element_type=jnp.float32,
+        row_of.reshape(-1),
+        norm_gain,
+        RING_ROWS,
     )
-    mixed = residual_in.astype(jnp.float32) + moe
-    gained = (mixed * norm_gain[None, :]).astype(jnp.bfloat16)
-    full_gained = lax.all_gather(gained, "tensor", axis=1, tiled=True)
-    square_total = lax.psum(jnp.sum(mixed * mixed, axis=1), "tensor")
-    inverse_rms = lax.rsqrt(square_total / D + 1e-05)
-    projected = jnp.dot(full_gained, full_projection, preferred_element_type=jnp.float32)
-    return (projected * inverse_rms[:, None]).astype(jnp.bfloat16)
+    gathered = lax.all_gather(gather_rows, "tensor")
+    ring_acc = ring_projection(ring_rows, full_projection, "tensor", n_tensor)
+    return final(gathered, full_projection, ring_acc, tok_group)
 
 
 def solution(mesh):
     return jax.shard_map(
-        shards,
+        functools.partial(shards, n_tensor=mesh.shape["tensor"]),
         mesh=mesh,
         in_specs=(
             P("expert", None, "tensor"),

time: 259 us -> 269 us (1.039)
  starting transfers between devices: 16.2 us -> 65.2 us
  waiting for transfers between devices: 98 us -> 69.8 us
  blocking collectives: 104 us -> 81.1 us
  Pallas kernels: 8.31 us -> 17.4 us
    all_gather x1, waiting for transfers between devices: 86.3 us -> 0.01 us  [shards(): gathered = lax.all_gather(gather_rows, 'tensor')]
    ppermute x0 -> x15, waiting for transfers between devices: none -> 58.4 us  [the longest x8 55.4 us: ring_projection(): ahead = lax.ppermute(ahead, axis, onward)]
    ppermute x0 -> x15, starting transfers between devices: none -> 49.2 us  [the longest x7 33.4 us: ring_projection(): behind = lax.ppermute(behind, axis, back)]
    psum x2 -> x1, blocking collectives: 104 us -> 81.1 us  [shards(): sums = lax.psum((*parts[:-1], spare), 'tensor')]
    pallas_call x0 -> x2, Pallas kernels: none -> 9.18 us  [the longest x1 7.41 us: final(): pl.pallas_call(final_kernel, grid=(n // per_step,), out_shape=jax.ShapeDt...]
    dot_general x2 -> x16, matrix products: 11.4 us -> 13.3 us  [product(): return jnp.dot(block, part, preferred_element_type=jnp.float32)]
  transfers between devices with their start and end apart: 3 -> 18, of which waited for: 2 -> 10; matrix products, arithmetic and copies ran while one was open for 2% -> 6% of each run, Pallas kernels for 3% -> 3%
where the time goes in v3:
time: 269 us; the launch traced here: 266 us
  blocking collectives  81.1 us (30%)
  waiting for transfers between devices  69.8 us (26%)
  starting transfers between devices  65.2 us (24%)
  Pallas kernels  17.4 us (6%)
  between operations  13.9 us (5%)
  matrix products  13.4 us (5%)
  local copies, waits for them, and re-layouts  3.59 us (1%)
    psum x1, blocking collectives, shards(): sums = lax.psum((*parts[:-1], spare), 'tensor')  81.1 us
    ppermute x8, waiting for transfers between devices, ring_projection(): ahead = lax.ppermute(ahead, axis, onward)  55.4 us
    ppermute x7, starting transfers between devices, ring_projection(): behind = lax.ppermute(behind, axis, back)  33.4 us
    all_to_all x1, starting transfers between devices, shards(): lax.all_to_all(outgoing, 'expert', split_axis=0, concat_axis=0, tiled=True)  16 us
    ppermute x8, starting transfers between devices, ring_projection(): ahead = lax.ppermute(ahead, axis, onward)  15.7 us
    dot_general x16, matrix products, product(): return jnp.dot(block, part, preferred_element_type=jnp.float32)  13.3 us
    all_to_all x1, waiting for transfers between devices, shards(): lax.all_to_all(outgoing, 'expert', split_axis=0, concat_axis=0, tiled=True)  11.3 us
    pallas_call x1, Pallas kernels, final(): pl.pallas_call(final_kernel, grid=(n // per_step,), out_shape=jax.ShapeDt...  7.41 us
  transfers between devices with their start and end apart: 18, of which 10 were waited for; matrix products, arithmetic and copies ran while one was open for 6% of the time, Pallas kernels for 3%

profile of v3, /device:TPU:1, one launch (start us, length us, event | category | flops | bytes accessed | tf_op | source)
XLA Modules:
  0.0 265.8 jit_solution(18415434617322655887)
XLA Ops:
  6.5 1.3 copy-done
  7.8 1.3 copy-done.1
  9.1 0.9 copy-done.3
  10.0 2.8 %gate_up.1 = (f32[16,768]{1,0:T(8,128)}, f32[16,768]{1,0:T(8,128)}, f32[16,768]{1,0:T(8,128)}, f32[16,768]{1,0:T(8,128)}, f32[16,768]{1,0:T(8,128)}, /*index=5*/...) custom-call(bf16[256,384]{1,0:T(8,128)(2,1)S(1)} %bitcast.29, ...), custom_call_target="tpu_custom_call" | custom-call | tf_op jit(solution)/shard_map/gate_up/pallas_call | solution.py:48
  12.8 81.1 %all-reduce.2 = (f32[16,768]{1,0:T(8,128)}, f32[16,768]{1,0:T(8,128)}, f32[16,768]{1,0:T(8,128)}, f32[16,768]{1,0:T(8,128)}, f32[16,768]{1,0:T(8,128)}, /*index=...) all-reduce(f32[16,768]{1,0:T(8,128)} %get-tuple-element.74, ...), channel_id=1, replica_groups=mesh['expert'=32,'tensor'=16] {'tensor'}, use_global_device_ids=true, to_apply=%region_1.2 | all-reduce | flops 787456 | bytes 6299648 | tf_op jit(solution)/shard_map/psum | solution.py:265
  94.1 0.6 multiply_add_fusion.slot_ref
  94.7 5.5 %expert_tail.1 = bf16[768,384]{1,0:T(8,128)(2,1)} custom-call(bf16[1536,384]{1,0:T(8,128)(2,1)} %bitcast.32, f32[1,256]{1,0:T(1,128)} %combine_ref.1, s32[1,256]{1,0:T(1,128)} %multiply_add_fusion.slot_ref, f32[16,768]{1,0:T(8,128)} %get-tuple-element.143.refs_0_, f32[16,768]{1,0:T(8,128)} %get-tuple-element.144.refs_1_, ...), custom_call_target="tpu_custom_call" | custom-call | tf_op jit(solution)/shard_map/expert_tail/pallas_call | solution.py:94
  100.2 16.0 %all-to-all-start = ((bf16[32,24,384]{2,1,0:T(8,128)(2,1)}), bf16[32,24,384]{2,1,0:T(8,128)(2,1)S(1)}, u32[]{:S(2)}, u32[]{:S(2)}) async-start(bf16[32,24,384]{2,1,0:T(8,128)(2,1)} %bitcast.31), calls=%async_computation | async-start | bytes 1179648 | tf_op jit(solution)/shard_map/all_to_all | solution.py:268
  116.4 0.6 select_reduce_fusion
  117.2 11.3 %all-to-all-done = bf16[32,24,384]{2,1,0:T(8,128)(2,1)S(1)} async-done(((bf16[32,24,384]{2,1,0:T(8,128)(2,1)}), bf16[32,24,384]{2,1,0:T(8,128)(2,1)S(1)}, u32[]{:S(2)}, u32[]{:S(2)}) %all-to-all-start) | async-done | bytes 589856 | tf_op jit(solution)/shard_map/all_to_all | solution.py:268
  128.4 1.8 mix.1
  130.2 2.2 collective-permute-start
  132.4 4.3 %collective-permute-start.1 = (bf16[384,384]{1,0:T(8,128)(2,1)S(1)}, bf16[384,384]{1,0:T(8,128)(2,1)S(1)}, u32[]{:S(2)}, u32[]{:S(2)}) collective-permute-start(bf16[384,384]{1,0:T(8,128)(2,1)S(1)} %get-tuple-element.142), channel_id=1, source_target_pairs={{0,15},{1,0},{2,1},{3,2},{4,3},{5,4},{6,5},{7,6},{8,7},{9,8},{10,9... | collective-permute-start | bytes 884744 | tf_op jit(solution)/shard_map/ppermute | solution.py:219
  136.7 5.4 %collective-permute-done = bf16[384,384]{1,0:T(8,128)(2,1)S(1)} collective-permute-done((bf16[384,384]{1,0:T(8,128)(2,1)S(1)}, bf16[384,384]{1,0:T(8,128)(2,1)S(1)}, u32[]{:S(2)}, u32[]{:S(2)}) %collective-permute-start) | collective-permute-done | bytes 294944 | tf_op jit(solution)/shard_map/ppermute | solution.py:217
  142.1 1.9 collective-permute-start.2
  144.0 2.3 collective-permute-done.1
  146.4 5.4 %collective-permute-start.3 = (bf16[384,384]{1,0:T(8,128)(2,1)S(1)}, bf16[384,384]{1,0:T(8,128)(2,1)S(1)}, u32[]{:S(2)}, u32[]{:S(2)}) collective-permute-start(bf16[384,384]{1,0:T(8,128)(2,1)S(1)} %collective-permute-done.1), channel_id=1, source_target_pairs={{0,15},{1,0},{2,1},{3,2},{4,3},{5,4},{6,5},{7,6},{8,7},{9,8},{10,9... | collective-permute-start | bytes 884744 | tf_op jit(solution)/shard_map/ppermute | solution.py:219
  151.8 8.2 %collective-permute-done.2 = bf16[384,384]{1,0:T(8,128)(2,1)S(1)} collective-permute-done((bf16[384,384]{1,0:T(8,128)(2,1)S(1)}, bf16[384,384]{1,0:T(8,128)(2,1)S(1)}, u32[]{:S(2)}, u32[]{:S(2)}) %collective-permute-start.2) | collective-permute-done | bytes 294944 | tf_op jit(solution)/shard_map/ppermute | solution.py:217
  160.0 1.9 collective-permute-start.4
  161.9 0.7 collective-permute-done.3
  162.7 5.4 %collective-permute-start.5 = (bf16[384,384]{1,0:T(8,128)(2,1)S(1)}, bf16[384,384]{1,0:T(8,128)(2,1)S(1)}, u32[]{:S(2)}, u32[]{:S(2)}) collective-permute-start(bf16[384,384]{1,0:T(8,128)(2,1)S(1)} %collective-permute-done.3), channel_id=1, source_target_pairs={{0,15},{1,0},{2,1},{3,2},{4,3},{5,4},{6,5},{7,6},{8,7},{9,8},{10,9... | collective-permute-start | bytes 884744 | tf_op jit(solution)/shard_map/ppermute | solution.py:219
  168.1 9.8 %collective-permute-done.4 = bf16[384,384]{1,0:T(8,128)(2,1)S(1)} collective-permute-done((bf16[384,384]{1,0:T(8,128)(2,1)S(1)}, bf16[384,384]{1,0:T(8,128)(2,1)S(1)}, u32[]{:S(2)}, u32[]{:S(2)}) %collective-permute-start.4) | collective-permute-done | bytes 294944 | tf_op jit(solution)/shard_map/ppermute | solution.py:217
  177.9 1.9 collective-permute-start.6
  179.8 4.6 %collective-permute-start.7 = (bf16[384,384]{1,0:T(8,128)(2,1)S(1)}, bf16[384,384]{1,0:T(8,128)(2,1)S(1)}, u32[]{:S(2)}, u32[]{:S(2)}) collective-permute-start(bf16[384,384]{1,0:T(8,128)(2,1)S(1)} %collective-permute-done.5), channel_id=1, source_target_pairs={{0,15},{1,0},{2,1},{3,2},{4,3},{5,4},{6,5},{7,6},{8,7},{9,8},{10,9... | collective-permute-start | bytes 884744 | tf_op jit(solution)/shard_map/ppermute | solution.py:219
  184.4 10.1 %collective-permute-done.6 = bf16[384,384]{1,0:T(8,128)(2,1)S(1)} collective-permute-done((bf16[384,384]{1,0:T(8,128)(2,1)S(1)}, bf16[384,384]{1,0:T(8,128)(2,1)S(1)}, u32[]{:S(2)}, u32[]{:S(2)}) %collective-permute-start.6) | collective-permute-done | bytes 294944 | tf_op jit(solution)/shard_map/ppermute | solution.py:217
  194.5 1.9 collective-permute-start.8
  196.5 4.6 %collective-permute-start.9 = (bf16[384,384]{1,0:T(8,128)(2,1)S(1)}, bf16[384,384]{1,0:T(8,128)(2,1)}, u32[]{:S(2)}, u32[]{:S(2)}) collective-permute-start(bf16[384,384]{1,0:T(8,128)(2,1)S(1)} %collective-permute-done.7), channel_id=1, source_target_pairs={{0,15},{1,0},{2,1},{3,2},{4,3},{5,4},{6,5},{7,6},{8,7},{9,8},{10,9... | collective-permute-start | bytes 884744 | tf_op jit(solution)/shard_map/ppermute | solution.py:219
  201.1 10.0 %collective-permute-done.8 = bf16[384,384]{1,0:T(8,128)(2,1)S(1)} collective-permute-done((bf16[384,384]{1,0:T(8,128)(2,1)S(1)}, bf16[384,384]{1,0:T(8,128)(2,1)S(1)}, u32[]{:S(2)}, u32[]{:S(2)}) %collective-permute-start.8) | collective-permute-done | bytes 294944 | tf_op jit(solution)/shard_map/ppermute | solution.py:217
  211.0 1.9 collective-permute-start.10
  213.0 4.6 %collective-permute-start.11 = (bf16[384,384]{1,0:T(8,128)(2,1)}, bf16[384,384]{1,0:T(8,128)(2,1)S(1)}, u32[]{:S(2)}, u32[]{:S(2)}) collective-permute-start(bf16[384,384]{1,0:T(8,128)(2,1)} %collective-permute-done.9), channel_id=1, source_target_pairs={{0,15},{1,0},{2,1},{3,2},{4,3},{5,4},{6,5},{7,6},{8,7},{9,8},{10,9... | collective-permute-start | bytes 884744 | tf_op jit(solution)/shard_map/ppermute | solution.py:219
  217.5 8.5 %collective-permute-done.10 = bf16[384,384]{1,0:T(8,128)(2,1)S(1)} collective-permute-done((bf16[384,384]{1,0:T(8,128)(2,1)S(1)}, bf16[384,384]{1,0:T(8,128)(2,1)S(1)}, u32[]{:S(2)}, u32[]{:S(2)}) %collective-permute-start.10) | collective-permute-done | bytes 294944 | tf_op jit(solution)/shard_map/ppermute | solution.py:217
  226.1 1.9 collective-permute-start.12
  228.1 4.6 %collective-permute-start.13 = (bf16[384,384]{1,0:T(8,128)(2,1)S(1)}, bf16[384,384]{1,0:T(8,128)(2,1)}, u32[]{:S(2)}, u32[]{:S(2)}) collective-permute-start(bf16[384,384]{1,0:T(8,128)(2,1)S(1)} %collective-permute-done.11), channel_id=1, source_target_pairs={{0,15},{1,0},{2,1},{3,2},{4,3},{5,4},{6,5},{7,6},{8,7},{9,8},{10,9... | collective-permute-start | bytes 884744 | tf_op jit(solution)/shard_map/ppermute | solution.py:219
  232.7 3.3 %collective-permute-done.12 = bf16[384,384]{1,0:T(8,128)(2,1)S(1)} collective-permute-done((bf16[384,384]{1,0:T(8,128)(2,1)S(1)}, bf16[384,384]{1,0:T(8,128)(2,1)S(1)}, u32[]{:S(2)}, u32[]{:S(2)}) %collective-permute-start.12) | collective-permute-done | bytes 294944 | tf_op jit(solution)/shard_map/ppermute | solution.py:217
  236.0 2.1 collective-permute-start.14
  238.2 1.4 fusion.28
  239.6 1.3 fusion.23
  240.9 1.3 fusion.20
  242.3 1.4 fusion.17
  243.7 1.3 fusion.14
  245.3 0.3 convolution_add_fusion.7
  245.7 0.3 fusion.5
  246.0 0.3 fusion.4
  246.4 0.3 fusion.3
  246.7 0.3 fusion.2
  247.8 1.3 fusion.8
  249.4 2.1 convolution_add_fusion.ring_ref
  251.6 7.4 %final.1 = bf16[768,384]{1,0:T(8,128)(2,1)} custom-call(bf16[16,400,384]{2,1,0:T(8,128)(2,1)} %bitcast.30, bf16[6144,384]{1,0:T(8,128)(2,1)} %all-gather.4.cloned.1.call-done.proj_ref, f32[384,384]{1,0:T(8,128)} %convolution_add_fusion.ring_ref), custom_call_target="tpu_custom_call" | custom-call | tf_op jit(solution)/shard_map/final/pallas_call | solution.py:185
  (39 shorter events, 1.9 us)
Async XLA Ops:
  6.5 231.6 %all-gather.4.cloned.1.call-start = ((), (), s32[]{:S(2)}) async-start(), calls=%async_computation.1 | async-start | bytes 4866048 | tf_op jit(solution)/shard_map/all_gather | solution.py:248
  6.5 1.3 copy-start
  7.8 1.3 copy-start.1
  9.1 0.9 copy-start.3
  10.0 83.9 %copy-start.6 = (s32[32,256]{1,0:T(8,128)S(1)}, s32[32,256]{1,0:T(8,128)}, u32[]{:S(2)}) copy-start(s32[32,256]{1,0:T(8,128)} %param.15) | copy-start | bytes 98308
  12.8 103.4 %copy-start.7 = (s32[32,256]{1,0:T(8,128)S(1)}, s32[32,256]{1,0:T(8,128)}, u32[]{:S(2)}) copy-start(s32[32,256]{1,0:T(8,128)} %param.16) | copy-start | bytes 98308
  12.8 104.3 %copy-start.8 = (f32[384]{0:T(512)S(1)}, f32[384]{0:T(512)}, u32[]{:S(2)}) copy-start(f32[384]{0:T(512)} %param.18) | copy-start | bytes 4612
  12.8 115.6 %copy-start.2 = (bf16[768,384]{1,0:T(8,128)(2,1)S(1)}, bf16[768,384]{1,0:T(8,128)(2,1)}, u32[]{:S(2)}) copy-start(bf16[768,384]{1,0:T(8,128)(2,1)} %residual_ref.1) | copy-start | bytes 1769476
  100.2 28.3 %all-to-all-start = ((bf16[32,24,384]{2,1,0:T(8,128)(2,1)}), bf16[32,24,384]{2,1,0:T(8,128)(2,1)S(1)}, u32[]{:S(2)}, u32[]{:S(2)}) async-start(bf16[32,24,384]{2,1,0:T(8,128)(2,1)} %bitcast.31), calls=%async_computation | async-start | bytes 1179648 | tf_op jit(solution)/shard_map/all_to_all | solution.py:268
  116.2 135.4 %all-gather.6.cloned.1.call-start = ((), (), s32[]{:S(2)}) async-start(), calls=%async_computation.2 | async-start | bytes 5222400 | tf_op jit(solution)/shard_map/all_gather | solution.py:276
  130.2 11.9 %collective-permute-start = (bf16[384,384]{1,0:T(8,128)(2,1)S(1)}, bf16[384,384]{1,0:T(8,128)(2,1)S(1)}, u32[]{:S(2)}, u32[]{:S(2)}) collective-permute-start(bf16[384,384]{1,0:T(8,128)(2,1)S(1)} %get-tuple-element.142), channel_id=1, source_target_pairs={{0,1},{1,2},{2,3},{3,4},{4,5},{5,6},{6,7},{7,8},{8,9},{9,10},{10,1... | collective-permute-start | bytes 884744 | tf_op jit(solution)/shard_map/ppermute | solution.py:217
  132.4 14.0 %collective-permute-start.1 = (bf16[384,384]{1,0:T(8,128)(2,1)S(1)}, bf16[384,384]{1,0:T(8,128)(2,1)S(1)}, u32[]{:S(2)}, u32[]{:S(2)}) collective-permute-start(bf16[384,384]{1,0:T(8,128)(2,1)S(1)} %get-tuple-element.142), channel_id=1, source_target_pairs={{0,15},{1,0},{2,1},{3,2},{4,3},{5,4},{6,5},{7,6},{8,7},{9,8},{10,9... | collective-permute-start | bytes 884744 | tf_op jit(solution)/shard_map/ppermute | solution.py:219
  142.1 17.9 %collective-permute-start.2 = (bf16[384,384]{1,0:T(8,128)(2,1)S(1)}, bf16[384,384]{1,0:T(8,128)(2,1)S(1)}, u32[]{:S(2)}, u32[]{:S(2)}) collective-permute-start(bf16[384,384]{1,0:T(8,128)(2,1)S(1)} %collective-permute-done), channel_id=1, source_target_pairs={{0,1},{1,2},{2,3},{3,4},{4,5},{5,6},{6,7},{7,8},{8,9},{9,10},{10,1... | collective-permute-start | bytes 884744 | tf_op jit(solution)/shard_map/ppermute | solution.py:217
  146.4 16.3 %collective-permute-start.3 = (bf16[384,384]{1,0:T(8,128)(2,1)S(1)}, bf16[384,384]{1,0:T(8,128)(2,1)S(1)}, u32[]{:S(2)}, u32[]{:S(2)}) collective-permute-start(bf16[384,384]{1,0:T(8,128)(2,1)S(1)} %collective-permute-done.1), channel_id=1, source_target_pairs={{0,15},{1,0},{2,1},{3,2},{4,3},{5,4},{6,5},{7,6},{8,7},{9,8},{10,9... | collective-permute-start | bytes 884744 | tf_op jit(solution)/shard_map/ppermute | solution.py:219
  160.0 17.9 %collective-permute-start.4 = (bf16[384,384]{1,0:T(8,128)(2,1)S(1)}, bf16[384,384]{1,0:T(8,128)(2,1)S(1)}, u32[]{:S(2)}, u32[]{:S(2)}) collective-permute-start(bf16[384,384]{1,0:T(8,128)(2,1)S(1)} %collective-permute-done.2), channel_id=1, source_target_pairs={{0,1},{1,2},{2,3},{3,4},{4,5},{5,6},{6,7},{7,8},{8,9},{9,10},{10,1... | collective-permute-start | bytes 884744 | tf_op jit(solution)/shard_map/ppermute | solution.py:217
  162.7 17.2 %collective-permute-start.5 = (bf16[384,384]{1,0:T(8,128)(2,1)S(1)}, bf16[384,384]{1,0:T(8,128)(2,1)S(1)}, u32[]{:S(2)}, u32[]{:S(2)}) collective-permute-start(bf16[384,384]{1,0:T(8,128)(2,1)S(1)} %collective-permute-done.3), channel_id=1, source_target_pairs={{0,15},{1,0},{2,1},{3,2},{4,3},{5,4},{6,5},{7,6},{8,7},{9,8},{10,9... | collective-permute-start | bytes 884744 | tf_op jit(solution)/shard_map/ppermute | solution.py:219
  177.9 16.6 %collective-permute-start.6 = (bf16[384,384]{1,0:T(8,128)(2,1)S(1)}, bf16[384,384]{1,0:T(8,128)(2,1)S(1)}, u32[]{:S(2)}, u32[]{:S(2)}) collective-permute-start(bf16[384,384]{1,0:T(8,128)(2,1)S(1)} %collective-permute-done.4), channel_id=1, source_target_pairs={{0,1},{1,2},{2,3},{3,4},{4,5},{5,6},{6,7},{7,8},{8,9},{9,10},{10,1... | collective-permute-start | bytes 884744 | tf_op jit(solution)/shard_map/ppermute | solution.py:217
  179.8 16.6 %collective-permute-start.7 = (bf16[384,384]{1,0:T(8,128)(2,1)S(1)}, bf16[384,384]{1,0:T(8,128)(2,1)S(1)}, u32[]{:S(2)}, u32[]{:S(2)}) collective-permute-start(bf16[384,384]{1,0:T(8,128)(2,1)S(1)} %collective-permute-done.5), channel_id=1, source_target_pairs={{0,15},{1,0},{2,1},{3,2},{4,3},{5,4},{6,5},{7,6},{8,7},{9,8},{10,9... | collective-permute-start | bytes 884744 | tf_op jit(solution)/shard_map/ppermute | solution.py:219
  194.5 16.5 %collective-permute-start.8 = (bf16[384,384]{1,0:T(8,128)(2,1)S(1)}, bf16[384,384]{1,0:T(8,128)(2,1)S(1)}, u32[]{:S(2)}, u32[]{:S(2)}) collective-permute-start(bf16[384,384]{1,0:T(8,128)(2,1)S(1)} %collective-permute-done.6), channel_id=1, source_target_pairs={{0,1},{1,2},{2,3},{3,4},{4,5},{5,6},{6,7},{7,8},{8,9},{9,10},{10,1... | collective-permute-start | bytes 884744 | tf_op jit(solution)/shard_map/ppermute | solution.py:217
  196.5 21.1 %copy-start.5 = (bf16[384,384]{1,0:T(8,128)(2,1)}, bf16[384,384]{1,0:T(8,128)(2,1)S(1)}, u32[]{:S(2)}) copy-start(bf16[384,384]{1,0:T(8,128)(2,1)S(1)} %collective-permute-done.7) | copy-start | bytes 884740
  196.5 16.5 %collective-permute-start.9 = (bf16[384,384]{1,0:T(8,128)(2,1)S(1)}, bf16[384,384]{1,0:T(8,128)(2,1)}, u32[]{:S(2)}, u32[]{:S(2)}) collective-permute-start(bf16[384,384]{1,0:T(8,128)(2,1)S(1)} %collective-permute-done.7), channel_id=1, source_target_pairs={{0,15},{1,0},{2,1},{3,2},{4,3},{5,4},{6,5},{7,6},{8,7},{9,8},{10,9... | collective-permute-start | bytes 884744 | tf_op jit(solution)/shard_map/ppermute | solution.py:219
  211.0 15.1 %collective-permute-start.10 = (bf16[384,384]{1,0:T(8,128)(2,1)S(1)}, bf16[384,384]{1,0:T(8,128)(2,1)S(1)}, u32[]{:S(2)}, u32[]{:S(2)}) collective-permute-start(bf16[384,384]{1,0:T(8,128)(2,1)S(1)} %collective-permute-done.8), channel_id=1, source_target_pairs={{0,1},{1,2},{2,3},{3,4},{4,5},{5,6},{6,7},{7,8},{8,9},{9,10},{10,1... | collective-permute-start | bytes 884744 | tf_op jit(solution)/shard_map/ppermute | solution.py:217
  213.0 15.2 %collective-permute-start.11 = (bf16[384,384]{1,0:T(8,128)(2,1)}, bf16[384,384]{1,0:T(8,128)(2,1)S(1)}, u32[]{:S(2)}, u32[]{:S(2)}) collective-permute-start(bf16[384,384]{1,0:T(8,128)(2,1)} %collective-permute-done.9), channel_id=1, source_target_pairs={{0,15},{1,0},{2,1},{3,2},{4,3},{5,4},{6,5},{7,6},{8,7},{9,8},{10,9... | collective-permute-start | bytes 884744 | tf_op jit(solution)/shard_map/ppermute | solution.py:219
  226.1 9.9 %collective-permute-start.12 = (bf16[384,384]{1,0:T(8,128)(2,1)S(1)}, bf16[384,384]{1,0:T(8,128)(2,1)S(1)}, u32[]{:S(2)}, u32[]{:S(2)}) collective-permute-start(bf16[384,384]{1,0:T(8,128)(2,1)S(1)} %collective-permute-done.10), channel_id=1, source_target_pairs={{0,1},{1,2},{2,3},{3,4},{4,5},{5,6},{6,7},{7,8},{8,9},{9,10},{10,1... | collective-permute-start | bytes 884744 | tf_op jit(solution)/shard_map/ppermute | solution.py:217
  228.1 19.6 %collective-permute-start.13 = (bf16[384,384]{1,0:T(8,128)(2,1)S(1)}, bf16[384,384]{1,0:T(8,128)(2,1)}, u32[]{:S(2)}, u32[]{:S(2)}) collective-permute-start(bf16[384,384]{1,0:T(8,128)(2,1)S(1)} %collective-permute-done.11), channel_id=1, source_target_pairs={{0,15},{1,0},{2,1},{3,2},{4,3},{5,4},{6,5},{7,6},{8,7},{9,8},{10,9... | collective-permute-start | bytes 884744 | tf_op jit(solution)/shard_map/ppermute | solution.py:219
  236.0 13.4 %collective-permute-start.14 = (bf16[384,384]{1,0:T(8,128)(2,1)S(1)}, bf16[384,384]{1,0:T(8,128)(2,1)}, u32[]{:S(2)}, u32[]{:S(2)}) collective-permute-start(bf16[384,384]{1,0:T(8,128)(2,1)S(1)} %collective-permute-done.12), channel_id=1, source_target_pairs={{0,1},{1,2},{2,3},{3,4},{4,5},{5,6},{6,7},{7,8},{8,9},{9,10},{10,1... | collective-permute-start | bytes 884744 | tf_op jit(solution)/shard_map/ppermute | solution.py:217
  238.1 5.5 %copy-start.4 = (bf16[6144,384]{1,0:T(8,128)(2,1)S(1)}, bf16[6144,384]{1,0:T(8,128)(2,1)}, u32[]{:S(2)}) copy-start(bf16[6144,384]{1,0:T(8,128)(2,1)} %all-gather.4.cloned.1.call-done.proj_ref) | copy-start | bytes 14155780
Sparse Core Ops, SparseCore 0:
  12.9 67.9 all-gather.3
  130.3 92.5 all-gather.5

commit v4 on v1

v4 whole, which is shorter than its diff:
```python
import jax
import jax.numpy as jnp
from jax import lax
from jax.experimental import pallas as pl
from jax.experimental.pallas import tpu as pltpu
from jax.sharding import PartitionSpec as P

D = 6144
PART_TYPE = jnp.bfloat16
VMEM_BYTES = 63 * 1024 * 1024
SPARES = 40
CHUNKS = 2
PART_ROWS = 16


def gate_up_kernel(rows_hbm, gate_hbm, up_hbm, *refs):
    spare_ref, rows_ref, mats_ref, parts_ref, in_sems, out_sems, spare_sems = refs[-7:]
    n_parts = len(refs) - 7 - SPARES
    out_refs, spare_hbms = refs[:n_parts], refs[n_parts:-7]
    capacity, ff = rows_hbm.shape[0], gate_hbm.shape[1]
    cols = ff // CHUNKS
    spare_ref[...] = jnp.zeros_like(spare_ref)
    get_rows = pltpu.make_async_copy(rows_hbm, rows_ref, in_sems.at[2 * CHUNKS])
    get_rows.start()
    gets = []
    for half, mat in enumerate((gate_hbm, up_hbm)):
        for c in range(CHUNKS):
            span = slice(c * cols, (c + 1) * cols)
            gets.append(
                pltpu.make_async_copy(
                    mat.at[:, span], mats_ref.at[half, :, span], in_sems.at[half * CHUNKS + c]
                )
            )
            gets[-1].start()
    spare_puts = [
        pltpu.make_async_copy(spare_ref, spare_hbm, spare_sems.at[n]) for n, spare_hbm in enumerate(spare_hbms)
    ]
    for put in spare_puts:
        put.start()
    get_rows.wait()
    puts = []
    for half in range(2):
        for c in range(CHUNKS):
            span = slice(c * cols, (c + 1) * cols)
            gets[half * CHUNKS + c].wait()
            parts_ref[half * capacity : (half + 1) * capacity, span] = jnp.dot(
                rows_ref[...], mats_ref[half, :, span], preferred_element_type=jnp.float32
            ).astype(parts_ref.dtype)
        for n in range(half * n_parts // 2, (half + 1) * n_parts // 2):
            puts.append(
                pltpu.make_async_copy(
                    parts_ref.at[n * PART_ROWS : (n + 1) * PART_ROWS], out_refs[n], out_sems.at[n]
                )
            )
            puts[-1].start()
    for put in spare_puts + puts:
        put.wait()


def gate_up(rows, gate_mat, up_mat):
    capacity, depth = rows.shape
    ff = gate_mat.shape[1]
    n_parts = 2 * capacity // PART_ROWS
    return pl.pallas_call(
        gate_up_kernel,
        out_shape=[pltpu.HBM((PART_ROWS, ff), PART_TYPE)] * n_parts
        + [pltpu.HBM((16, 128), PART_TYPE)] * SPARES,
        in_specs=[pl.BlockSpec(memory_space=pltpu.HBM)] * 3,
        out_specs=[pl.BlockSpec(memory_space=pltpu.HBM)] * (n_parts + SPARES),
        scratch_shapes=[
            pltpu.VMEM((16, 128), PART_TYPE),
            pltpu.VMEM((capacity, depth), rows.dtype),
            pltpu.VMEM((2, depth, ff), gate_mat.dtype),
            pltpu.VMEM((2 * capacity, ff), PART_TYPE),
            pltpu.SemaphoreType.DMA((2 * CHUNKS + 1,)),
            pltpu.SemaphoreType.DMA((n_parts,)),
            pltpu.SemaphoreType.DMA((SPARES,)),
        ],
        compiler_params=pltpu.CompilerParams(vmem_limit_bytes=VMEM_BYTES),
        name="gate_up",
    )(rows, gate_mat, up_mat)


def tail_kernel(down_hbm, combine_ref, slot_ref, *refs):
    out_ref, sums_ref, down_ref, hidden_ref, sems = refs[-5:]
    capacity = hidden_ref.shape[0]
    half = capacity // PART_ROWS
    sum_hbms = refs[: 2 * half]
    gets = []
    for c in range(half):
        for n in (c, half + c):
            gets.append(
                pltpu.make_async_copy(
                    sum_hbms[n], sums_ref.at[n * PART_ROWS : (n + 1) * PART_ROWS], sems.at[n]
                )
            )
            gets[-1].start()
    get_down = pltpu.make_async_copy(down_hbm, down_ref, sems.at[2 * half])
    get_down.start()
    for c in range(half):
        gets[2 * c].wait()
        gets[2 * c + 1].wait()
        start = c * PART_ROWS
        gate = sums_ref[start : start + PART_ROWS].astype(jnp.float32)
        up = sums_ref[capacity + start : capacity + start + PART_ROWS].astype(jnp.float32)
        hidden_ref[start : start + PART_ROWS] = (gate / (1.0 + jnp.exp(-gate)) * up).astype(jnp.bfloat16)
    get_down.wait()
    expert_out = jnp.dot(hidden_ref[...], down_ref[...], preferred_element_type=jnp.float32)
    combine = jnp.broadcast_to(combine_ref[...], (128, capacity)).T[:, 0:1]
    weighted = (combine * expert_out).astype(jnp.bfloat16)
    slots = out_ref.shape[0]
    slot_ids = lax.broadcasted_iota(jnp.int32, (slots, capacity), 0)
    table = jnp.where(slot_ref[...] == slot_ids, 1.0, 0.0).astype(jnp.bfloat16)
    out_ref[...] = jnp.dot(table, weighted, preferred_element_type=jnp.float32).astype(jnp.bfloat16)


def expert_tail(sums, down_mat, combine, slot, slots):
    ff, width = down_mat.shape
    capacity = combine.shape[0]
    return pl.pallas_call(
        tail_kernel,
        out_shape=jax.ShapeDtypeStruct((slots, width), jnp.bfloat16),
        in_specs=[pl.BlockSpec(memory_space=pltpu.HBM)]
        + [pl.BlockSpec(memory_space=pltpu.VMEM)] * 2
        + [pl.BlockSpec(memory_space=pltpu.HBM)] * len(sums),
        out_specs=pl.BlockSpec(memory_space=pltpu.VMEM),
        scratch_shapes=[
            pltpu.VMEM((2 * capacity, ff), PART_TYPE),
            pltpu.VMEM((ff, width), down_mat.dtype),
            pltpu.VMEM((capacity, ff), jnp.bfloat16),
            pltpu.SemaphoreType.DMA((2 * capacity // PART_ROWS + 1,)),
        ],
        compiler_params=pltpu.CompilerParams(vmem_limit_bytes=VMEM_BYTES),
        name="expert_tail",
    )(down_mat, combine[None, :], slot[None, :], *sums)


def mix_kernel(residual_ref, received_ref, row_ref, gain_ref, out_ref, squares_ref):
    tokens, width = residual_ref.shape
    slots = received_ref.shape[0]
    token_ids = lax.broadcasted_iota(jnp.int32, (tokens, slots), 0)
    table = jnp.where(row_ref[...] == token_ids, 1.0, 0.0).astype(jnp.bfloat16)
    moe = jnp.dot(table, received_ref[...], preferred_element_type=jnp.float32)
    mixed = residual_ref[...].astype(jnp.float32) + moe
    out_ref[...] = (mixed * gain_ref[...]).astype(jnp.bfloat16)
    squares = jnp.sum(mixed * mixed, axis=1, keepdims=True)
    squares_ref[...] = jnp.broadcast_to(squares, (tokens, 128)).T[0:1]


def mix(residual, received, row_of, gain):
    tokens, width = residual.shape
    return pl.pallas_call(
        mix_kernel,
        out_shape=[
            jax.ShapeDtypeStruct((tokens, width), jnp.bfloat16),
            jax.ShapeDtypeStruct((1, tokens), jnp.float32),
        ],
        in_specs=[pl.BlockSpec(memory_space=pltpu.VMEM)] * 4,
        out_specs=[pl.BlockSpec(memory_space=pltpu.VMEM)] * 2,
        compiler_params=pltpu.CompilerParams(vmem_limit_bytes=40 * 1024 * 1024),
        name="mix",
    )(residual, received, row_of[None, :], gain[None, :])


def final_kernel(gathered_ref, proj_ref, squares_ref, out_ref, acc_ref):
    step = pl.program_id(0)
    per_step, tokens, width = gathered_ref.shape
    pair = 2 * width
    total = None
    for z in range(0, per_step, 2):
        block = jnp.concatenate([gathered_ref[z], gathered_ref[z + 1]], axis=1)
        part = jnp.dot(
            block, proj_ref[z * width : z * width + pair], preferred_element_type=jnp.float32
        )
        total = part if total is None else total + part

    @pl.when(step == 0)
    def _():
        acc_ref[...] = total

    @pl.when(step > 0)
    def _():
        acc_ref[...] += total

    @pl.when(step == pl.num_programs(0) - 1)
    def _():
        inverse = lax.rsqrt(squares_ref[...] / D + 1e-05)
        column = jnp.broadcast_to(inverse, (128, tokens)).T[:, 0:1]
        out_ref[...] = (acc_ref[...] * column).astype(jnp.bfloat16)


def final(gathered, full_projection, square_total):
    n, tokens, width = gathered.shape
    columns = full_projection.shape[1]
    per_step = 2
    return pl.pallas_call(
        final_kernel,
        grid=(n // per_step,),
        out_shape=jax.ShapeDtypeStruct((tokens, columns), jnp.bfloat16),
        in_specs=[
            pl.BlockSpec((per_step, tokens, width), lambda i: (i, 0, 0)),
            pl.BlockSpec((per_step * width, columns), lambda i: (i, 0)),
            pl.BlockSpec((1, tokens), lambda i: (0, 0)),
        ],
        out_specs=pl.BlockSpec((tokens, columns), lambda i: (0, 0)),
        scratch_shapes=[pltpu.VMEM((tokens, columns), jnp.float32)],
        compiler_params=pltpu.CompilerParams(vmem_limit_bytes=VMEM_BYTES),
        name="final",
    )(gathered, full_projection, square_total)


def shards(
    picked_rows,
    w_gate,
    w_up,
    w_down,
    combine_gate,
    pick_owner,
    pick_row,
    residual_in,
    norm_gain,
    projection,
):
    my_rows = picked_rows[0]
    capacity = my_rows.shape[0]
    n_groups = pick_owner.shape[0]
    slot_most = max(3 * capacity // n_groups, 2)
    width = residual_in.shape[1]
    my_index = lax.axis_index("expert")

    parts = gate_up(my_rows, w_gate[0], w_up[0])
    full_projection = lax.all_gather(projection, "expert", axis=0, tiled=True)

    my_owner = lax.dynamic_index_in_dim(pick_owner, my_index, 0, keepdims=False)
    pick_ids = jnp.arange(capacity, dtype=jnp.int32)
    same_earlier = (my_owner[:, None] == my_owner[None, :]) & (pick_ids[:, None] < pick_ids[None, :])
    my_position = jnp.sum(same_earlier.astype(jnp.int32), axis=0)
    my_slot = my_owner * slot_most + my_position

    mine = pick_owner == my_index
    before = (pick_ids[:, None] < pick_ids[None, :]).astype(jnp.bfloat16)
    position = jnp.dot(
        mine.astype(jnp.bfloat16), before, preferred_element_type=jnp.float32
    ).astype(jnp.int32)
    slot_range = jnp.arange(slot_most, dtype=jnp.int32)
    matches = mine[:, None, :] & (position[:, None, :] == slot_range[None, :, None])
    row_of = jnp.sum(jnp.where(matches, pick_row[:, None, :] + 1, 0), axis=2) - 1

    sums = lax.psum(tuple(parts), "tensor")
    outgoing = expert_tail(sums, w_down[0], combine_gate[0], my_slot, n_groups * slot_most)
    outgoing = outgoing.reshape(n_groups, slot_most, width)
    received = lax.all_to_all(outgoing, "expert", split_axis=0, concat_axis=0, tiled=True)
    gained, squares = mix(
        residual_in, received.reshape(n_groups * slot_most, width), row_of.reshape(-1), norm_gain
    )
    full_gained = lax.all_gather(gained, "tensor")
    square_total = lax.psum(squares, "tensor")
    return final(full_gained, full_projection, square_total)


def solution(mesh):
    return jax.shard_map(
        shards,
        mesh=mesh,
        in_specs=(
            P("expert", None, "tensor"),
            P("expert", "tensor", None),
            P("expert", "tensor", None),
            P("expert", None, "tensor"),
            P("expert", None),
            P(),
            P(),
            P("expert", "tensor"),
            P("tensor"),
            P("expert", "tensor"),
        ),
        out_specs=P("expert", "tensor"),
        check_vma=False,
    )
```

time: 333 us -> 248 us (0.74)
  local copies, waits for them, and re-layouts: 82.7 us -> 0.12 us
  Pallas kernels: 2.74 us -> 22.5 us
  matrix products: 11.5 us -> 0.15 us
  blocking collectives: 103 us -> 94.4 us
    unnamed x265 -> x8, local copies, waits for them, and re-layouts: 81.1 us -> 0.03 us
    pallas_call x1 -> x3, Pallas kernels: 0.97 us -> 17.9 us  [the longest x1 11.6 us: final(): pl.pallas_call(final_kernel, grid=(n // per_step,), out_shape=jax.ShapeDt...]
    dot_general x2 -> x0, matrix products: 11.3 us -> none  [the longest x1 9.72 us: shards(): jnp.dot(full_gained, full_projection, preferred_element_type=jnp.float32)]
    psum x1, blocking collectives: 80.2 us -> 71.6 us  [shards(): sums = lax.psum(tuple(parts), 'tensor')]
  transfers between devices with their start and end apart: 3 -> 3, of which waited for: 2 -> 2; matrix products, arithmetic and copies ran while one was open for 2% -> 1% of each run, Pallas kernels for 1% -> 4%
where the time goes in v4:
time: 248 us
  waiting for transfers between devices  98.2 us (40%)
  blocking collectives  94.4 us (38%)
  Pallas kernels  22.5 us (9%)
  starting transfers between devices  17.5 us (7%)
  between operations  13.5 us (5%)
    all_gather x1, waiting for transfers between devices, shards(): full_gained = lax.all_gather(gained, 'tensor')  86.2 us
    psum x1, blocking collectives, shards(): sums = lax.psum(tuple(parts), 'tensor')  71.6 us
    psum x1, blocking collectives, shards(): square_total = lax.psum(squares, 'tensor')  22.8 us
    all_to_all x1, starting transfers between devices, shards(): lax.all_to_all(outgoing, 'expert', split_axis=0, concat_axis=0, tiled=True)  17.5 us
    pallas_call x1, Pallas kernels, final(): pl.pallas_call(final_kernel, grid=(n // per_step,), out_shape=jax.ShapeDt...  11.6 us
    all_to_all x1, waiting for transfers between devices, shards(): lax.all_to_all(outgoing, 'expert', split_axis=0, concat_axis=0, tiled=True)  11.3 us
  transfers between devices with their start and end apart: 3, of which 2 were waited for; matrix products, arithmetic and copies ran while one was open for 1% of the time, Pallas kernels for 4%

profile of v4, /device:TPU:1, one launch (start us, length us, event | category | flops | bytes accessed | tf_op | source)
XLA Modules:
  0.0 247.7 jit_solution(3132717956267631663)
XLA Ops:
  6.5 0.0 all-gather.4.cloned.1.call-start
  6.5 0.7 all-gather.4.cloned.1.call-update
  7.3 4.7 %gate_up.1 = (bf16[16,1536]{1,0:T(8,128)(2,1)}, bf16[16,1536]{1,0:T(8,128)(2,1)}, bf16[16,1536]{1,0:T(8,128)(2,1)}, bf16[16,1536]{1,0:T(8,128)(2,1)}, bf16[16,15...) custom-call(bf16[256,384]{1,0:T(8,128)(2,1)} %bitcast.16, ...), custom_call_target="tpu_custom_call" | custom-call | tf_op jit(solution)/shard_map/gate_up/pallas_call | solution.py:64
  11.9 0.0 copy-start.1
  11.9 71.6 %all-reduce.2 = (bf16[16,1536]{1,0:T(8,128)(2,1)}, bf16[16,1536]{1,0:T(8,128)(2,1)}, bf16[16,1536]{1,0:T(8,128)(2,1)}, bf16[16,1536]{1,0:T(8,128)(2,1)}, bf16[16...) all-reduce(bf16[16,1536]{1,0:T(8,128)(2,1)} %get-tuple-element.79, ...), channel_id=1, replica_groups=mesh['expert'=32,'tensor'=16] {'tensor'}, use_global_device_ids=true, to_apply=%region_1.2 | all-reduce | flops 868352 | bytes 3473408 | tf_op jit(solution)/shard_map/psum | solution.py:249
  83.6 0.0 copy-done.1
  83.6 0.1 convert_reduce_fusion
  83.7 0.6 multiply_add_fusion.slot_ref
  84.3 4.6 %expert_tail.1 = bf16[768,384]{1,0:T(8,128)(2,1)} custom-call(bf16[1536,384]{1,0:T(8,128)(2,1)} %bitcast.13, f32[1,256]{1,0:T(1,128)} %combine_ref.1, s32[1,256]{1,0:T(1,128)} %multiply_add_fusion.slot_ref, bf16[16,1536]{1,0:T(8,128)(2,1)} %get-tuple-element.153.refs_0_, bf16[16,1536]{1,0:T(8,128)(2,1)} %get-tuple-element.154.refs_1_, ...), custom_call_target="tpu_custom_call" | custom-call | tf_op jit(solution)/shard_map/expert_tail/pallas_call | solution.py:120
  88.9 0.0 copy-start.2
  88.9 0.0 copy-start.3
  88.9 0.0 copy-start
  88.9 17.5 %all-to-all-start = ((bf16[32,24,384]{2,1,0:T(8,128)(2,1)}), bf16[32,24,384]{2,1,0:T(8,128)(2,1)S(1)}, u32[]{:S(2)}, u32[]{:S(2)}) async-start(bf16[32,24,384]{2,1,0:T(8,128)(2,1)} %bitcast.12), calls=%async_computation | async-start | bytes 1179648 | tf_op jit(solution)/shard_map/all_to_all | solution.py:252
  106.4 0.0 all-gather.6.cloned.1.call-start
  106.5 0.0 copy-done.2
  106.5 0.2 convolution_convert_fusion
  106.6 0.6 select_reduce_fusion
  107.3 0.1 sub.7.row_ref
  107.4 0.0 copy-done.3
  107.4 11.3 %all-to-all-done = bf16[32,24,384]{2,1,0:T(8,128)(2,1)S(1)} async-done(((bf16[32,24,384]{2,1,0:T(8,128)(2,1)}), bf16[32,24,384]{2,1,0:T(8,128)(2,1)S(1)}, u32[]{:S(2)}, u32[]{:S(2)}) %all-to-all-start) | async-done | bytes 589856 | tf_op jit(solution)/shard_map/all_to_all | solution.py:252
  118.7 0.0 copy-done
  118.7 1.6 mix.1
  120.3 0.0 all-gather.6.cloned.1.call-update
  120.3 22.8 %psum.583.squares_ref = f32[1,768]{1,0:T(1,128)} all-reduce(f32[1,768]{1,0:T(1,128)S(1)} %get-tuple-element.152), channel_id=1, replica_groups=mesh['expert'=32,'tensor'=16] {'tensor'}, use_global_device_ids=true, to_apply=%region_74.75 | all-reduce | flops 768 | bytes 6144 | tf_op jit(solution)/shard_map/psum | solution.py:257
  143.1 0.0 all-gather.4.cloned.1.call-done.proj_ref
  143.1 86.2 %all-gather.6.cloned.1.call-done = bf16[12288,384]{1,0:T(8,128)(2,1)} async-done(((bf16[768,384]{1,0:T(8,128)(2,1)}), bf16[12288,384]{1,0:T(8,128)(2,1)}) %all-gather.6.cloned.1.call-update) | async-done | bytes 9437200 | tf_op jit(solution)/shard_map/all_gather | solution.py:256
  229.3 11.6 %final.1 = bf16[768,384]{1,0:T(8,128)(2,1)} custom-call(bf16[16,768,384]{2,1,0:T(8,128)(2,1)} %bitcast.11, bf16[6144,384]{1,0:T(8,128)(2,1)} %all-gather.4.cloned.1.call-done.proj_ref, f32[1,768]{1,0:T(1,128)} %psum.583.squares_ref), custom_call_target="tpu_custom_call" | custom-call | tf_op jit(solution)/shard_map/final/pallas_call | solution.py:196
  (5 shorter events, 0.0 us)
Async XLA Ops:
  6.5 136.6 %all-gather.4.cloned.1.call-start = ((), (), s32[]{:S(2)}) async-start(), calls=%async_computation.1 | async-start | bytes 4866048 | tf_op jit(solution)/shard_map/all_gather | solution.py:232
  11.9 71.6 %copy-start.1 = (s32[32,256]{1,0:T(8,128)S(1)}, s32[32,256]{1,0:T(8,128)}, u32[]{:S(2)}) copy-start(s32[32,256]{1,0:T(8,128)} %param.15) | copy-start | bytes 98308
  88.9 17.6 %copy-start.2 = (s32[32,256]{1,0:T(8,128)S(1)}, s32[32,256]{1,0:T(8,128)}, u32[]{:S(2)}) copy-start(s32[32,256]{1,0:T(8,128)} %param.16) | copy-start | bytes 98308
  88.9 18.5 %copy-start.3 = (f32[384]{0:T(512)S(1)}, f32[384]{0:T(512)}, u32[]{:S(2)}) copy-start(f32[384]{0:T(512)} %param.18) | copy-start | bytes 4612
  88.9 29.8 %copy-start = (bf16[768,384]{1,0:T(8,128)(2,1)S(1)}, bf16[768,384]{1,0:T(8,128)(2,1)}, u32[]{:S(2)}) copy-start(bf16[768,384]{1,0:T(8,128)(2,1)} %residual_ref.1) | copy-start | bytes 1769476
  88.9 29.7 %all-to-all-start = ((bf16[32,24,384]{2,1,0:T(8,128)(2,1)}), bf16[32,24,384]{2,1,0:T(8,128)(2,1)S(1)}, u32[]{:S(2)}, u32[]{:S(2)}) async-start(bf16[32,24,384]{2,1,0:T(8,128)(2,1)} %bitcast.12), calls=%async_computation | async-start | bytes 1179648 | tf_op jit(solution)/shard_map/all_to_all | solution.py:252
  106.4 122.9 %all-gather.6.cloned.1.call-start = ((), (), s32[]{:S(2)}) async-start(), calls=%async_computation.2 | async-start | bytes 10027008 | tf_op jit(solution)/shard_map/all_gather | solution.py:256
Sparse Core Ops, SparseCore 0:
  10.5 67.8 all-gather.3
  120.5 108.8 all-gather.5

commit v5 on v4

--- a/solution.py
+++ b/solution.py
@@ -8,8 +8,8 @@
 D = 6144
 PART_TYPE = jnp.bfloat16
 VMEM_BYTES = 63 * 1024 * 1024
-SPARES = 40
-CHUNKS = 2
+SPARES = 33
+CHUNKS = 1
 PART_ROWS = 16
 
 
@@ -35,8 +35,6 @@
     spare_puts = [
         pltpu.make_async_copy(spare_ref, spare_hbm, spare_sems.at[n]) for n, spare_hbm in enumerate(spare_hbms)
     ]
-    for put in spare_puts:
-        put.start()
     get_rows.wait()
     puts = []
     for half in range(2):
@@ -53,6 +51,8 @@
                 )
             )
             puts[-1].start()
+    for put in spare_puts:
+        put.start()
     for put in spare_puts + puts:
         put.wait()
 
@@ -165,14 +165,8 @@
 def final_kernel(gathered_ref, proj_ref, squares_ref, out_ref, acc_ref):
     step = pl.program_id(0)
     per_step, tokens, width = gathered_ref.shape
-    pair = 2 * width
-    total = None
-    for z in range(0, per_step, 2):
-        block = jnp.concatenate([gathered_ref[z], gathered_ref[z + 1]], axis=1)
-        part = jnp.dot(
-            block, proj_ref[z * width : z * width + pair], preferred_element_type=jnp.float32
-        )
-        total = part if total is None else total + part
+    block = jnp.concatenate([gathered_ref[z] for z in range(per_step)], axis=1)
+    total = jnp.dot(block, proj_ref[...], preferred_element_type=jnp.float32)
 
     @pl.when(step == 0)
     def _():
@@ -192,7 +186,7 @@
 def final(gathered, full_projection, square_total):
     n, tokens, width = gathered.shape
     columns = full_projection.shape[1]
-    per_step = 2
+    per_step = 8
     return pl.pallas_call(
         final_kernel,
         grid=(n // per_step,),
@@ -229,7 +223,6 @@
     my_index = lax.axis_index("expert")
 
     parts = gate_up(my_rows, w_gate[0], w_up[0])
-    full_projection = lax.all_gather(projection, "expert", axis=0, tiled=True)
 
     my_owner = lax.dynamic_index_in_dim(pick_owner, my_index, 0, keepdims=False)
     pick_ids = jnp.arange(capacity, dtype=jnp.int32)
@@ -255,6 +248,10 @@
     )
     full_gained = lax.all_gather(gained, "tensor")
     square_total = lax.psum(squares, "tensor")
+    square_total, projection = lax.optimization_barrier((square_total, projection))
+    copies = jnp.broadcast_to(projection[None], (n_groups, *projection.shape))
+    full_projection = lax.all_to_all(copies, "expert", split_axis=0, concat_axis=0, tiled=True)
+    full_projection = full_projection.reshape(n_groups * projection.shape[0], width)
     return final(full_gained, full_projection, square_total)
 
 

time: 248 us -> 246 us (level)
  waiting for transfers between devices: 98.2 us -> 31.2 us
  blocking collectives: 94.4 us -> 156 us
  starting transfers between devices: 17.5 us -> 20.9 us
  Pallas kernels: 22.5 us -> 19.9 us
    all_gather x1, waiting for transfers between devices: 86.2 us -> 19.9 us  [shards(): full_gained = lax.all_gather(gained, 'tensor')]
    all_to_all x0 -> x1, blocking collectives: none -> 65.2 us  [shards(): lax.all_to_all(copies, 'expert', split_axis=0, concat_axis=0, tiled=True)]
    psum x1, blocking collectives: 71.6 us -> 68 us  [shards(): sums = lax.psum(tuple(parts), 'tensor')]
    all_to_all x1, starting transfers between devices: 17.5 us -> 20.9 us  [shards(): lax.all_to_all(outgoing, 'expert', split_axis=0, concat_axis=0, tiled=True)]
  transfers between devices with their start and end apart: 3 -> 2, of which waited for: 2 -> 2; matrix products, arithmetic and copies ran while one was open for 1% -> 1% of each run, Pallas kernels for 4% -> 0%
where the time goes in v5:
time: 246 us; the launch traced here: 245 us
  blocking collectives  156 us (63%)
  waiting for transfers between devices  31.2 us (13%)
  starting transfers between devices  20.9 us (8%)
  Pallas kernels  19.9 us (8%)
  between operations  13.5 us (5%)
    psum x1, blocking collectives, shards(): sums = lax.psum(tuple(parts), 'tensor')  68 us
    all_to_all x1, blocking collectives, shards(): lax.all_to_all(copies, 'expert', split_axis=0, concat_axis=0, tiled=True)  65.2 us
    psum x1, blocking collectives, shards(): square_total = lax.psum(squares, 'tensor')  22.7 us
    all_to_all x1, starting transfers between devices, shards(): lax.all_to_all(outgoing, 'expert', split_axis=0, concat_axis=0, tiled=True)  20.9 us
    all_gather x1, waiting for transfers between devices, shards(): full_gained = lax.all_gather(gained, 'tensor')  19.9 us
    all_to_all x1, waiting for transfers between devices, shards(): lax.all_to_all(outgoing, 'expert', split_axis=0, concat_axis=0, tiled=True)  11.3 us
    pallas_call x1, Pallas kernels, final(): pl.pallas_call(final_kernel, grid=(n // per_step,), out_shape=jax.ShapeDt...  9.63 us
  transfers between devices with their start and end apart: 2, of which 2 were waited for; matrix products, arithmetic and copies ran while one was open for 1% of the time, Pallas kernels for 0%

profile of v5, /device:TPU:1, one launch (start us, length us, event | category | flops | bytes accessed | tf_op | source)
XLA Modules:
  0.0 245.1 jit_solution(7497412610448272779)
XLA Ops:
  6.5 0.0 copy-start.2
  6.5 0.0 copy-start.3
  6.5 0.8 constant_dynamic-slice_fusion
  7.3 0.1 convert_reduce_fusion
  7.4 1.2 multiply_add_fusion.slot_ref
  8.7 0.0 copy-start.4
  8.7 0.0 copy-start
  8.7 4.0 %gate_up.1 = (bf16[16,1536]{1,0:T(8,128)(2,1)}, bf16[16,1536]{1,0:T(8,128)(2,1)}, bf16[16,1536]{1,0:T(8,128)(2,1)}, bf16[16,1536]{1,0:T(8,128)(2,1)}, bf16[16,15...) custom-call(bf16[256,384]{1,0:T(8,128)(2,1)} %bitcast.18, ...), custom_call_target="tpu_custom_call" | custom-call | tf_op jit(solution)/shard_map/gate_up/pallas_call | solution.py:64
  12.7 0.0 copy-start.1
  12.7 68.0 %all-reduce.2 = (bf16[16,1536]{1,0:T(8,128)(2,1)}, bf16[16,1536]{1,0:T(8,128)(2,1)}, bf16[16,1536]{1,0:T(8,128)(2,1)}, bf16[16,1536]{1,0:T(8,128)(2,1)}, bf16[16...) all-reduce(bf16[16,1536]{1,0:T(8,128)(2,1)} %get-tuple-element.74, ...), channel_id=1, replica_groups=mesh['expert'=32,'tensor'=16] {'tensor'}, use_global_device_ids=true, to_apply=%region_1.2 | all-reduce | flops 854016 | bytes 3416064 | tf_op jit(solution)/shard_map/psum | solution.py:242
  80.8 4.6 %expert_tail.1 = bf16[768,384]{1,0:T(8,128)(2,1)} custom-call(bf16[1536,384]{1,0:T(8,128)(2,1)} %bitcast.17, f32[1,256]{1,0:T(1,128)} %combine_ref.1, s32[1,256]{1,0:T(1,128)} %multiply_add_fusion.slot_ref, bf16[16,1536]{1,0:T(8,128)(2,1)} %get-tuple-element.143.refs_0_, bf16[16,1536]{1,0:T(8,128)(2,1)} %get-tuple-element.144.refs_1_, ...), custom_call_target="tpu_custom_call" | custom-call | tf_op jit(solution)/shard_map/expert_tail/pallas_call | solution.py:120
  85.3 20.9 %all-to-all-start = ((bf16[32,24,384]{2,1,0:T(8,128)(2,1)}), bf16[32,24,384]{2,1,0:T(8,128)(2,1)S(1)}, u32[]{:S(2)}, u32[]{:S(2)}) async-start(bf16[32,24,384]{2,1,0:T(8,128)(2,1)} %bitcast.14), calls=%async_computation | async-start | bytes 1179648 | tf_op jit(solution)/shard_map/all_to_all | solution.py:245
  106.2 0.0 all-gather.3.cloned.1.call-start
  106.3 0.0 copy-done.2
  106.3 0.0 copy-done.3
  106.3 0.2 convolution_convert_fusion
  106.5 0.6 select_reduce_fusion
  107.1 0.1 sub.7.row_ref
  107.2 0.0 copy-done.4
  107.2 11.3 %all-to-all-done = bf16[32,24,384]{2,1,0:T(8,128)(2,1)S(1)} async-done(((bf16[32,24,384]{2,1,0:T(8,128)(2,1)}), bf16[32,24,384]{2,1,0:T(8,128)(2,1)S(1)}, u32[]{:S(2)}, u32[]{:S(2)}) %all-to-all-start) | async-done | bytes 589856 | tf_op jit(solution)/shard_map/all_to_all | solution.py:245
  118.5 0.0 copy-done
  118.5 1.6 mix.1
  120.1 0.0 all-gather.3.cloned.1.call-update
  120.1 22.7 %psum.527.squares_ref = f32[1,768]{1,0:T(1,128)} all-reduce(f32[1,768]{1,0:T(1,128)S(1)} %get-tuple-element.140), channel_id=1, replica_groups=mesh['expert'=32,'tensor'=16] {'tensor'}, use_global_device_ids=true, to_apply=%region_67.68 | all-reduce | flops 768 | bytes 6144 | tf_op jit(solution)/shard_map/psum | solution.py:250
  142.9 0.0 copy-done.1
  142.9 0.7 broadcast_in_dim.19
  143.6 65.2 %all_to_all.10 = bf16[32,192,384]{2,1,0:T(8,128)(2,1)} all-to-all(bf16[32,192,384]{2,1,0:T(8,128)(2,1)S(1)} %broadcast_in_dim.19), channel_id=1, replica_groups=mesh['expert'=32,'tensor'=16] {'expert'}, dimensions={0} | all-to-all | bytes 9437184 | tf_op jit(solution)/shard_map/all_to_all | solution.py:253
  208.8 19.9 %all-gather.3.cloned.1.call-done = bf16[12288,384]{1,0:T(8,128)(2,1)} async-done(((bf16[768,384]{1,0:T(8,128)(2,1)}), bf16[12288,384]{1,0:T(8,128)(2,1)}) %all-gather.3.cloned.1.call-update) | async-done | bytes 9437200 | tf_op jit(solution)/shard_map/all_gather | solution.py:249
  228.7 9.6 %final.1 = bf16[768,384]{1,0:T(8,128)(2,1)} custom-call(bf16[16,768,384]{2,1,0:T(8,128)(2,1)} %bitcast.13, bf16[6144,384]{1,0:T(8,128)(2,1)} %bitcast.12, f32[1,768]{1,0:T(1,128)} %psum.527.squares_ref), custom_call_target="tpu_custom_call" | custom-call | tf_op jit(solution)/shard_map/final/pallas_call | solution.py:190
  (4 shorter events, 0.0 us)
Async XLA Ops:
  6.5 99.7 %copy-start.2 = (s32[32,256]{1,0:T(8,128)S(1)}, s32[32,256]{1,0:T(8,128)}, u32[]{:S(2)}) copy-start(s32[32,256]{1,0:T(8,128)} %param.15) | copy-start | bytes 98308
  6.5 99.7 %copy-start.3 = (s32[32,256]{1,0:T(8,128)S(1)}, s32[32,256]{1,0:T(8,128)}, u32[]{:S(2)}) copy-start(s32[32,256]{1,0:T(8,128)} %param.16) | copy-start | bytes 98308
  8.7 98.5 %copy-start.4 = (f32[384]{0:T(512)S(1)}, f32[384]{0:T(512)}, u32[]{:S(2)}) copy-start(f32[384]{0:T(512)} %param.18) | copy-start | bytes 4612
  8.7 109.8 %copy-start = (bf16[768,384]{1,0:T(8,128)(2,1)S(1)}, bf16[768,384]{1,0:T(8,128)(2,1)}, u32[]{:S(2)}) copy-start(bf16[768,384]{1,0:T(8,128)(2,1)} %residual_ref.1) | copy-start | bytes 1769476
  12.7 130.1 %copy-start.1 = (bf16[192,384]{1,0:T(8,128)(2,1)S(1)}, bf16[192,384]{1,0:T(8,128)(2,1)}, u32[]{:S(2)}) copy-start(bf16[192,384]{1,0:T(8,128)(2,1)} %param.19) | copy-start | bytes 442372
  85.3 33.1 %all-to-all-start = ((bf16[32,24,384]{2,1,0:T(8,128)(2,1)}), bf16[32,24,384]{2,1,0:T(8,128)(2,1)S(1)}, u32[]{:S(2)}, u32[]{:S(2)}) async-start(bf16[32,24,384]{2,1,0:T(8,128)(2,1)} %bitcast.14), calls=%async_computation | async-start | bytes 1179648 | tf_op jit(solution)/shard_map/all_to_all | solution.py:245
  106.2 122.5 %all-gather.3.cloned.1.call-start = ((), (), s32[]{:S(2)}) async-start(), calls=%async_computation.2 | async-start | bytes 10027008 | tf_op jit(solution)/shard_map/all_gather | solution.py:249
Sparse Core Ops, SparseCore 0:
  120.3 108.3 all-gather.2

commit v6 on v5

--- a/solution.py
+++ b/solution.py
@@ -81,7 +81,7 @@
     )(rows, gate_mat, up_mat)
 
 
-def tail_kernel(down_hbm, combine_ref, slot_ref, *refs):
+def tail_kernel(down_hbm, combine_ref, owner_ref, *refs):
     out_ref, sums_ref, down_ref, hidden_ref, sems = refs[-5:]
     capacity = hidden_ref.shape[0]
     half = capacity // PART_ROWS
@@ -95,6 +95,14 @@
                 )
             )
             gets[-1].start()
+    slots = out_ref.shape[0]
+    owners = owner_ref[pl.ds(lax.axis_index("expert"), 1)].astype(jnp.float32)
+    owner_column = jnp.broadcast_to(owners, (128, capacity)).T[:, 0:1]
+    pick_row = lax.broadcasted_iota(jnp.int32, (capacity, capacity), 0)
+    pick_column = lax.broadcasted_iota(jnp.int32, (capacity, capacity), 1)
+    earlier = (owner_column == owners) & (pick_row < pick_column)
+    position = jnp.sum(jnp.where(earlier, 1.0, 0.0), axis=0, keepdims=True)
+    slot = (owners * (slots // owner_ref.shape[0]) + position).astype(jnp.int32)
     get_down = pltpu.make_async_copy(down_hbm, down_ref, sems.at[2 * half])
     get_down.start()
     for c in range(half):
@@ -108,13 +116,12 @@
     expert_out = jnp.dot(hidden_ref[...], down_ref[...], preferred_element_type=jnp.float32)
     combine = jnp.broadcast_to(combine_ref[...], (128, capacity)).T[:, 0:1]
     weighted = (combine * expert_out).astype(jnp.bfloat16)
-    slots = out_ref.shape[0]
     slot_ids = lax.broadcasted_iota(jnp.int32, (slots, capacity), 0)
-    table = jnp.where(slot_ref[...] == slot_ids, 1.0, 0.0).astype(jnp.bfloat16)
+    table = jnp.where(slot == slot_ids, 1.0, 0.0).astype(jnp.bfloat16)
     out_ref[...] = jnp.dot(table, weighted, preferred_element_type=jnp.float32).astype(jnp.bfloat16)
 
 
-def expert_tail(sums, down_mat, combine, slot, slots):
+def expert_tail(sums, down_mat, combine, pick_owner, slots):
     ff, width = down_mat.shape
     capacity = combine.shape[0]
     return pl.pallas_call(
@@ -132,7 +139,7 @@
         ],
         compiler_params=pltpu.CompilerParams(vmem_limit_bytes=VMEM_BYTES),
         name="expert_tail",
-    )(down_mat, combine[None, :], slot[None, :], *sums)
+    )(down_mat, combine[None, :], pick_owner, *sums)
 
 
 def mix_kernel(residual_ref, received_ref, row_ref, gain_ref, out_ref, squares_ref):
@@ -224,11 +231,7 @@
 
     parts = gate_up(my_rows, w_gate[0], w_up[0])
 
-    my_owner = lax.dynamic_index_in_dim(pick_owner, my_index, 0, keepdims=False)
     pick_ids = jnp.arange(capacity, dtype=jnp.int32)
-    same_earlier = (my_owner[:, None] == my_owner[None, :]) & (pick_ids[:, None] < pick_ids[None, :])
-    my_position = jnp.sum(same_earlier.astype(jnp.int32), axis=0)
-    my_slot = my_owner * slot_most + my_position
 
     mine = pick_owner == my_index
     before = (pick_ids[:, None] < pick_ids[None, :]).astype(jnp.bfloat16)
@@ -240,7 +243,7 @@
     row_of = jnp.sum(jnp.where(matches, pick_row[:, None, :] + 1, 0), axis=2) - 1
 
     sums = lax.psum(tuple(parts), "tensor")
-    outgoing = expert_tail(sums, w_down[0], combine_gate[0], my_slot, n_groups * slot_most)
+    outgoing = expert_tail(sums, w_down[0], combine_gate[0], pick_owner, n_groups * slot_most)
     outgoing = outgoing.reshape(n_groups, slot_most, width)
     received = lax.all_to_all(outgoing, "expert", split_axis=0, concat_axis=0, tiled=True)
     gained, squares = mix(

time: 246 us -> 244 us (level)
  no operation moved by 1% of the time
where the time goes in v6:
time: 244 us; the launch traced here: 243 us
  blocking collectives  157 us (64%)
  waiting for transfers between devices  31.2 us (13%)
  starting transfers between devices  20.3 us (8%)
  Pallas kernels  20 us (8%)
  between operations  13.5 us (6%)
    psum x1, blocking collectives, shards(): sums = lax.psum(tuple(parts), 'tensor')  68.6 us
    all_to_all x1, blocking collectives, shards(): lax.all_to_all(copies, 'expert', split_axis=0, concat_axis=0, tiled=True)  65.2 us
    psum x1, blocking collectives, shards(): square_total = lax.psum(squares, 'tensor')  22.7 us
    all_to_all x1, starting transfers between devices, shards(): lax.all_to_all(outgoing, 'expert', split_axis=0, concat_axis=0, tiled=True)  20.3 us
    all_gather x1, waiting for transfers between devices, shards(): full_gained = lax.all_gather(gained, 'tensor')  19.9 us
    all_to_all x1, waiting for transfers between devices, shards(): lax.all_to_all(outgoing, 'expert', split_axis=0, concat_axis=0, tiled=True)  11.3 us
    pallas_call x1, Pallas kernels, final(): pl.pallas_call(final_kernel, grid=(n // per_step,), out_shape=jax.ShapeDt...  9.63 us
  transfers between devices with their start and end apart: 2, of which 2 were waited for; matrix products, arithmetic and copies ran while one was open for 1% of the time, Pallas kernels for 0%

profile of v6, /device:TPU:1, one launch (start us, length us, event | category | flops | bytes accessed | tf_op | source)
XLA Modules:
  0.0 243.2 jit_solution(2540261158779686834)
XLA Ops:
  6.5 0.0 copy-start.2
  6.5 0.0 copy-start.3
  6.5 0.0 copy-start.4
  6.5 0.0 copy-start
  6.5 4.1 %gate_up.1 = (bf16[16,1536]{1,0:T(8,128)(2,1)}, bf16[16,1536]{1,0:T(8,128)(2,1)}, bf16[16,1536]{1,0:T(8,128)(2,1)}, bf16[16,1536]{1,0:T(8,128)(2,1)}, bf16[16,15...) custom-call(bf16[256,384]{1,0:T(8,128)(2,1)} %bitcast.16, ...), custom_call_target="tpu_custom_call" | custom-call | tf_op jit(solution)/shard_map/gate_up/pallas_call | solution.py:64
  10.7 0.0 copy-start.1
  10.7 68.6 %all-reduce.2 = (bf16[16,1536]{1,0:T(8,128)(2,1)}, bf16[16,1536]{1,0:T(8,128)(2,1)}, bf16[16,1536]{1,0:T(8,128)(2,1)}, bf16[16,1536]{1,0:T(8,128)(2,1)}, bf16[16...) all-reduce(bf16[16,1536]{1,0:T(8,128)(2,1)} %get-tuple-element.74, ...), channel_id=1, replica_groups=mesh['expert'=32,'tensor'=16] {'tensor'}, use_global_device_ids=true, to_apply=%region_0.1 | all-reduce | flops 854016 | bytes 3416064 | tf_op jit(solution)/shard_map/psum | solution.py:245
  79.3 4.7 %expert_tail.1 = bf16[768,384]{1,0:T(8,128)(2,1)} custom-call(bf16[1536,384]{1,0:T(8,128)(2,1)} %bitcast.13, f32[1,256]{1,0:T(1,128)} %combine_ref.1, s32[32,256]{1,0:T(8,128)} %owner_ref.1, bf16[16,1536]{1,0:T(8,128)(2,1)} %get-tuple-element.143.refs_0_, bf16[16,1536]{1,0:T(8,128)(2,1)} %get-tuple-element.144.refs_1_, ...), custom_call_target="tpu_custom_call" | custom-call | tf_op jit(solution)/shard_map/expert_tail/pallas_call | solution.py:127
  84.0 20.3 %all-to-all-start = ((bf16[32,24,384]{2,1,0:T(8,128)(2,1)}), bf16[32,24,384]{2,1,0:T(8,128)(2,1)S(1)}, u32[]{:S(2)}, u32[]{:S(2)}) async-start(bf16[32,24,384]{2,1,0:T(8,128)(2,1)} %bitcast.12), calls=%async_computation | async-start | bytes 1179648 | tf_op jit(solution)/shard_map/all_to_all | solution.py:248
  104.2 0.0 all-gather.3.cloned.1.call-start
  104.3 0.0 copy-done.2
  104.3 0.0 copy-done.3
  104.3 0.2 convolution_convert_fusion
  104.5 0.6 select_reduce_fusion
  105.1 0.1 sub.7.row_ref
  105.2 0.0 copy-done.4
  105.3 11.3 %all-to-all-done = bf16[32,24,384]{2,1,0:T(8,128)(2,1)S(1)} async-done(((bf16[32,24,384]{2,1,0:T(8,128)(2,1)}), bf16[32,24,384]{2,1,0:T(8,128)(2,1)S(1)}, u32[]{:S(2)}, u32[]{:S(2)}) %all-to-all-start) | async-done | bytes 589856 | tf_op jit(solution)/shard_map/all_to_all | solution.py:248
  116.5 0.0 copy-done
  116.5 1.6 mix.1
  118.2 0.0 all-gather.3.cloned.1.call-update
  118.2 22.7 %psum.527.squares_ref = f32[1,768]{1,0:T(1,128)} all-reduce(f32[1,768]{1,0:T(1,128)S(1)} %get-tuple-element.140), channel_id=1, replica_groups=mesh['expert'=32,'tensor'=16] {'tensor'}, use_global_device_ids=true, to_apply=%region_66.67 | all-reduce | flops 768 | bytes 6144 | tf_op jit(solution)/shard_map/psum | solution.py:253
  140.9 0.0 copy-done.1
  140.9 0.7 broadcast_in_dim.30
  141.6 65.2 %all_to_all.10 = bf16[32,192,384]{2,1,0:T(8,128)(2,1)} all-to-all(bf16[32,192,384]{2,1,0:T(8,128)(2,1)S(1)} %broadcast_in_dim.30), channel_id=1, replica_groups=mesh['expert'=32,'tensor'=16] {'expert'}, dimensions={0} | all-to-all | bytes 9437184 | tf_op jit(solution)/shard_map/all_to_all | solution.py:256
  206.8 19.9 %all-gather.3.cloned.1.call-done = bf16[12288,384]{1,0:T(8,128)(2,1)} async-done(((bf16[768,384]{1,0:T(8,128)(2,1)}), bf16[12288,384]{1,0:T(8,128)(2,1)}) %all-gather.3.cloned.1.call-update) | async-done | bytes 9437200 | tf_op jit(solution)/shard_map/all_gather | solution.py:252
  226.7 9.6 %final.1 = bf16[768,384]{1,0:T(8,128)(2,1)} custom-call(bf16[16,768,384]{2,1,0:T(8,128)(2,1)} %bitcast.11, bf16[6144,384]{1,0:T(8,128)(2,1)} %bitcast.10, f32[1,768]{1,0:T(1,128)} %psum.527.squares_ref), custom_call_target="tpu_custom_call" | custom-call | tf_op jit(solution)/shard_map/final/pallas_call | solution.py:197
  (4 shorter events, 0.0 us)
Async XLA Ops:
  6.5 97.8 %copy-start.2 = (s32[32,256]{1,0:T(8,128)S(1)}, s32[32,256]{1,0:T(8,128)}, u32[]{:S(2)}) copy-start(s32[32,256]{1,0:T(8,128)} %owner_ref.1) | copy-start | bytes 98308
  6.5 97.8 %copy-start.3 = (s32[32,256]{1,0:T(8,128)S(1)}, s32[32,256]{1,0:T(8,128)}, u32[]{:S(2)}) copy-start(s32[32,256]{1,0:T(8,128)} %param.16) | copy-start | bytes 98308
  6.5 98.7 %copy-start.4 = (f32[384]{0:T(512)S(1)}, f32[384]{0:T(512)}, u32[]{:S(2)}) copy-start(f32[384]{0:T(512)} %param.18) | copy-start | bytes 4612
  6.5 110.0 %copy-start = (bf16[768,384]{1,0:T(8,128)(2,1)S(1)}, bf16[768,384]{1,0:T(8,128)(2,1)}, u32[]{:S(2)}) copy-start(bf16[768,384]{1,0:T(8,128)(2,1)} %residual_ref.1) | copy-start | bytes 1769476
  10.7 130.2 %copy-start.1 = (bf16[192,384]{1,0:T(8,128)(2,1)S(1)}, bf16[192,384]{1,0:T(8,128)(2,1)}, u32[]{:S(2)}) copy-start(bf16[192,384]{1,0:T(8,128)(2,1)} %param.19) | copy-start | bytes 442372
  84.0 32.5 %all-to-all-start = ((bf16[32,24,384]{2,1,0:T(8,128)(2,1)}), bf16[32,24,384]{2,1,0:T(8,128)(2,1)S(1)}, u32[]{:S(2)}, u32[]{:S(2)}) async-start(bf16[32,24,384]{2,1,0:T(8,128)(2,1)} %bitcast.12), calls=%async_computation | async-start | bytes 1179648 | tf_op jit(solution)/shard_map/all_to_all | solution.py:248
  104.2 122.4 %all-gather.3.cloned.1.call-start = ((), (), s32[]{:S(2)}) async-start(), calls=%async_computation.2 | async-start | bytes 10027008 | tf_op jit(solution)/shard_map/all_gather | solution.py:252
Sparse Core Ops, SparseCore 0:
  118.3 108.3 all-gather.2

commit v7 on v6

--- a/solution.py
+++ b/solution.py
@@ -1,3 +1,5 @@
+import functools
+
 import jax
 import jax.numpy as jnp
 from jax import lax
@@ -9,6 +11,7 @@
 PART_TYPE = jnp.bfloat16
 VMEM_BYTES = 63 * 1024 * 1024
 SPARES = 33
+EXTRA_ROWS = 16
 CHUNKS = 1
 PART_ROWS = 16
 
@@ -142,25 +145,34 @@
     )(down_mat, combine[None, :], pick_owner, *sums)
 
 
-def mix_kernel(residual_ref, received_ref, row_ref, gain_ref, out_ref, squares_ref):
+def mix_kernel(residual_ref, received_ref, row_ref, gain_ref, first_ref, second_ref):
     tokens, width = residual_ref.shape
     slots = received_ref.shape[0]
     token_ids = lax.broadcasted_iota(jnp.int32, (tokens, slots), 0)
     table = jnp.where(row_ref[...] == token_ids, 1.0, 0.0).astype(jnp.bfloat16)
     moe = jnp.dot(table, received_ref[...], preferred_element_type=jnp.float32)
     mixed = residual_ref[...].astype(jnp.float32) + moe
-    out_ref[...] = (mixed * gain_ref[...]).astype(jnp.bfloat16)
+    gained = (mixed * gain_ref[...]).astype(jnp.bfloat16)
+    half = second_ref.shape[0]
+    first_ref[:half] = gained[:half]
+    second_ref[...] = gained[half:]
     squares = jnp.sum(mixed * mixed, axis=1, keepdims=True)
-    squares_ref[...] = jnp.broadcast_to(squares, (tokens, 128)).T[0:1]
+    flat = jnp.broadcast_to(squares, (tokens, 128)).T[0:1]
+    high = flat.astype(jnp.bfloat16).astype(jnp.float32)
+    low = flat - high
+    lines = [part[:, i : i + width] for part in (high, low) for i in range(0, tokens, width)]
+    lines.append(jnp.zeros((EXTRA_ROWS - len(lines), width), jnp.float32))
+    first_ref[half:] = jnp.concatenate(lines, axis=0).astype(jnp.bfloat16)
 
 
 def mix(residual, received, row_of, gain):
     tokens, width = residual.shape
+    half = tokens // 2
     return pl.pallas_call(
         mix_kernel,
         out_shape=[
-            jax.ShapeDtypeStruct((tokens, width), jnp.bfloat16),
-            jax.ShapeDtypeStruct((1, tokens), jnp.float32),
+            jax.ShapeDtypeStruct((half + EXTRA_ROWS, width), jnp.bfloat16),
+            jax.ShapeDtypeStruct((half, width), jnp.bfloat16),
         ],
         in_specs=[pl.BlockSpec(memory_space=pltpu.VMEM)] * 4,
         out_specs=[pl.BlockSpec(memory_space=pltpu.VMEM)] * 2,
@@ -169,45 +181,66 @@
     )(residual, received, row_of[None, :], gain[None, :])
 
 
-def final_kernel(gathered_ref, proj_ref, squares_ref, out_ref, acc_ref):
-    step = pl.program_id(0)
-    per_step, tokens, width = gathered_ref.shape
-    block = jnp.concatenate([gathered_ref[z] for z in range(per_step)], axis=1)
-    total = jnp.dot(block, proj_ref[...], preferred_element_type=jnp.float32)
-
-    @pl.when(step == 0)
-    def _():
-        acc_ref[...] = total
-
-    @pl.when(step > 0)
-    def _():
-        acc_ref[...] += total
-
-    @pl.when(step == pl.num_programs(0) - 1)
-    def _():
-        inverse = lax.rsqrt(squares_ref[...] / D + 1e-05)
-        column = jnp.broadcast_to(inverse, (128, tokens)).T[:, 0:1]
-        out_ref[...] = (acc_ref[...] * column).astype(jnp.bfloat16)
-
-
-def final(gathered, full_projection, square_total):
-    n, tokens, width = gathered.shape
-    columns = full_projection.shape[1]
-    per_step = 8
+def scale_kernel(first_ref, second_ref, squares_ref, out_ref):
+    half, width = first_ref.shape[0], squares_ref.shape[1]
+    lines = out_ref.shape[0] // width
+    columns = []
+    for i in range(lines):
+        line = squares_ref[i : i + 1] + squares_ref[lines + i : lines + i + 1]
+        columns.append(jnp.broadcast_to(line, (128, width)).T[:, 0:1])
+    inverse = lax.rsqrt(jnp.concatenate(columns, axis=0) / D + 1e-05)
+    out_ref[:half] = (first_ref[...] * inverse[:half]).astype(jnp.bfloat16)
+    out_ref[half:] = (second_ref[...] * inverse[half:]).astype(jnp.bfloat16)
+
+
+def scale(first, second, squares):
     return pl.pallas_call(
-        final_kernel,
-        grid=(n // per_step,),
-        out_shape=jax.ShapeDtypeStruct((tokens, columns), jnp.bfloat16),
-        in_specs=[
-            pl.BlockSpec((per_step, tokens, width), lambda i: (i, 0, 0)),
-            pl.BlockSpec((per_step * width, columns), lambda i: (i, 0)),
-            pl.BlockSpec((1, tokens), lambda i: (0, 0)),
-        ],
-        out_specs=pl.BlockSpec((tokens, columns), lambda i: (0, 0)),
-        scratch_shapes=[pltpu.VMEM((tokens, columns), jnp.float32)],
-        compiler_params=pltpu.CompilerParams(vmem_limit_bytes=VMEM_BYTES),
-        name="final",
-    )(gathered, full_projection, square_total)
+        scale_kernel,
+        out_shape=jax.ShapeDtypeStruct((first.shape[0] + second.shape[0], first.shape[1]), jnp.bfloat16),
+        in_specs=[pl.BlockSpec(memory_space=pltpu.VMEM)] * 3,
+        out_specs=pl.BlockSpec(memory_space=pltpu.VMEM),
+        compiler_params=pltpu.CompilerParams(vmem_limit_bytes=40 * 1024 * 1024),
+        name="scale",
+    )(first, second, squares)
+
+
+def ring_projection(halves, full_projection, axis, n):
+    me = lax.axis_index(axis)
+    rows, width = halves[1].shape
+    onward = [(i, (i + 1) % n) for i in range(n)]
+    back = [(i, (i - 1) % n) for i in range(n)]
+
+    def product(source, block):
+        part = lax.dynamic_slice_in_dim(full_projection, lax.rem(source, n) * width, width, 0)
+        return jnp.dot(block[:rows], part, preferred_element_type=jnp.float32)
+
+    arrived = [[(me, block)] for block in halves]
+    moving = [[block, block] for block in halves]
+    totals = [None, None]
+    squares = [halves[0][rows:]]
+    for k in range(1, n // 2 + 1):
+        for c in range(2):
+            if k < n // 2:
+                moved = [
+                    (me + n - k, lax.ppermute(moving[c][0], axis, onward)),
+                    (me + k, lax.ppermute(moving[c][1], axis, back)),
+                ]
+            elif c == 0:
+                moved = [(me + k, lax.ppermute(moving[c][0], axis, onward))]
+            else:
+                moved = [(me + k, lax.ppermute(moving[c][1], axis, back))]
+            for source, block in arrived[c]:
+                part = product(source, block)
+                totals[c] = part if totals[c] is None else totals[c] + part
+            blocks, totals[c] = lax.optimization_barrier(([block for _, block in moved], totals[c]))
+            arrived[c] = [(source, block) for (source, _), block in zip(moved, blocks)]
+            moving[c] = blocks
+            if c == 0:
+                squares += [block[rows:] for block in blocks]
+    for c in range(2):
+        for source, block in arrived[c]:
+            totals[c] = totals[c] + product(source, block)
+    return totals, sum(part.astype(jnp.float32) for part in squares)
 
 
 def shards(
@@ -221,6 +254,7 @@
     residual_in,
     norm_gain,
     projection,
+    n_tensor,
 ):
     my_rows = picked_rows[0]
     capacity = my_rows.shape[0]
@@ -229,6 +263,9 @@
     width = residual_in.shape[1]
     my_index = lax.axis_index("expert")
 
+    copies = jnp.broadcast_to(projection[None], (n_groups, *projection.shape))
+    full_projection = lax.all_to_all(copies, "expert", split_axis=0, concat_axis=0, tiled=True)
+    full_projection = full_projection.reshape(n_groups * projection.shape[0], projection.shape[1])
     parts = gate_up(my_rows, w_gate[0], w_up[0])
 
     pick_ids = jnp.arange(capacity, dtype=jnp.int32)
@@ -243,24 +280,21 @@
     row_of = jnp.sum(jnp.where(matches, pick_row[:, None, :] + 1, 0), axis=2) - 1
 
     sums = lax.psum(tuple(parts), "tensor")
+    first, full_projection = lax.optimization_barrier((sums[0], full_projection))
+    sums = (first, *sums[1:])
     outgoing = expert_tail(sums, w_down[0], combine_gate[0], pick_owner, n_groups * slot_most)
     outgoing = outgoing.reshape(n_groups, slot_most, width)
     received = lax.all_to_all(outgoing, "expert", split_axis=0, concat_axis=0, tiled=True)
-    gained, squares = mix(
+    halves = mix(
         residual_in, received.reshape(n_groups * slot_most, width), row_of.reshape(-1), norm_gain
     )
-    full_gained = lax.all_gather(gained, "tensor")
-    square_total = lax.psum(squares, "tensor")
-    square_total, projection = lax.optimization_barrier((square_total, projection))
-    copies = jnp.broadcast_to(projection[None], (n_groups, *projection.shape))
-    full_projection = lax.all_to_all(copies, "expert", split_axis=0, concat_axis=0, tiled=True)
-    full_projection = full_projection.reshape(n_groups * projection.shape[0], width)
-    return final(full_gained, full_projection, square_total)
+    totals, squares = ring_projection(halves, full_projection, "tensor", n_tensor)
+    return scale(*totals, squares)
 
 
 def solution(mesh):
     return jax.shard_map(
-        shards,
+        functools.partial(shards, n_tensor=mesh.shape["tensor"]),
         mesh=mesh,
         in_specs=(
             P("expert", None, "tensor"),

time: 244 us -> 277 us (1.14)
  the two profiles are of different devices: /device:TPU:1 before, /device:TPU:32 now
where the time goes in v7:
time: 277 us; the launch traced here: 275 us
  starting transfers between devices  119 us (43%)
  blocking collectives  77.1 us (28%)
  matrix products  41.8 us (15%)
  waiting for transfers between devices  20 us (7%)
  Pallas kernels  11.1 us (4%)
  local copies, waits for them, and re-layouts  3.92 us (1%)
    psum x1, blocking collectives, shards(): sums = lax.psum(tuple(parts), 'tensor')  77.1 us
    ppermute x14, starting transfers between devices, ring_projection(): lax.ppermute(moving[c][1], axis, back)  65 us
    dot_general x32, matrix products, product(): return jnp.dot(block[:rows], part, preferred_element_type=jnp.float32)  41.7 us
    ppermute x14, starting transfers between devices, ring_projection(): lax.ppermute(moving[c][0], axis, onward)  32.6 us
    all_to_all x1, waiting for transfers between devices, shards(): lax.all_to_all(outgoing, 'expert', split_axis=0, concat_axis=0, tiled=True)  10.8 us
    all_to_all x1, starting transfers between devices, shards(): lax.all_to_all(copies, 'expert', split_axis=0, concat_axis=0, tiled=True)  7.43 us
    all_to_all x1, starting transfers between devices, shards(): lax.all_to_all(outgoing, 'expert', split_axis=0, concat_axis=0, tiled=True)  7.07 us
  transfers between devices with their start and end apart: 32, of which 4 were waited for; matrix products, arithmetic and copies ran while one was open for 15% of the time, Pallas kernels for 2%

profile of v7, /device:TPU:32, one launch (start us, length us, event | category | flops | bytes accessed | tf_op | source)
XLA Modules:
  0.0 274.9 jit_solution(16721895961826071143)
XLA Ops:
  0.0 3.8 %broadcast_in_dim.12 = bf16[32,192,384]{2,1,0:T(8,128)(2,1)} broadcast(bf16[192,384]{1,0:T(8,128)(2,1)} %param.19), dimensions={1,2} | broadcast | bytes 4866048 | tf_op jit(solution)/shard_map/broadcast_in_dim | solution.py:266
  3.8 7.4 %all-to-all-start = ((bf16[32,192,384]{2,1,0:T(8,128)(2,1)}), bf16[32,192,384]{2,1,0:T(8,128)(2,1)}, u32[]{:S(2)}, u32[]{:S(2)}) async-start(bf16[32,192,384]{2,1,0:T(8,128)(2,1)} %broadcast_in_dim.12), calls=%async_computation | async-start | bytes 9437184 | tf_op jit(solution)/shard_map/all_to_all | solution.py:267
  11.4 4.2 %gate_up.1 = (bf16[16,1536]{1,0:T(8,128)(2,1)}, bf16[16,1536]{1,0:T(8,128)(2,1)}, bf16[16,1536]{1,0:T(8,128)(2,1)}, bf16[16,1536]{1,0:T(8,128)(2,1)}, bf16[16,15...) custom-call(bf16[256,384]{1,0:T(8,128)(2,1)} %bitcast.29, ...), custom_call_target="tpu_custom_call" | custom-call | tf_op jit(solution)/shard_map/gate_up/pallas_call | solution.py:67
  15.6 77.1 %all-reduce.2 = (bf16[16,1536]{1,0:T(8,128)(2,1)}, bf16[16,1536]{1,0:T(8,128)(2,1)}, bf16[16,1536]{1,0:T(8,128)(2,1)}, bf16[16,1536]{1,0:T(8,128)(2,1)}, bf16[16...) all-reduce(bf16[16,1536]{1,0:T(8,128)(2,1)} %get-tuple-element.120,, ...), channel_id=1, replica_groups=mesh['expert'=32,'tensor'=16] {'tensor'}, use_global_device_ids=true, to_apply=%region_0.1 | all-reduce | flops 854016 | bytes 3416064 | tf_op jit(solution)/shard_map/psum | solution.py:282
  92.7 4.8 %expert_tail.1 = bf16[768,384]{1,0:T(8,128)(2,1)} custom-call(bf16[1536,384]{1,0:T(8,128)(2,1)} %bitcast.26, f32[1,256]{1,0:T(1,128)} %combine_ref.1, s32[32,256]{1,0:T(8,128)} %owner_ref.1, bf16[16,1536]{1,0:T(8,128)(2,1)} %get-tuple-element.121.refs_0_, bf16[16,1536]{1,0:T(8,128)(2,1)} %get-tuple-element.236.refs_1_, ...), custom_call_target="tpu_custom_call" | custom-call | tf_op jit(solution)/shard_map/expert_tail/pallas_call | solution.py:130
  97.5 7.1 %all-to-all-start.1 = ((bf16[32,24,384]{2,1,0:T(8,128)(2,1)}), bf16[32,24,384]{2,1,0:T(8,128)(2,1)S(1)}, u32[]{:S(2)}, u32[]{:S(2)}) async-start(bf16[32,24,384]{2,1,0:T(8,128)(2,1)} %bitcast.25), calls=%async_computation.1 | async-start | bytes 1179648 | tf_op jit(solution)/shard_map/all_to_all | solution.py:287
  105.5 10.8 %all-to-all-done.1 = bf16[32,24,384]{2,1,0:T(8,128)(2,1)S(1)} async-done(((bf16[32,24,384]{2,1,0:T(8,128)(2,1)}), bf16[32,24,384]{2,1,0:T(8,128)(2,1)S(1)}, u32[]{:S(2)}, u32[]{:S(2)}) %all-to-all-start.1) | async-done | bytes 589856 | tf_op jit(solution)/shard_map/all_to_all | solution.py:287
  117.4 3.3 %collective-permute-start = (bf16[400,384]{1,0:T(8,128)(2,1)S(1)}, bf16[400,384]{1,0:T(8,128)(2,1)S(1)}, u32[]{:S(2)}, u32[]{:S(2)}) collective-permute-start(bf16[400,384]{1,0:T(8,128)(2,1)S(1)} %get-tuple-element.186), channel_id=1, source_target_pairs={{0,1},{1,2},{2,3},{3,4},{4,5},{5,6},{6,7},{7,8},{8,9},{9,10},{10,1... | collective-permute-start | bytes 921608 | tf_op jit(solution)/shard_map/ppermute | solution.py:225
  120.7 3.2 %collective-permute-start.1 = (bf16[400,384]{1,0:T(8,128)(2,1)S(1)}, bf16[400,384]{1,0:T(8,128)(2,1)S(1)}, u32[]{:S(2)}, u32[]{:S(2)}) collective-permute-start(bf16[400,384]{1,0:T(8,128)(2,1)S(1)} %get-tuple-element.186), channel_id=1, source_target_pairs={{0,15},{1,0},{2,1},{3,2},{4,3},{5,4},{6,5},{7,6},{8,7},{9,8},{10,9... | collective-permute-start | bytes 921608 | tf_op jit(solution)/shard_map/ppermute | solution.py:226
  123.9 2.7 collective-permute-start.15
  126.6 4.4 %collective-permute-start.16 = (bf16[384,384]{1,0:T(8,128)(2,1)S(1)}, bf16[384,384]{1,0:T(8,128)(2,1)S(1)}, u32[]{:S(2)}, u32[]{:S(2)}) collective-permute-start(bf16[384,384]{1,0:T(8,128)(2,1)S(1)} %get-tuple-element.211), channel_id=1, source_target_pairs={{0,15},{1,0},{2,1},{3,2},{4,3},{5,4},{6,5},{7,6},{8,7},{9,8},{10,9... | collective-permute-start | bytes 884744 | tf_op jit(solution)/shard_map/ppermute | solution.py:226
  133.6 2.8 %collective-permute-done.15 = bf16[384,384]{1,0:T(8,128)(2,1)S(1)} collective-permute-done((bf16[384,384]{1,0:T(8,128)(2,1)S(1)}, bf16[384,384]{1,0:T(8,128)(2,1)S(1)}, u32[]{:S(2)}, u32[]{:S(2)}) %collective-permute-start.15) | collective-permute-done | bytes 294944 | tf_op jit(solution)/shard_map/ppermute | solution.py:225
  136.4 2.2 collective-permute-done.16
  138.6 3.6 %collective-permute-start.17 = (bf16[384,384]{1,0:T(8,128)(2,1)S(1)}, bf16[384,384]{1,0:T(8,128)(2,1)S(1)}, u32[]{:S(2)}, u32[]{:S(2)}) collective-permute-start(bf16[384,384]{1,0:T(8,128)(2,1)S(1)} %collective-permute-done.15), channel_id=1, source_target_pairs={{0,1},{1,2},{2,3},{3,4},{4,5},{5,6},{6,7},{7,8},{8,9},{9,10},{10,1... | collective-permute-start | bytes 884744 | tf_op jit(solution)/shard_map/ppermute | solution.py:225
  142.2 1.3 fusion.103
  143.5 2.2 collective-permute-start.18
  145.7 1.3 add_add_fusion.6
  148.4 3.6 %collective-permute-start.2 = (bf16[400,384]{1,0:T(8,128)(2,1)S(1)}, bf16[400,384]{1,0:T(8,128)(2,1)S(1)}, u32[]{:S(2)}, u32[]{:S(2)}) collective-permute-start(bf16[400,384]{1,0:T(8,128)(2,1)S(1)} %collective-permute-done), channel_id=1, source_target_pairs={{0,1},{1,2},{2,3},{3,4},{4,5},{5,6},{6,7},{7,8},{8,9},{9,10},{10,1... | collective-permute-start | bytes 921608 | tf_op jit(solution)/shard_map/ppermute | solution.py:225
  152.0 3.8 %collective-permute-start.3 = (bf16[400,384]{1,0:T(8,128)(2,1)S(1)}, bf16[400,384]{1,0:T(8,128)(2,1)S(1)}, u32[]{:S(2)}, u32[]{:S(2)}) collective-permute-start(bf16[400,384]{1,0:T(8,128)(2,1)S(1)} %collective-permute-done.1), channel_id=1, source_target_pairs={{0,15},{1,0},{2,1},{3,2},{4,3},{5,4},{6,5},{7,6},{8,7},{9,8},{10,9... | collective-permute-start | bytes 921608 | tf_op jit(solution)/shard_map/ppermute | solution.py:226
  155.9 1.3 add_add_fusion.13
  157.2 2.0 collective-permute-start.19
  160.5 5.0 %collective-permute-start.20 = (bf16[384,384]{1,0:T(8,128)(2,1)S(1)}, bf16[384,384]{1,0:T(8,128)(2,1)S(1)}, u32[]{:S(2)}, u32[]{:S(2)}) collective-permute-start(bf16[384,384]{1,0:T(8,128)(2,1)S(1)} %collective-permute-done.18), channel_id=1, source_target_pairs={{0,15},{1,0},{2,1},{3,2},{4,3},{5,4},{6,5},{7,6},{8,7},{9,8},{10,9... | collective-permute-start | bytes 884744 | tf_op jit(solution)/shard_map/ppermute | solution.py:226
  165.6 1.3 add_add_fusion.5
  168.2 1.9 collective-permute-start.4
  170.2 5.1 %collective-permute-start.5 = (bf16[400,384]{1,0:T(8,128)(2,1)S(1)}, bf16[400,384]{1,0:T(8,128)(2,1)S(1)}, u32[]{:S(2)}, u32[]{:S(2)}) collective-permute-start(bf16[400,384]{1,0:T(8,128)(2,1)S(1)} %collective-permute-done.3), channel_id=1, source_target_pairs={{0,15},{1,0},{2,1},{3,2},{4,3},{5,4},{6,5},{7,6},{8,7},{9,8},{10,9... | collective-permute-start | bytes 921608 | tf_op jit(solution)/shard_map/ppermute | solution.py:226
  175.3 1.3 add_add_fusion.12
  176.6 1.9 collective-permute-start.21
  179.9 5.3 %collective-permute-start.22 = (bf16[384,384]{1,0:T(8,128)(2,1)S(1)}, bf16[384,384]{1,0:T(8,128)(2,1)S(1)}, u32[]{:S(2)}, u32[]{:S(2)}) collective-permute-start(bf16[384,384]{1,0:T(8,128)(2,1)S(1)} %collective-permute-done.20), channel_id=1, source_target_pairs={{0,15},{1,0},{2,1},{3,2},{4,3},{5,4},{6,5},{7,6},{8,7},{9,8},{10,9... | collective-permute-start | bytes 884744 | tf_op jit(solution)/shard_map/ppermute | solution.py:226
  187.8 1.9 collective-permute-start.6
  189.8 5.1 %collective-permute-start.7 = (bf16[400,384]{1,0:T(8,128)(2,1)S(1)}, bf16[400,384]{1,0:T(8,128)(2,1)S(1)}, u32[]{:S(2)}, u32[]{:S(2)}) collective-permute-start(bf16[400,384]{1,0:T(8,128)(2,1)S(1)} %collective-permute-done.5), channel_id=1, source_target_pairs={{0,15},{1,0},{2,1},{3,2},{4,3},{5,4},{6,5},{7,6},{8,7},{9,8},{10,9... | collective-permute-start | bytes 921608 | tf_op jit(solution)/shard_map/ppermute | solution.py:226
  196.2 1.9 collective-permute-start.23
  199.5 5.1 %collective-permute-start.24 = (bf16[384,384]{1,0:T(8,128)(2,1)S(1)}, bf16[384,384]{1,0:T(8,128)(2,1)S(1)}, u32[]{:S(2)}, u32[]{:S(2)}) collective-permute-start(bf16[384,384]{1,0:T(8,128)(2,1)S(1)} %collective-permute-done.22), channel_id=1, source_target_pairs={{0,15},{1,0},{2,1},{3,2},{4,3},{5,4},{6,5},{7,6},{8,7},{9,8},{10,9... | collective-permute-start | bytes 884744 | tf_op jit(solution)/shard_map/ppermute | solution.py:226
  207.2 1.9 collective-permute-start.8
  209.2 5.1 %collective-permute-start.9 = (bf16[400,384]{1,0:T(8,128)(2,1)S(1)}, bf16[400,384]{1,0:T(8,128)(2,1)S(1)}, u32[]{:S(2)}, u32[]{:S(2)}) collective-permute-start(bf16[400,384]{1,0:T(8,128)(2,1)S(1)} %collective-permute-done.7), channel_id=1, source_target_pairs={{0,15},{1,0},{2,1},{3,2},{4,3},{5,4},{6,5},{7,6},{8,7},{9,8},{10,9... | collective-permute-start | bytes 921608 | tf_op jit(solution)/shard_map/ppermute | solution.py:226
  215.6 1.9 collective-permute-start.25
  218.9 5.1 %collective-permute-start.26 = (bf16[384,384]{1,0:T(8,128)(2,1)S(1)}, bf16[384,384]{1,0:T(8,128)(2,1)S(1)}, u32[]{:S(2)}, u32[]{:S(2)}) collective-permute-start(bf16[384,384]{1,0:T(8,128)(2,1)S(1)} %collective-permute-done.24), channel_id=1, source_target_pairs={{0,15},{1,0},{2,1},{3,2},{4,3},{5,4},{6,5},{7,6},{8,7},{9,8},{10,9... | collective-permute-start | bytes 884744 | tf_op jit(solution)/shard_map/ppermute | solution.py:226
  226.7 1.9 collective-permute-start.10
  228.6 5.1 %collective-permute-start.11 = (bf16[400,384]{1,0:T(8,128)(2,1)S(1)}, bf16[400,384]{1,0:T(8,128)(2,1)S(1)}, u32[]{:S(2)}, u32[]{:S(2)}) collective-permute-start(bf16[400,384]{1,0:T(8,128)(2,1)S(1)} %collective-permute-done.9), channel_id=1, source_target_pairs={{0,15},{1,0},{2,1},{3,2},{4,3},{5,4},{6,5},{7,6},{8,7},{9,8},{10,9... | collective-permute-start | bytes 921608 | tf_op jit(solution)/shard_map/ppermute | solution.py:226
  233.7 1.3 add_add_fusion.9
  235.1 1.9 collective-permute-start.27
  237.0 1.3 fusion.63
  238.3 5.1 %collective-permute-start.28 = (bf16[384,384]{1,0:T(8,128)(2,1)S(1)}, bf16[384,384]{1,0:T(8,128)(2,1)S(1)}, u32[]{:S(2)}, u32[]{:S(2)}) collective-permute-start(bf16[384,384]{1,0:T(8,128)(2,1)S(1)} %collective-permute-done.26), channel_id=1, source_target_pairs={{0,15},{1,0},{2,1},{3,2},{4,3},{5,4},{6,5},{7,6},{8,7},{9,8},{10,9... | collective-permute-start | bytes 884744 | tf_op jit(solution)/shard_map/ppermute | solution.py:226
  246.1 1.9 collective-permute-start.12
  248.0 5.1 %collective-permute-start.13 = (bf16[400,384]{1,0:T(8,128)(2,1)S(1)}, bf16[400,384]{1,0:T(8,128)(2,1)S(1)}, u32[]{:S(2)}, u32[]{:S(2)}) collective-permute-start(bf16[400,384]{1,0:T(8,128)(2,1)S(1)} %collective-permute-done.11), channel_id=1, source_target_pairs={{0,15},{1,0},{2,1},{3,2},{4,3},{5,4},{6,5},{7,6},{8,7},{9,8},{10,9... | collective-permute-start | bytes 921608 | tf_op jit(solution)/shard_map/ppermute | solution.py:226
  253.1 1.3 add_add_fusion.8
  254.5 5.1 %collective-permute-start.29 = (bf16[384,384]{1,0:T(8,128)(2,1)S(1)}, bf16[384,384]{1,0:T(8,128)(2,1)S(1)}, u32[]{:S(2)}, u32[]{:S(2)}) collective-permute-start(bf16[384,384]{1,0:T(8,128)(2,1)S(1)} %collective-permute-done.28), channel_id=1, source_target_pairs={{0,15},{1,0},{2,1},{3,2},{4,3},{5,4},{6,5},{7,6},{8,7},{9,8},{10,9... | collective-permute-start | bytes 884744 | tf_op jit(solution)/shard_map/ppermute | solution.py:231
  263.6 1.9 collective-permute-start.14
  268.2 4.1 %collective-permute-done.14 = bf16[400,384]{1,0:T(8,128)(2,1)S(1)} collective-permute-done((bf16[400,384]{1,0:T(8,128)(2,1)S(1)}, bf16[400,384]{1,0:T(8,128)(2,1)S(1)}, u32[]{:S(2)}, u32[]{:S(2)}) %collective-permute-start.14) | collective-permute-done | bytes 307232 | tf_op jit(solution)/shard_map/ppermute | solution.py:229
  (72 shorter events, 34.6 us)
Async XLA Ops:
  3.8 88.9 %all-to-all-start = ((bf16[32,192,384]{2,1,0:T(8,128)(2,1)}), bf16[32,192,384]{2,1,0:T(8,128)(2,1)}, u32[]{:S(2)}, u32[]{:S(2)}) async-start(bf16[32,192,384]{2,1,0:T(8,128)(2,1)} %broadcast_in_dim.12), calls=%async_computation | async-start | bytes 9437184 | tf_op jit(solution)/shard_map/all_to_all | solution.py:267
  11.3 81.4 %copy-start.1 = (s32[32,256]{1,0:T(8,128)S(1)}, s32[32,256]{1,0:T(8,128)}, u32[]{:S(2)}) copy-start(s32[32,256]{1,0:T(8,128)} %owner_ref.1) | copy-start | bytes 98308
  11.3 81.4 %copy-start.2 = (s32[32,256]{1,0:T(8,128)S(1)}, s32[32,256]{1,0:T(8,128)}, u32[]{:S(2)}) copy-start(s32[32,256]{1,0:T(8,128)} %param.16) | copy-start | bytes 98308
  11.4 94.1 %copy-start.3 = (f32[384]{0:T(512)S(1)}, f32[384]{0:T(512)}, u32[]{:S(2)}) copy-start(f32[384]{0:T(512)} %param.18) | copy-start | bytes 4612
  11.4 105.0 %copy-start = (bf16[768,384]{1,0:T(8,128)(2,1)S(1)}, bf16[768,384]{1,0:T(8,128)(2,1)}, u32[]{:S(2)}) copy-start(bf16[768,384]{1,0:T(8,128)(2,1)} %residual_ref.1) | copy-start | bytes 1769476
  97.5 18.9 %all-to-all-start.1 = ((bf16[32,24,384]{2,1,0:T(8,128)(2,1)}), bf16[32,24,384]{2,1,0:T(8,128)(2,1)S(1)}, u32[]{:S(2)}, u32[]{:S(2)}) async-start(bf16[32,24,384]{2,1,0:T(8,128)(2,1)} %bitcast.25), calls=%async_computation.1 | async-start | bytes 1179648 | tf_op jit(solution)/shard_map/all_to_all | solution.py:287
  117.4 29.7 %collective-permute-start = (bf16[400,384]{1,0:T(8,128)(2,1)S(1)}, bf16[400,384]{1,0:T(8,128)(2,1)S(1)}, u32[]{:S(2)}, u32[]{:S(2)}) collective-permute-start(bf16[400,384]{1,0:T(8,128)(2,1)S(1)} %get-tuple-element.186), channel_id=1, source_target_pairs={{0,1},{1,2},{2,3},{3,4},{4,5},{5,6},{6,7},{7,8},{8,9},{9,10},{10,1... | collective-permute-start | bytes 921608 | tf_op jit(solution)/shard_map/ppermute | solution.py:225
  120.7 26.4 %collective-permute-start.1 = (bf16[400,384]{1,0:T(8,128)(2,1)S(1)}, bf16[400,384]{1,0:T(8,128)(2,1)S(1)}, u32[]{:S(2)}, u32[]{:S(2)}) collective-permute-start(bf16[400,384]{1,0:T(8,128)(2,1)S(1)} %get-tuple-element.186), channel_id=1, source_target_pairs={{0,15},{1,0},{2,1},{3,2},{4,3},{5,4},{6,5},{7,6},{8,7},{9,8},{10,9... | collective-permute-start | bytes 921608 | tf_op jit(solution)/shard_map/ppermute | solution.py:226
  123.9 12.5 %collective-permute-start.15 = (bf16[384,384]{1,0:T(8,128)(2,1)S(1)}, bf16[384,384]{1,0:T(8,128)(2,1)S(1)}, u32[]{:S(2)}, u32[]{:S(2)}) collective-permute-start(bf16[384,384]{1,0:T(8,128)(2,1)S(1)} %get-tuple-element.211), channel_id=1, source_target_pairs={{0,1},{1,2},{2,3},{3,4},{4,5},{5,6},{6,7},{7,8},{8,9},{9,10},{10,1... | collective-permute-start | bytes 884744 | tf_op jit(solution)/shard_map/ppermute | solution.py:225
  126.6 12.0 %collective-permute-start.16 = (bf16[384,384]{1,0:T(8,128)(2,1)S(1)}, bf16[384,384]{1,0:T(8,128)(2,1)S(1)}, u32[]{:S(2)}, u32[]{:S(2)}) collective-permute-start(bf16[384,384]{1,0:T(8,128)(2,1)S(1)} %get-tuple-element.211), channel_id=1, source_target_pairs={{0,15},{1,0},{2,1},{3,2},{4,3},{5,4},{6,5},{7,6},{8,7},{9,8},{10,9... | collective-permute-start | bytes 884744 | tf_op jit(solution)/shard_map/ppermute | solution.py:226
  138.6 18.6 %collective-permute-start.17 = (bf16[384,384]{1,0:T(8,128)(2,1)S(1)}, bf16[384,384]{1,0:T(8,128)(2,1)S(1)}, u32[]{:S(2)}, u32[]{:S(2)}) collective-permute-start(bf16[384,384]{1,0:T(8,128)(2,1)S(1)} %collective-permute-done.15), channel_id=1, source_target_pairs={{0,1},{1,2},{2,3},{3,4},{4,5},{5,6},{6,7},{7,8},{8,9},{9,10},{10,1... | collective-permute-start | bytes 884744 | tf_op jit(solution)/shard_map/ppermute | solution.py:225
  143.5 13.7 %collective-permute-start.18 = (bf16[384,384]{1,0:T(8,128)(2,1)S(1)}, bf16[384,384]{1,0:T(8,128)(2,1)S(1)}, u32[]{:S(2)}, u32[]{:S(2)}) collective-permute-start(bf16[384,384]{1,0:T(8,128)(2,1)S(1)} %collective-permute-done.16), channel_id=1, source_target_pairs={{0,15},{1,0},{2,1},{3,2},{4,3},{5,4},{6,5},{7,6},{8,7},{9,8},{10,9... | collective-permute-start | bytes 884744 | tf_op jit(solution)/shard_map/ppermute | solution.py:226
  148.4 18.5 %collective-permute-start.2 = (bf16[400,384]{1,0:T(8,128)(2,1)S(1)}, bf16[400,384]{1,0:T(8,128)(2,1)S(1)}, u32[]{:S(2)}, u32[]{:S(2)}) collective-permute-start(bf16[400,384]{1,0:T(8,128)(2,1)S(1)} %collective-permute-done), channel_id=1, source_target_pairs={{0,1},{1,2},{2,3},{3,4},{4,5},{5,6},{6,7},{7,8},{8,9},{9,10},{10,1... | collective-permute-start | bytes 921608 | tf_op jit(solution)/shard_map/ppermute | solution.py:225
  152.0 14.9 %collective-permute-start.3 = (bf16[400,384]{1,0:T(8,128)(2,1)S(1)}, bf16[400,384]{1,0:T(8,128)(2,1)S(1)}, u32[]{:S(2)}, u32[]{:S(2)}) collective-permute-start(bf16[400,384]{1,0:T(8,128)(2,1)S(1)} %collective-permute-done.1), channel_id=1, source_target_pairs={{0,15},{1,0},{2,1},{3,2},{4,3},{5,4},{6,5},{7,6},{8,7},{9,8},{10,9... | collective-permute-start | bytes 921608 | tf_op jit(solution)/shard_map/ppermute | solution.py:226
  157.2 19.4 %collective-permute-start.19 = (bf16[384,384]{1,0:T(8,128)(2,1)S(1)}, bf16[384,384]{1,0:T(8,128)(2,1)S(1)}, u32[]{:S(2)}, u32[]{:S(2)}) collective-permute-start(bf16[384,384]{1,0:T(8,128)(2,1)S(1)} %collective-permute-done.17), channel_id=1, source_target_pairs={{0,1},{1,2},{2,3},{3,4},{4,5},{5,6},{6,7},{7,8},{8,9},{9,10},{10,1... | collective-permute-start | bytes 884744 | tf_op jit(solution)/shard_map/ppermute | solution.py:225
  160.5 16.1 %collective-permute-start.20 = (bf16[384,384]{1,0:T(8,128)(2,1)S(1)}, bf16[384,384]{1,0:T(8,128)(2,1)S(1)}, u32[]{:S(2)}, u32[]{:S(2)}) collective-permute-start(bf16[384,384]{1,0:T(8,128)(2,1)S(1)} %collective-permute-done.18), channel_id=1, source_target_pairs={{0,15},{1,0},{2,1},{3,2},{4,3},{5,4},{6,5},{7,6},{8,7},{9,8},{10,9... | collective-permute-start | bytes 884744 | tf_op jit(solution)/shard_map/ppermute | solution.py:226
  168.2 18.3 %collective-permute-start.4 = (bf16[400,384]{1,0:T(8,128)(2,1)S(1)}, bf16[400,384]{1,0:T(8,128)(2,1)S(1)}, u32[]{:S(2)}, u32[]{:S(2)}) collective-permute-start(bf16[400,384]{1,0:T(8,128)(2,1)S(1)} %collective-permute-done.2), channel_id=1, source_target_pairs={{0,1},{1,2},{2,3},{3,4},{4,5},{5,6},{6,7},{7,8},{8,9},{9,10},{10,1... | collective-permute-start | bytes 921608 | tf_op jit(solution)/shard_map/ppermute | solution.py:225
  170.2 16.4 %collective-permute-start.5 = (bf16[400,384]{1,0:T(8,128)(2,1)S(1)}, bf16[400,384]{1,0:T(8,128)(2,1)S(1)}, u32[]{:S(2)}, u32[]{:S(2)}) collective-permute-start(bf16[400,384]{1,0:T(8,128)(2,1)S(1)} %collective-permute-done.3), channel_id=1, source_target_pairs={{0,15},{1,0},{2,1},{3,2},{4,3},{5,4},{6,5},{7,6},{8,7},{9,8},{10,9... | collective-permute-start | bytes 921608 | tf_op jit(solution)/shard_map/ppermute | solution.py:226
  176.6 19.6 %collective-permute-start.21 = (bf16[384,384]{1,0:T(8,128)(2,1)S(1)}, bf16[384,384]{1,0:T(8,128)(2,1)S(1)}, u32[]{:S(2)}, u32[]{:S(2)}) collective-permute-start(bf16[384,384]{1,0:T(8,128)(2,1)S(1)} %collective-permute-done.19), channel_id=1, source_target_pairs={{0,1},{1,2},{2,3},{3,4},{4,5},{5,6},{6,7},{7,8},{8,9},{9,10},{10,1... | collective-permute-start | bytes 884744 | tf_op jit(solution)/shard_map/ppermute | solution.py:225
  179.9 16.3 %collective-permute-start.22 = (bf16[384,384]{1,0:T(8,128)(2,1)S(1)}, bf16[384,384]{1,0:T(8,128)(2,1)S(1)}, u32[]{:S(2)}, u32[]{:S(2)}) collective-permute-start(bf16[384,384]{1,0:T(8,128)(2,1)S(1)} %collective-permute-done.20), channel_id=1, source_target_pairs={{0,15},{1,0},{2,1},{3,2},{4,3},{5,4},{6,5},{7,6},{8,7},{9,8},{10,9... | collective-permute-start | bytes 884744 | tf_op jit(solution)/shard_map/ppermute | solution.py:226
  187.8 18.1 %collective-permute-start.6 = (bf16[400,384]{1,0:T(8,128)(2,1)S(1)}, bf16[400,384]{1,0:T(8,128)(2,1)S(1)}, u32[]{:S(2)}, u32[]{:S(2)}) collective-permute-start(bf16[400,384]{1,0:T(8,128)(2,1)S(1)} %collective-permute-done.4), channel_id=1, source_target_pairs={{0,1},{1,2},{2,3},{3,4},{4,5},{5,6},{6,7},{7,8},{8,9},{9,10},{10,1... | collective-permute-start | bytes 921608 | tf_op jit(solution)/shard_map/ppermute | solution.py:225
  189.8 16.2 %collective-permute-start.7 = (bf16[400,384]{1,0:T(8,128)(2,1)S(1)}, bf16[400,384]{1,0:T(8,128)(2,1)S(1)}, u32[]{:S(2)}, u32[]{:S(2)}) collective-permute-start(bf16[400,384]{1,0:T(8,128)(2,1)S(1)} %collective-permute-done.5), channel_id=1, source_target_pairs={{0,15},{1,0},{2,1},{3,2},{4,3},{5,4},{6,5},{7,6},{8,7},{9,8},{10,9... | collective-permute-start | bytes 921608 | tf_op jit(solution)/shard_map/ppermute | solution.py:226
  196.2 19.4 %collective-permute-start.23 = (bf16[384,384]{1,0:T(8,128)(2,1)S(1)}, bf16[384,384]{1,0:T(8,128)(2,1)S(1)}, u32[]{:S(2)}, u32[]{:S(2)}) collective-permute-start(bf16[384,384]{1,0:T(8,128)(2,1)S(1)} %collective-permute-done.21), channel_id=1, source_target_pairs={{0,1},{1,2},{2,3},{3,4},{4,5},{5,6},{6,7},{7,8},{8,9},{9,10},{10,1... | collective-permute-start | bytes 884744 | tf_op jit(solution)/shard_map/ppermute | solution.py:225
  199.5 16.2 %collective-permute-start.24 = (bf16[384,384]{1,0:T(8,128)(2,1)S(1)}, bf16[384,384]{1,0:T(8,128)(2,1)S(1)}, u32[]{:S(2)}, u32[]{:S(2)}) collective-permute-start(bf16[384,384]{1,0:T(8,128)(2,1)S(1)} %collective-permute-done.22), channel_id=1, source_target_pairs={{0,15},{1,0},{2,1},{3,2},{4,3},{5,4},{6,5},{7,6},{8,7},{9,8},{10,9... | collective-permute-start | bytes 884744 | tf_op jit(solution)/shard_map/ppermute | solution.py:226
  207.2 18.1 %collective-permute-start.8 = (bf16[400,384]{1,0:T(8,128)(2,1)S(1)}, bf16[400,384]{1,0:T(8,128)(2,1)S(1)}, u32[]{:S(2)}, u32[]{:S(2)}) collective-permute-start(bf16[400,384]{1,0:T(8,128)(2,1)S(1)} %collective-permute-done.6), channel_id=1, source_target_pairs={{0,1},{1,2},{2,3},{3,4},{4,5},{5,6},{6,7},{7,8},{8,9},{9,10},{10,1... | collective-permute-start | bytes 921608 | tf_op jit(solution)/shard_map/ppermute | solution.py:225
  209.2 16.2 %collective-permute-start.9 = (bf16[400,384]{1,0:T(8,128)(2,1)S(1)}, bf16[400,384]{1,0:T(8,128)(2,1)S(1)}, u32[]{:S(2)}, u32[]{:S(2)}) collective-permute-start(bf16[400,384]{1,0:T(8,128)(2,1)S(1)} %collective-permute-done.7), channel_id=1, source_target_pairs={{0,15},{1,0},{2,1},{3,2},{4,3},{5,4},{6,5},{7,6},{8,7},{9,8},{10,9... | collective-permute-start | bytes 921608 | tf_op jit(solution)/shard_map/ppermute | solution.py:226
  215.6 19.4 %collective-permute-start.25 = (bf16[384,384]{1,0:T(8,128)(2,1)S(1)}, bf16[384,384]{1,0:T(8,128)(2,1)S(1)}, u32[]{:S(2)}, u32[]{:S(2)}) collective-permute-start(bf16[384,384]{1,0:T(8,128)(2,1)S(1)} %collective-permute-done.23), channel_id=1, source_target_pairs={{0,1},{1,2},{2,3},{3,4},{4,5},{5,6},{6,7},{7,8},{8,9},{9,10},{10,1... | collective-permute-start | bytes 884744 | tf_op jit(solution)/shard_map/ppermute | solution.py:225
  218.9 16.2 %collective-permute-start.26 = (bf16[384,384]{1,0:T(8,128)(2,1)S(1)}, bf16[384,384]{1,0:T(8,128)(2,1)S(1)}, u32[]{:S(2)}, u32[]{:S(2)}) collective-permute-start(bf16[384,384]{1,0:T(8,128)(2,1)S(1)} %collective-permute-done.24), channel_id=1, source_target_pairs={{0,15},{1,0},{2,1},{3,2},{4,3},{5,4},{6,5},{7,6},{8,7},{9,8},{10,9... | collective-permute-start | bytes 884744 | tf_op jit(solution)/shard_map/ppermute | solution.py:226
  226.7 18.1 %collective-permute-start.10 = (bf16[400,384]{1,0:T(8,128)(2,1)S(1)}, bf16[400,384]{1,0:T(8,128)(2,1)S(1)}, u32[]{:S(2)}, u32[]{:S(2)}) collective-permute-start(bf16[400,384]{1,0:T(8,128)(2,1)S(1)} %collective-permute-done.8), channel_id=1, source_target_pairs={{0,1},{1,2},{2,3},{3,4},{4,5},{5,6},{6,7},{7,8},{8,9},{9,10},{10,1... | collective-permute-start | bytes 921608 | tf_op jit(solution)/shard_map/ppermute | solution.py:225
  228.6 16.2 %collective-permute-start.11 = (bf16[400,384]{1,0:T(8,128)(2,1)S(1)}, bf16[400,384]{1,0:T(8,128)(2,1)S(1)}, u32[]{:S(2)}, u32[]{:S(2)}) collective-permute-start(bf16[400,384]{1,0:T(8,128)(2,1)S(1)} %collective-permute-done.9), channel_id=1, source_target_pairs={{0,15},{1,0},{2,1},{3,2},{4,3},{5,4},{6,5},{7,6},{8,7},{9,8},{10,9... | collective-permute-start | bytes 921608 | tf_op jit(solution)/shard_map/ppermute | solution.py:226
  235.1 19.4 %collective-permute-start.27 = (bf16[384,384]{1,0:T(8,128)(2,1)S(1)}, bf16[384,384]{1,0:T(8,128)(2,1)S(1)}, u32[]{:S(2)}, u32[]{:S(2)}) collective-permute-start(bf16[384,384]{1,0:T(8,128)(2,1)S(1)} %collective-permute-done.25), channel_id=1, source_target_pairs={{0,1},{1,2},{2,3},{3,4},{4,5},{5,6},{6,7},{7,8},{8,9},{9,10},{10,1... | collective-permute-start | bytes 884744 | tf_op jit(solution)/shard_map/ppermute | solution.py:225
  238.3 16.2 %collective-permute-start.28 = (bf16[384,384]{1,0:T(8,128)(2,1)S(1)}, bf16[384,384]{1,0:T(8,128)(2,1)S(1)}, u32[]{:S(2)}, u32[]{:S(2)}) collective-permute-start(bf16[384,384]{1,0:T(8,128)(2,1)S(1)} %collective-permute-done.26), channel_id=1, source_target_pairs={{0,15},{1,0},{2,1},{3,2},{4,3},{5,4},{6,5},{7,6},{8,7},{9,8},{10,9... | collective-permute-start | bytes 884744 | tf_op jit(solution)/shard_map/ppermute | solution.py:226
  246.1 16.2 %collective-permute-start.12 = (bf16[400,384]{1,0:T(8,128)(2,1)S(1)}, bf16[400,384]{1,0:T(8,128)(2,1)S(1)}, u32[]{:S(2)}, u32[]{:S(2)}) collective-permute-start(bf16[400,384]{1,0:T(8,128)(2,1)S(1)} %collective-permute-done.10), channel_id=1, source_target_pairs={{0,1},{1,2},{2,3},{3,4},{4,5},{5,6},{6,7},{7,8},{8,9},{9,10},{10,1... | collective-permute-start | bytes 921608 | tf_op jit(solution)/shard_map/ppermute | solution.py:225
  248.0 14.2 %collective-permute-start.13 = (bf16[400,384]{1,0:T(8,128)(2,1)S(1)}, bf16[400,384]{1,0:T(8,128)(2,1)S(1)}, u32[]{:S(2)}, u32[]{:S(2)}) collective-permute-start(bf16[400,384]{1,0:T(8,128)(2,1)S(1)} %collective-permute-done.11), channel_id=1, source_target_pairs={{0,15},{1,0},{2,1},{3,2},{4,3},{5,4},{6,5},{7,6},{8,7},{9,8},{10,9... | collective-permute-start | bytes 921608 | tf_op jit(solution)/shard_map/ppermute | solution.py:226
  254.5 12.3 %collective-permute-start.29 = (bf16[384,384]{1,0:T(8,128)(2,1)S(1)}, bf16[384,384]{1,0:T(8,128)(2,1)S(1)}, u32[]{:S(2)}, u32[]{:S(2)}) collective-permute-start(bf16[384,384]{1,0:T(8,128)(2,1)S(1)} %collective-permute-done.28), channel_id=1, source_target_pairs={{0,15},{1,0},{2,1},{3,2},{4,3},{5,4},{6,5},{7,6},{8,7},{9,8},{10,9... | collective-permute-start | bytes 884744 | tf_op jit(solution)/shard_map/ppermute | solution.py:231
  263.6 8.7 %collective-permute-start.14 = (bf16[400,384]{1,0:T(8,128)(2,1)S(1)}, bf16[400,384]{1,0:T(8,128)(2,1)S(1)}, u32[]{:S(2)}, u32[]{:S(2)}) collective-permute-start(bf16[400,384]{1,0:T(8,128)(2,1)S(1)} %collective-permute-done.12), channel_id=1, source_target_pairs={{0,1},{1,2},{2,3},{3,4},{4,5},{5,6},{6,7},{7,8},{8,9},{9,10},{10,1... | collective-permute-start | bytes 921608 | tf_op jit(solution)/shard_map/ppermute | solution.py:229

commit v8 on v6

--- a/solution.py
+++ b/solution.py
@@ -8,6 +8,7 @@
 D = 6144
 PART_TYPE = jnp.bfloat16
 VMEM_BYTES = 63 * 1024 * 1024
+TAIL_BYTES = 49152 * 1024
 SPARES = 33
 CHUNKS = 1
 PART_ROWS = 16
@@ -81,20 +82,11 @@
     )(rows, gate_mat, up_mat)
 
 
-def tail_kernel(down_hbm, combine_ref, owner_ref, *refs):
-    out_ref, sums_ref, down_ref, hidden_ref, sems = refs[-5:]
+def tail_kernel(down_ref, combine_ref, owner_ref, *refs):
+    out_ref, hidden_ref = refs[-2:]
     capacity = hidden_ref.shape[0]
     half = capacity // PART_ROWS
-    sum_hbms = refs[: 2 * half]
-    gets = []
-    for c in range(half):
-        for n in (c, half + c):
-            gets.append(
-                pltpu.make_async_copy(
-                    sum_hbms[n], sums_ref.at[n * PART_ROWS : (n + 1) * PART_ROWS], sems.at[n]
-                )
-            )
-            gets[-1].start()
+    sum_refs = refs[: 2 * half]
     slots = out_ref.shape[0]
     owners = owner_ref[pl.ds(lax.axis_index("expert"), 1)].astype(jnp.float32)
     owner_column = jnp.broadcast_to(owners, (128, capacity)).T[:, 0:1]
@@ -103,16 +95,11 @@
     earlier = (owner_column == owners) & (pick_row < pick_column)
     position = jnp.sum(jnp.where(earlier, 1.0, 0.0), axis=0, keepdims=True)
     slot = (owners * (slots // owner_ref.shape[0]) + position).astype(jnp.int32)
-    get_down = pltpu.make_async_copy(down_hbm, down_ref, sems.at[2 * half])
-    get_down.start()
     for c in range(half):
-        gets[2 * c].wait()
-        gets[2 * c + 1].wait()
         start = c * PART_ROWS
-        gate = sums_ref[start : start + PART_ROWS].astype(jnp.float32)
-        up = sums_ref[capacity + start : capacity + start + PART_ROWS].astype(jnp.float32)
+        gate = sum_refs[c][...].astype(jnp.float32)
+        up = sum_refs[half + c][...].astype(jnp.float32)
         hidden_ref[start : start + PART_ROWS] = (gate / (1.0 + jnp.exp(-gate)) * up).astype(jnp.bfloat16)
-    get_down.wait()
     expert_out = jnp.dot(hidden_ref[...], down_ref[...], preferred_element_type=jnp.float32)
     combine = jnp.broadcast_to(combine_ref[...], (128, capacity)).T[:, 0:1]
     weighted = (combine * expert_out).astype(jnp.bfloat16)
@@ -124,20 +111,17 @@
 def expert_tail(sums, down_mat, combine, pick_owner, slots):
     ff, width = down_mat.shape
     capacity = combine.shape[0]
+    n_parts = 2 * capacity // PART_ROWS
     return pl.pallas_call(
         tail_kernel,
         out_shape=jax.ShapeDtypeStruct((slots, width), jnp.bfloat16),
-        in_specs=[pl.BlockSpec(memory_space=pltpu.HBM)]
-        + [pl.BlockSpec(memory_space=pltpu.VMEM)] * 2
-        + [pl.BlockSpec(memory_space=pltpu.HBM)] * len(sums),
+        in_specs=[pl.BlockSpec(memory_space=pltpu.VMEM)] * (3 + n_parts)
+        + [pl.BlockSpec(memory_space=pl.ANY)] * (len(sums) - n_parts),
         out_specs=pl.BlockSpec(memory_space=pltpu.VMEM),
         scratch_shapes=[
-            pltpu.VMEM((2 * capacity, ff), PART_TYPE),
-            pltpu.VMEM((ff, width), down_mat.dtype),
             pltpu.VMEM((capacity, ff), jnp.bfloat16),
-            pltpu.SemaphoreType.DMA((2 * capacity // PART_ROWS + 1,)),
-        ],
-        compiler_params=pltpu.CompilerParams(vmem_limit_bytes=VMEM_BYTES),
+        ],
+        compiler_params=pltpu.CompilerParams(vmem_limit_bytes=TAIL_BYTES),
         name="expert_tail",
     )(down_mat, combine[None, :], pick_owner, *sums)
 

time: 244 us -> 243 us (level)
  local copies, waits for them, and re-layouts: 0.81 us -> 3.51 us
  Pallas kernels: 20 us -> 17.3 us
    pallas_call x1, Pallas kernels: 4.68 us -> 1.94 us  [expert_tail(): pl.pallas_call(tail_kernel, out_shape=jax.ShapeDtypeStruct((slots, width)...]
    unnamed x10 -> x16, local copies, waits for them, and re-layouts: 0.02 us -> 2.72 us
where the time goes in v8:
time: 243 us
  blocking collectives  156 us (64%)
  waiting for transfers between devices  31.2 us (13%)
  starting transfers between devices  20.3 us (8%)
  Pallas kernels  17.3 us (7%)
  between operations  13.5 us (6%)
  local copies, waits for them, and re-layouts  3.51 us (1%)
    psum x1, blocking collectives, shards(): sums = lax.psum(tuple(parts), 'tensor')  68.2 us
    all_to_all x1, blocking collectives, shards(): lax.all_to_all(copies, 'expert', split_axis=0, concat_axis=0, tiled=True)  65.2 us
    psum x1, blocking collectives, shards(): square_total = lax.psum(squares, 'tensor')  22.8 us
    all_to_all x1, starting transfers between devices, shards(): lax.all_to_all(outgoing, 'expert', split_axis=0, concat_axis=0, tiled=True)  20.2 us
    all_gather x1, waiting for transfers between devices, shards(): full_gained = lax.all_gather(gained, 'tensor')  20 us
    all_to_all x1, waiting for transfers between devices, shards(): lax.all_to_all(outgoing, 'expert', split_axis=0, concat_axis=0, tiled=True)  11.3 us
    pallas_call x1, Pallas kernels, final(): pl.pallas_call(final_kernel, grid=(n // per_step,), out_shape=jax.ShapeDt...  9.63 us
  transfers between devices with their start and end apart: 2, of which 2 were waited for; matrix products, arithmetic and copies ran while one was open for 1% of the time, Pallas kernels for 0%

profile of v8, /device:TPU:1, one launch (start us, length us, event | category | flops | bytes accessed | tf_op | source)
XLA Modules:
  0.0 242.8 jit_solution(18265582180470509143)
XLA Ops:
  6.5 0.0 copy-start.3
  6.5 0.0 copy-start.6
  6.5 0.0 copy-start.7
  6.5 0.0 copy-start.1
  6.5 4.1 %gate_up.1 = (bf16[16,1536]{1,0:T(8,128)(2,1)}, bf16[16,1536]{1,0:T(8,128)(2,1)}, bf16[16,1536]{1,0:T(8,128)(2,1)}, bf16[16,1536]{1,0:T(8,128)(2,1)}, bf16[16,15...) custom-call(bf16[256,384]{1,0:T(8,128)(2,1)} %bitcast.15, ...), custom_call_target="tpu_custom_call" | custom-call | tf_op jit(solution)/shard_map/gate_up/pallas_call | solution.py:65
  10.7 0.0 copy-start.5
  10.7 68.2 %all-reduce.2 = (bf16[16,1536]{1,0:T(8,128)(2,1)S(1)}, bf16[16,1536]{1,0:T(8,128)(2,1)S(1)}, bf16[16,1536]{1,0:T(8,128)(2,1)S(1)}, bf16[16,1536]{1,0:T(8,128)(2,...) all-reduce(bf16[16,1536]{1,0:T(8,128)(2,1)} %get-tuple-element.74, ...), channel_id=1, replica_groups=mesh['expert'=32,'tensor'=16] {'tensor'}, use_global_device_ids=true, to_apply=%region_0.1 | all-reduce | flops 854016 | bytes 3416064 | tf_op jit(solution)/shard_map/psum | solution.py:229
  78.9 0.0 copy-start
  78.9 1.3 copy-done
  80.2 0.0 copy-start.2
  80.2 0.8 copy-done.2
  80.9 0.0 copy-start.4
  80.9 0.7 copy-done.4
  81.6 1.9 expert_tail.1
  83.5 20.2 %all-to-all-start = ((bf16[32,24,384]{2,1,0:T(8,128)(2,1)}), bf16[32,24,384]{2,1,0:T(8,128)(2,1)S(1)}, u32[]{:S(2)}, u32[]{:S(2)}) async-start(bf16[32,24,384]{2,1,0:T(8,128)(2,1)} %bitcast.4), calls=%async_computation | async-start | bytes 1179648 | tf_op jit(solution)/shard_map/all_to_all | solution.py:232
  103.8 0.0 all-gather.3.cloned.1.call-start
  103.8 0.0 copy-done.3
  103.9 0.0 copy-done.6
  103.9 0.2 convolution_convert_fusion
  104.0 0.6 select_reduce_fusion
  104.7 0.1 sub.7.row_ref
  104.8 0.0 copy-done.7
  104.8 11.3 %all-to-all-done = bf16[32,24,384]{2,1,0:T(8,128)(2,1)S(1)} async-done(((bf16[32,24,384]{2,1,0:T(8,128)(2,1)}), bf16[32,24,384]{2,1,0:T(8,128)(2,1)S(1)}, u32[]{:S(2)}, u32[]{:S(2)}) %all-to-all-start) | async-done | bytes 589856 | tf_op jit(solution)/shard_map/all_to_all | solution.py:232
  116.1 0.0 copy-done.1
  116.1 1.6 mix.1
  117.7 0.0 all-gather.3.cloned.1.call-update
  117.7 22.8 %psum.527.squares_ref = f32[1,768]{1,0:T(1,128)} all-reduce(f32[1,768]{1,0:T(1,128)S(1)} %get-tuple-element.140), channel_id=1, replica_groups=mesh['expert'=32,'tensor'=16] {'tensor'}, use_global_device_ids=true, to_apply=%region_66.67 | all-reduce | flops 768 | bytes 6144 | tf_op jit(solution)/shard_map/psum | solution.py:237
  140.5 0.0 copy-done.5
  140.5 0.7 broadcast_in_dim.30
  141.2 65.2 %all_to_all.10 = bf16[32,192,384]{2,1,0:T(8,128)(2,1)} all-to-all(bf16[32,192,384]{2,1,0:T(8,128)(2,1)S(1)} %broadcast_in_dim.30), channel_id=1, replica_groups=mesh['expert'=32,'tensor'=16] {'expert'}, dimensions={0} | all-to-all | bytes 9437184 | tf_op jit(solution)/shard_map/all_to_all | solution.py:240
  206.3 20.0 %all-gather.3.cloned.1.call-done = bf16[12288,384]{1,0:T(8,128)(2,1)} async-done(((bf16[768,384]{1,0:T(8,128)(2,1)}), bf16[12288,384]{1,0:T(8,128)(2,1)}) %all-gather.3.cloned.1.call-update) | async-done | bytes 9437200 | tf_op jit(solution)/shard_map/all_gather | solution.py:236
  226.3 9.6 %final.1 = bf16[768,384]{1,0:T(8,128)(2,1)} custom-call(bf16[16,768,384]{2,1,0:T(8,128)(2,1)} %bitcast.12, bf16[6144,384]{1,0:T(8,128)(2,1)} %bitcast.11, f32[1,768]{1,0:T(1,128)} %psum.527.squares_ref), custom_call_target="tpu_custom_call" | custom-call | tf_op jit(solution)/shard_map/final/pallas_call | solution.py:181
  (4 shorter events, 0.0 us)
Async XLA Ops:
  6.5 97.3 %copy-start.3 = (s32[32,256]{1,0:T(8,128)S(1)}, s32[32,256]{1,0:T(8,128)}, u32[]{:S(2)}) copy-start(s32[32,256]{1,0:T(8,128)} %owner_ref.1) | copy-start | bytes 98308
  6.5 97.3 %copy-start.6 = (s32[32,256]{1,0:T(8,128)S(1)}, s32[32,256]{1,0:T(8,128)}, u32[]{:S(2)}) copy-start(s32[32,256]{1,0:T(8,128)} %param.16) | copy-start | bytes 98308
  6.5 98.2 %copy-start.7 = (f32[384]{0:T(512)S(1)}, f32[384]{0:T(512)}, u32[]{:S(2)}) copy-start(f32[384]{0:T(512)} %param.18) | copy-start | bytes 4612
  6.5 109.5 %copy-start.1 = (bf16[768,384]{1,0:T(8,128)(2,1)S(1)}, bf16[768,384]{1,0:T(8,128)(2,1)}, u32[]{:S(2)}) copy-start(bf16[768,384]{1,0:T(8,128)(2,1)} %residual_ref.1) | copy-start | bytes 1769476
  10.7 129.8 %copy-start.5 = (bf16[192,384]{1,0:T(8,128)(2,1)S(1)}, bf16[192,384]{1,0:T(8,128)(2,1)}, u32[]{:S(2)}) copy-start(bf16[192,384]{1,0:T(8,128)(2,1)} %param.19) | copy-start | bytes 442372
  78.9 1.3 copy-start
  80.2 0.8 copy-start.2
  80.9 0.7 copy-start.4
  83.5 32.5 %all-to-all-start = ((bf16[32,24,384]{2,1,0:T(8,128)(2,1)}), bf16[32,24,384]{2,1,0:T(8,128)(2,1)S(1)}, u32[]{:S(2)}, u32[]{:S(2)}) async-start(bf16[32,24,384]{2,1,0:T(8,128)(2,1)} %bitcast.4), calls=%async_computation | async-start | bytes 1179648 | tf_op jit(solution)/shard_map/all_to_all | solution.py:232
  103.8 122.5 %all-gather.3.cloned.1.call-start = ((), (), s32[]{:S(2)}) async-start(), calls=%async_computation.2 | async-start | bytes 10027008 | tf_op jit(solution)/shard_map/all_gather | solution.py:236
Sparse Core Ops, SparseCore 0:
  117.8 108.4 all-gather.2

commit v9 on v8

--- a/solution.py
+++ b/solution.py
@@ -82,26 +82,26 @@
     )(rows, gate_mat, up_mat)
 
 
-def tail_kernel(down_ref, combine_ref, owner_ref, *refs):
+def tail_kernel(down_ref, picks_ref, *refs):
     out_ref, hidden_ref = refs[-2:]
     capacity = hidden_ref.shape[0]
     half = capacity // PART_ROWS
     sum_refs = refs[: 2 * half]
     slots = out_ref.shape[0]
-    owners = owner_ref[pl.ds(lax.axis_index("expert"), 1)].astype(jnp.float32)
+    owners = picks_ref[pl.ds(lax.axis_index("expert") + 1, 1)]
     owner_column = jnp.broadcast_to(owners, (128, capacity)).T[:, 0:1]
     pick_row = lax.broadcasted_iota(jnp.int32, (capacity, capacity), 0)
     pick_column = lax.broadcasted_iota(jnp.int32, (capacity, capacity), 1)
     earlier = (owner_column == owners) & (pick_row < pick_column)
     position = jnp.sum(jnp.where(earlier, 1.0, 0.0), axis=0, keepdims=True)
-    slot = (owners * (slots // owner_ref.shape[0]) + position).astype(jnp.int32)
+    slot = (owners * (slots // (picks_ref.shape[0] - 1)) + position).astype(jnp.int32)
     for c in range(half):
         start = c * PART_ROWS
         gate = sum_refs[c][...].astype(jnp.float32)
         up = sum_refs[half + c][...].astype(jnp.float32)
         hidden_ref[start : start + PART_ROWS] = (gate / (1.0 + jnp.exp(-gate)) * up).astype(jnp.bfloat16)
     expert_out = jnp.dot(hidden_ref[...], down_ref[...], preferred_element_type=jnp.float32)
-    combine = jnp.broadcast_to(combine_ref[...], (128, capacity)).T[:, 0:1]
+    combine = jnp.broadcast_to(picks_ref[0:1], (128, capacity)).T[:, 0:1]
     weighted = (combine * expert_out).astype(jnp.bfloat16)
     slot_ids = lax.broadcasted_iota(jnp.int32, (slots, capacity), 0)
     table = jnp.where(slot == slot_ids, 1.0, 0.0).astype(jnp.bfloat16)
@@ -112,10 +112,11 @@
     ff, width = down_mat.shape
     capacity = combine.shape[0]
     n_parts = 2 * capacity // PART_ROWS
+    picks = jnp.concatenate([combine[None, :], pick_owner.astype(jnp.float32)], axis=0)
     return pl.pallas_call(
         tail_kernel,
         out_shape=jax.ShapeDtypeStruct((slots, width), jnp.bfloat16),
-        in_specs=[pl.BlockSpec(memory_space=pltpu.VMEM)] * (3 + n_parts)
+        in_specs=[pl.BlockSpec(memory_space=pltpu.VMEM)] * (2 + n_parts)
         + [pl.BlockSpec(memory_space=pl.ANY)] * (len(sums) - n_parts),
         out_specs=pl.BlockSpec(memory_space=pltpu.VMEM),
         scratch_shapes=[
@@ -123,7 +124,7 @@
         ],
         compiler_params=pltpu.CompilerParams(vmem_limit_bytes=TAIL_BYTES),
         name="expert_tail",
-    )(down_mat, combine[None, :], pick_owner, *sums)
+    )(down_mat, picks, *sums)
 
 
 def mix_kernel(residual_ref, received_ref, row_ref, gain_ref, out_ref, squares_ref):

time: 243 us -> 243 us (level)
  no operation moved by 1% of the time
where the time goes in v9:
time: 243 us
  blocking collectives  156 us (64%)
  waiting for transfers between devices  31.2 us (13%)
  starting transfers between devices  20.3 us (8%)
  Pallas kernels  17.4 us (7%)
  between operations  13.5 us (6%)
    psum x1, blocking collectives, shards(): sums = lax.psum(tuple(parts), 'tensor')  68.2 us
    all_to_all x1, blocking collectives, shards(): lax.all_to_all(copies, 'expert', split_axis=0, concat_axis=0, tiled=True)  65.1 us
    psum x1, blocking collectives, shards(): square_total = lax.psum(squares, 'tensor')  22.8 us
    all_to_all x1, starting transfers between devices, shards(): lax.all_to_all(outgoing, 'expert', split_axis=0, concat_axis=0, tiled=True)  20.2 us
    all_gather x1, waiting for transfers between devices, shards(): full_gained = lax.all_gather(gained, 'tensor')  20 us
    all_to_all x1, waiting for transfers between devices, shards(): lax.all_to_all(outgoing, 'expert', split_axis=0, concat_axis=0, tiled=True)  11.3 us
    pallas_call x1, Pallas kernels, final(): pl.pallas_call(final_kernel, grid=(n // per_step,), out_shape=jax.ShapeDt...  9.63 us
  transfers between devices with their start and end apart: 2, of which 2 were waited for; matrix products, arithmetic and copies ran while one was open for 1% of the time, Pallas kernels for 0%

profile of v9, /device:TPU:1, one launch (start us, length us, event | category | flops | bytes accessed | tf_op | source)
XLA Modules:
  0.0 242.9 jit_solution(8413748652438819200)
XLA Ops:
  6.5 0.0 copy-start.3
  6.5 0.0 copy-start.4
  6.5 0.8 convert_element_type.8
  7.4 0.7 pad_maximum_fusion.picks_ref
  8.1 0.0 copy-start.5
  8.1 0.0 copy-start.1
  8.1 4.2 %gate_up.1 = (bf16[16,1536]{1,0:T(8,128)(2,1)}, bf16[16,1536]{1,0:T(8,128)(2,1)}, bf16[16,1536]{1,0:T(8,128)(2,1)}, bf16[16,1536]{1,0:T(8,128)(2,1)}, bf16[16,15...) custom-call(bf16[256,384]{1,0:T(8,128)(2,1)} %bitcast.15, ...), custom_call_target="tpu_custom_call" | custom-call | tf_op jit(solution)/shard_map/gate_up/pallas_call | solution.py:65
  12.2 0.0 copy-start.2
  12.2 68.2 %all-reduce.2 = (bf16[16,1536]{1,0:T(8,128)(2,1)S(1)}, bf16[16,1536]{1,0:T(8,128)(2,1)S(1)}, bf16[16,1536]{1,0:T(8,128)(2,1)S(1)}, bf16[16,1536]{1,0:T(8,128)(2,...) all-reduce(bf16[16,1536]{1,0:T(8,128)(2,1)} %get-tuple-element.74, ...), channel_id=1, replica_groups=mesh['expert'=32,'tensor'=16] {'tensor'}, use_global_device_ids=true, to_apply=%region_0.1 | all-reduce | flops 854016 | bytes 3416064 | tf_op jit(solution)/shard_map/psum | solution.py:230
  80.5 0.0 copy-start
  80.5 1.3 copy-done
  81.7 1.9 expert_tail.1
  83.7 20.2 %all-to-all-start = ((bf16[32,24,384]{2,1,0:T(8,128)(2,1)}), bf16[32,24,384]{2,1,0:T(8,128)(2,1)S(1)}, u32[]{:S(2)}, u32[]{:S(2)}) async-start(bf16[32,24,384]{2,1,0:T(8,128)(2,1)} %bitcast.4), calls=%async_computation | async-start | bytes 1179648 | tf_op jit(solution)/shard_map/all_to_all | solution.py:233
  103.9 0.0 all-gather.3.cloned.1.call-start
  104.0 0.0 copy-done.3
  104.0 0.0 copy-done.4
  104.0 0.2 convolution_convert_fusion
  104.2 0.6 select_reduce_fusion
  104.8 0.1 sub.7.row_ref
  104.9 0.0 copy-done.5
  104.9 11.3 %all-to-all-done = bf16[32,24,384]{2,1,0:T(8,128)(2,1)S(1)} async-done(((bf16[32,24,384]{2,1,0:T(8,128)(2,1)}), bf16[32,24,384]{2,1,0:T(8,128)(2,1)S(1)}, u32[]{:S(2)}, u32[]{:S(2)}) %all-to-all-start) | async-done | bytes 589856 | tf_op jit(solution)/shard_map/all_to_all | solution.py:233
  116.2 0.0 copy-done.1
  116.2 1.6 mix.1
  117.8 0.0 all-gather.3.cloned.1.call-update
  117.9 22.8 %psum.527.squares_ref = f32[1,768]{1,0:T(1,128)} all-reduce(f32[1,768]{1,0:T(1,128)S(1)} %get-tuple-element.140), channel_id=1, replica_groups=mesh['expert'=32,'tensor'=16] {'tensor'}, use_global_device_ids=true, to_apply=%region_66.67 | all-reduce | flops 768 | bytes 6144 | tf_op jit(solution)/shard_map/psum | solution.py:238
  140.6 0.0 copy-done.2
  140.6 0.7 broadcast_in_dim.30
  141.3 65.1 %all_to_all.10 = bf16[32,192,384]{2,1,0:T(8,128)(2,1)} all-to-all(bf16[32,192,384]{2,1,0:T(8,128)(2,1)S(1)} %broadcast_in_dim.30), channel_id=1, replica_groups=mesh['expert'=32,'tensor'=16] {'expert'}, dimensions={0} | all-to-all | bytes 9437184 | tf_op jit(solution)/shard_map/all_to_all | solution.py:241
  206.5 20.0 %all-gather.3.cloned.1.call-done = bf16[12288,384]{1,0:T(8,128)(2,1)} async-done(((bf16[768,384]{1,0:T(8,128)(2,1)}), bf16[12288,384]{1,0:T(8,128)(2,1)}) %all-gather.3.cloned.1.call-update) | async-done | bytes 9437200 | tf_op jit(solution)/shard_map/all_gather | solution.py:237
  226.4 9.6 %final.1 = bf16[768,384]{1,0:T(8,128)(2,1)} custom-call(bf16[16,768,384]{2,1,0:T(8,128)(2,1)} %bitcast.12, bf16[6144,384]{1,0:T(8,128)(2,1)} %bitcast.11, f32[1,768]{1,0:T(1,128)} %psum.527.squares_ref), custom_call_target="tpu_custom_call" | custom-call | tf_op jit(solution)/shard_map/final/pallas_call | solution.py:182
  (4 shorter events, 0.0 us)
Async XLA Ops:
  6.5 97.4 %copy-start.3 = (s32[32,256]{1,0:T(8,128)S(1)}, s32[32,256]{1,0:T(8,128)}, u32[]{:S(2)}) copy-start(s32[32,256]{1,0:T(8,128)} %param.15) | copy-start | bytes 98308
  6.5 97.5 %copy-start.4 = (s32[32,256]{1,0:T(8,128)S(1)}, s32[32,256]{1,0:T(8,128)}, u32[]{:S(2)}) copy-start(s32[32,256]{1,0:T(8,128)} %param.16) | copy-start | bytes 98308
  8.1 96.9 %copy-start.5 = (f32[384]{0:T(512)S(1)}, f32[384]{0:T(512)}, u32[]{:S(2)}) copy-start(f32[384]{0:T(512)} %param.18) | copy-start | bytes 4612
  8.1 108.1 %copy-start.1 = (bf16[768,384]{1,0:T(8,128)(2,1)S(1)}, bf16[768,384]{1,0:T(8,128)(2,1)}, u32[]{:S(2)}) copy-start(bf16[768,384]{1,0:T(8,128)(2,1)} %residual_ref.1) | copy-start | bytes 1769476
  12.2 128.4 %copy-start.2 = (bf16[192,384]{1,0:T(8,128)(2,1)S(1)}, bf16[192,384]{1,0:T(8,128)(2,1)}, u32[]{:S(2)}) copy-start(bf16[192,384]{1,0:T(8,128)(2,1)} %param.19) | copy-start | bytes 442372
  80.5 1.3 copy-start
  83.7 32.5 %all-to-all-start = ((bf16[32,24,384]{2,1,0:T(8,128)(2,1)}), bf16[32,24,384]{2,1,0:T(8,128)(2,1)S(1)}, u32[]{:S(2)}, u32[]{:S(2)}) async-start(bf16[32,24,384]{2,1,0:T(8,128)(2,1)} %bitcast.4), calls=%async_computation | async-start | bytes 1179648 | tf_op jit(solution)/shard_map/all_to_all | solution.py:233
  103.9 122.5 %all-gather.3.cloned.1.call-start = ((), (), s32[]{:S(2)}) async-start(), calls=%async_computation.2 | async-start | bytes 10027008 | tf_op jit(solution)/shard_map/all_gather | solution.py:237
Sparse Core Ops, SparseCore 0:
  118.0 108.4 all-gather.2
